TPU v7x, 512 devices: a whole 4x8x8 slice. The times are simulated.
512 devices in a mesh: rows: 64 (over z, x, core), rep: 8 (over y).
Axes of the slice: x: 4, y: 8, z: 8, core: 2. Of those that a mesh axis runs over, the one named last changes fastest.
Arguments:
- features: bfloat16 [65536, 128], P(('rows', 'rep')), may hold values from -6 to 6
- degrees: int32 [65536], P(('rows', 'rep')), may hold values from 0 to 16
- tile_values: bfloat16 [49152, 128, 128], P(('rows', 'rep')), may hold values from 0 to 0.099609375
- tile_row: int32 [49152], P(('rows', 'rep')), may hold values from 0 to 511, as said below
- tile_col: int32 [49152], P(('rows', 'rep')), may hold values from 0 to 511, as said below
- tile_count: int32 [512], P(('rows', 'rep')), may hold values from 24 to 96, as said below
- weight: bfloat16 [128, 64], replicated, may hold values from -0.5 to 0.5
- out_bias: bfloat16 [64], replicated, may hold values from -3 to 3
- cotangent: bfloat16 [65536, 64], P(('rows', 'rep')), may hold values from -6 to 6
Outputs:
- mixed: bfloat16 [65536, 64], P(('rows', 'rep'))
- grad_features: bfloat16 [65536, 128], P(('rows', 'rep'))
- grad_weight: float32 [128, 64], replicated
Inputs may be any that keep to these rules, and one draw needn't show every extreme that they name: `tile_row`: on the device with rows index r and rep index p, every slot's row block lies in r * 8 to r * 8 + 7; the (row block, column block) pairs of one device's slots are all different. `tile_col`: on the device with rep index p, every slot's column block c has c % 8 == p. `tile_count`: some device has all 96 slots live.
All inputs are finite; a program needn't handle non-finite values.
Results may differ from a plain program's by a relative error of at most 0.015.
Values may be sent and summed in bfloat16 or wider, within the bound.
No kernel may reach another device: no remote copies, remote signals or barrier semaphores. Data moves between devices by JAX's collectives and lax.ppermute only.
A program may use at most 64 MiB of HBM per device.

v0:
```python
import math

import jax
import jax.numpy as jnp
from jax import lax
from jax.sharding import PartitionSpec as P


def silu_slope(preact):
    sigmoid_val = jax.nn.sigmoid(preact)
    return sigmoid_val * (1.0 + preact * (1.0 - sigmoid_val))


def shards(
    features, degrees, tile_values, tile_row, tile_col, tile_count, weight, out_bias, cotangent
):
    block = tile_values.shape[1]
    slots = tile_values.shape[0]
    width_in = features.shape[1]
    width_out = weight.shape[1]
    rep_count = lax.axis_size("rep")
    row_count = lax.axis_size("rows")
    row_index = lax.axis_index("rows")
    stride = 8
    live_count = tile_count[0]
    turns = (live_count + stride - 1) // stride
    local_rows = tile_row - row_index * rep_count
    gathered_slot = tile_col // rep_count
    scales = lax.rsqrt(degrees.astype(jnp.float32) + 1.0)
    scaled = (scales[:, None] * features.astype(jnp.float32)).astype(jnp.bfloat16)
    gathered = lax.all_gather(scaled, "rows", axis=0, tiled=True).reshape(
        row_count, block, width_in
    )

    def forward_turn(turn, running):
        first = turn * stride
        values = lax.dynamic_slice_in_dim(tile_values, first, stride, 0)
        rows_here = lax.dynamic_slice_in_dim(local_rows, first, stride, 0)
        cols_here = lax.dynamic_slice_in_dim(gathered_slot, first, stride, 0)
        live_here = (first + jnp.arange(stride) < live_count).astype(jnp.float32)
        picked = jnp.take(gathered, cols_here, axis=0)
        product = jnp.einsum("tij,tjf->tif", values, picked, preferred_element_type=jnp.float32)
        return running.at[rows_here].add(product * live_here[:, None, None])

    partial_rows = lax.fori_loop(
        0, turns, forward_turn, jnp.zeros((rep_count, block, width_in), jnp.float32)
    )
    partial_rows = partial_rows.reshape(rep_count * block, width_in)
    bias_row = out_bias.astype(jnp.float32)
    summed_own = lax.psum_scatter(partial_rows, "rep", scatter_dimension=0, tiled=True)
    aggregated = (scales[:, None] * (summed_own + scaled.astype(jnp.float32))).astype(jnp.bfloat16)
    preact = jnp.dot(aggregated, weight, preferred_element_type=jnp.float32) + bias_row
    grad_pre = (cotangent.astype(jnp.float32) * silu_slope(preact)).astype(jnp.bfloat16)
    lifted_own = (scales[:, None] * grad_pre.astype(jnp.float32)).astype(jnp.bfloat16)
    lifted_group = lax.all_gather(lifted_own, "rep", axis=0, tiled=True)
    mixed = jax.nn.silu(preact).astype(jnp.bfloat16)
    weight_part = jnp.einsum("nf,ng->fg", aggregated, grad_pre, preferred_element_type=jnp.float32)
    node_total = block * row_count * rep_count
    grad_weight = lax.psum(weight_part, ("rows", "rep")) / math.sqrt(node_total)
    lifted_blocks = lifted_group.reshape(rep_count, block, width_out)

    def backward_turn(turn, running):
        first = turn * stride
        values = lax.dynamic_slice_in_dim(tile_values, first, stride, 0)
        rows_here = lax.dynamic_slice_in_dim(local_rows, first, stride, 0)
        cols_here = lax.dynamic_slice_in_dim(gathered_slot, first, stride, 0)
        live_here = (first + jnp.arange(stride) < live_count).astype(jnp.float32)
        picked = jnp.take(lifted_blocks, rows_here, axis=0)
        product = jnp.einsum("tij,tif->tjf", values, picked, preferred_element_type=jnp.float32)
        return running.at[cols_here].add(product * live_here[:, None, None])

    column_terms = lax.fori_loop(
        0, turns, backward_turn, jnp.zeros((row_count, block, width_out), jnp.float32)
    )
    column_terms = column_terms.reshape(row_count * block, width_out)
    pulled_own = lax.psum_scatter(column_terms, "rows", scatter_dimension=0, tiled=True)
    grad_scaled = (scales[:, None] * (pulled_own + lifted_own.astype(jnp.float32))).astype(
        jnp.bfloat16
    )
    grad_features = jnp.einsum(
        "ng,fg->nf", grad_scaled, weight, preferred_element_type=jnp.float32
    ).astype(jnp.bfloat16)
    return (mixed, grad_features, grad_weight)


def solution(mesh):
    in_specs = (
        P(("rows", "rep"), None),
        P(("rows", "rep")),
        P(("rows", "rep"), None, None),
        P(("rows", "rep")),
        P(("rows", "rep")),
        P(("rows", "rep")),
        P(),
        P(),
        P(("rows", "rep"), None),
    )
    out_specs = (P(("rows", "rep"), None), P(("rows", "rep"), None), P())
    return jax.shard_map(shards, mesh=mesh, in_specs=in_specs, out_specs=out_specs, check_vma=False)
```

profile of v0, /device:TPU:32, one launch (start us, length us, event | category | flops | bytes accessed | tf_op | source)
XLA Modules:
  0.0 426.3 jit_solution(3929940306829397476)
XLA Ops:
  7.9 1.5 multiply_convert_fusion.1
  10.8 88.8 %all-gather.2.cloned.1.call-done = bf16[8192,128]{1,0:T(8,128)(2,1)} async-done(((bf16[128,128]{1,0:T(8,128)(2,1)}), bf16[8192,128]{1,0:T(8,128)(2,1)}) %all-gather.2.cloned.1.call-update) | async-done | bytes 2097168 | tf_op jit(solution)/shard_map/all_gather | solution.py:31
  99.7 21.3 %while.20 = (s32[]{:T(128)}, f32[8,128,128]{2,1,0:T(8,128)S(1)}, s32[]{:T(128)}, s32[96]{0:T(128)S(1)}, bf16[96,128,128]{2,1,0:T(8,128)(2,1)}, /*index=5*/s32[96...) while((s32[]{:T(128)}, f32[8,128,128]{2,1,0:T(8,128)S(1)}, ...), condition=%wide.region_2.3_spmd, body=%wide.region_0.2_spmd.sunk | while | flops 33948772 | bytes 3150311 | solution.py:45
  100.5 2.2 gather_fusion
  102.7 1.3 convolution_multiply_fusion.4
  104.0 1.0 scatter_fusion
  105.8 2.2 gather_fusion
  108.0 1.3 convolution_multiply_fusion.4
  109.3 1.0 scatter_fusion
  111.2 2.2 gather_fusion
  113.3 1.3 convolution_multiply_fusion.4
  114.6 1.0 scatter_fusion
  116.5 2.2 gather_fusion
  118.7 1.3 convolution_multiply_fusion.4
  119.9 1.0 scatter_fusion
  121.9 77.3 %reduce-scatter.3.cloned.1.call-done = f32[128,128]{1,0:T(8,128)} async-done(((f32[1024,128]{1,0:T(8,128)}), f32[128,128]{1,0:T(8,128)}) %reduce-scatter.3.cloned.1.call-update) | async-done | bytes 65552 | tf_op jit(solution)/shard_map/reduce_scatter | solution.py:50
  199.1 0.9 multiply_convert_fusion
  200.1 0.8 multiply_convert_fusion.3
  200.9 21.2 %all_gather.7 = bf16[1024,64]{0,1:T(8,128)(2,1)S(1)} all-gather(bf16[128,64]{0,1:T(8,128)(2,1)S(1)} %get-tuple-element.135), channel_id=1, replica_groups=mesh['rows'=64,'rep'=8] {'rep'}, dimensions={0}, use_global_device_ids=true | all-gather | bytes 147456 | tf_op jit(solution)/shard_map/all_gather | solution.py:55
  222.5 14.6 %while.21 = (s32[]{:T(128)}, f32[64,128,64]{1,2,0:T(8,128)S(1)}, s32[]{:T(128)}, s32[96]{0:T(128)S(1)}, bf16[96,128,128]{2,1,0:T(8,128)(2,1)}, /*index=5*/s32[96...) while((s32[]{:T(128)}, f32[64,128,64]{1,2,0:T(8,128)S(1)}, ...), condition=%wide.region_6.7_spmd, body=%wide.region_4.6_spmd.sunk | while | flops 16974948 | bytes 1708519 | solution.py:72
  223.9 1.3 convolution_multiply_fusion.5
  225.2 0.9 scatter_fusion.1
  227.6 1.3 convolution_multiply_fusion.5
  228.9 0.9 scatter_fusion.1
  231.2 1.3 convolution_multiply_fusion.5
  232.5 0.9 scatter_fusion.1
  234.8 1.3 convolution_multiply_fusion.5
  236.2 0.9 scatter_fusion.1
  237.1 1.5 copy_bitcast_fusion
  238.7 126.5 %psum.7 = f32[128,64]{0,1:T(8,128)S(1)} all-reduce(f32[128,64]{0,1:T(8,128)S(1)} %fusion.13), channel_id=1, replica_groups=mesh['rows'=64,'rep'=8] {'rows','rep'}, use_global_device_ids=true, to_apply=%region_8.9 | all-reduce | flops 8192 | bytes 65536 | tf_op jit(solution)/shard_map/psum | solution.py:59
  365.8 52.5 %reduce-scatter.5.cloned.1.call-done = f32[128,64]{0,1:T(8,128)} async-done(((f32[8192,64]{0,1:T(8,128)}), f32[128,64]{0,1:T(8,128)}) %reduce-scatter.5.cloned.1.call-update) | async-done | bytes 32784 | tf_op jit(solution)/shard_map/reduce_scatter | solution.py:76
  418.3 1.6 convolution_convert_fusion
  (52 shorter events, 12.4 us)
Async XLA Ops:
  7.2 192.9 %copy-start = (bf16[128,64]{0,1:T(8,128)(2,1)S(1)}, bf16[128,64]{0,1:T(8,128)(2,1)}, u32[]{:S(2)}) copy-start(bf16[128,64]{0,1:T(8,128)(2,1)} %param.19) | copy-start | bytes 49156
  7.2 92.4 %all-gather.2.cloned.1.call-start = ((), (), s32[]{:S(2)}) async-start(), calls=%async_computation.2 | async-start | bytes 2129920 | tf_op jit(solution)/shard_map/all_gather | solution.py:31
  9.4 189.8 %reduce-scatter.3.cloned.1.call-start = ((), (), s32[]{:S(2)}) async-start(), calls=%async_computation.3 | async-start | bytes 589824 | tf_op jit(solution)/shard_map/reduce_scatter | solution.py:50
  99.6 22.2 %copy-start.4 = (bf16[64]{0:T(256)(128)(2,1)S(1)}, bf16[64]{0:T(256)(128)(2,1)}, u32[]{:S(2)}) copy-start(bf16[64]{0:T(256)(128)(2,1)} %param.20) | copy-start | bytes 388
  99.6 99.5 %copy-start.2 = (bf16[128,128]{1,0:T(8,128)(2,1)S(1)}, bf16[128,128]{1,0:T(8,128)(2,1)}, u32[]{:S(2)}) copy-start(bf16[128,128]{1,0:T(8,128)(2,1)} %param.13) | copy-start | bytes 98308
  99.7 100.4 %copy-start.3 = (bf16[128,64]{0,1:T(8,128)(2,1)S(1)}, bf16[128,64]{0,1:T(8,128)(2,1)}, u32[]{:S(2)}) copy-start(bf16[128,64]{0,1:T(8,128)(2,1)} %param.21) | copy-start | bytes 49156
  121.0 0.8 copy-start.1
  121.8 296.5 %reduce-scatter.5.cloned.1.call-start = ((), (), s32[]{:S(2)}) async-start(), calls=%async_computation.4 | async-start | bytes 2129920 | tf_op jit(solution)/shard_map/reduce_scatter | solution.py:76
Sparse Core Ops, SparseCore 0:
  11.9 87.6 all-gather.1
  121.9 77.1 reduce-scatter.2
  238.7 179.5 reduce-scatter.4
where the time goes:
time: 428 us; the launch traced here: 426 us
  waiting for transfers between devices  219 us (51%)
  blocking collectives  148 us (35%)
  other arithmetic  18.5 us (4%)
  between operations  14.5 us (3%)
  local copies, waits for them, and re-layouts  13.9 us (3%)
  matrix products  12.7 us (3%)
    psum x1, blocking collectives, shards(): grad_weight = lax.psum(weight_part, ('rows', 'rep')) / math.sqrt(node_total)  126 us
    all_gather x1, waiting for transfers between devices, shards(): lax.all_gather(scaled, 'rows', axis=0, tiled=True)  88.8 us
    reduce_scatter x1, waiting for transfers between devices, shards(): lax.psum_scatter(partial_rows, 'rep', scatter_dimension=0, tiled=True)  77.3 us
    reduce_scatter x1, waiting for transfers between devices, shards(): lax.psum_scatter(column_terms, 'rows', scatter_dimension=0, tiled=True)  52.5 us
    all_gather x1, blocking collectives, shards(): lifted_group = lax.all_gather(lifted_own, 'rep', axis=0, tiled=True)  21.2 us
    gather x4, local copies, waits for them, and re-layouts, forward_turn(): picked = jnp.take(gathered, cols_here, axis=0)  8.75 us
  transfers between devices with their start and end apart: 3, of which 3 were waited for; matrix products, arithmetic and copies ran while one was open for 0% of the time, Pallas kernels for 0%

commit v1 on v0

v1 whole, which is shorter than its diff:
```python
import numpy as np

import jax
import jax.numpy as jnp
from jax import lax
from jax.experimental import pallas as pl
from jax.experimental.pallas import tpu as pltpu
from jax.sharding import Mesh, PartitionSpec as P

N_Z, N_X, N_C, N_Y = 8, 4, 2, 8
BLOCK = 128
F_IN = 128
F_OUT = 64
CHUNK = 8
HALF = N_X * N_Z
VMEM_BYTES = 32 * 1024 * 1024
f32 = jnp.float32
bf16 = jnp.bfloat16


def scale_row(degrees_ref):
    return lax.rsqrt(degrees_ref[...].astype(f32) + 1.0)


def scale_square(degrees_ref):
    return jnp.transpose(jnp.broadcast_to(scale_row(degrees_ref), (BLOCK, BLOCK)))


def place_of(col, core):
    owner = lax.shift_right_logical(col, 3)
    z = lax.shift_right_logical(owner, 3)
    x = jnp.bitwise_and(lax.shift_right_logical(owner, 1), 3)
    other = jnp.bitwise_xor(jnp.bitwise_and(owner, 1), core)
    return other * HALF + x * N_Z + z


def start_kernel(degrees_ref, features_ref, scaled_ref):
    scaled = (scale_square(degrees_ref) * features_ref[...].astype(f32)).astype(bf16)
    scaled_ref[...] = jnp.broadcast_to(scaled[None], scaled_ref.shape)


def chunk_copy(values_ref, held, sems, i):
    return pltpu.make_async_copy(
        values_ref.at[pl.ds(i * CHUNK, CHUNK)], held.at[pl.ds(i * CHUNK, CHUNK)], sems.at[i]
    )


def forward_kernel(
    rows_ref, cols_ref, count_ref, core_ref, own_ref, other_ref, values_ref, out_ref, held, gathered, acc, sems, gsems
):
    count = count_ref[0]
    core = core_ref[0]
    chunks = lax.div(count + (CHUNK - 1), CHUNK)
    own_copy = pltpu.make_async_copy(own_ref, gathered.at[pl.ds(0, HALF)], gsems.at[0])
    other_copy = pltpu.make_async_copy(other_ref, gathered.at[pl.ds(HALF, HALF)], gsems.at[1])
    own_copy.start()
    other_copy.start()

    def start(i, carry):
        chunk_copy(values_ref, held, sems, i).start()
        return carry

    lax.fori_loop(0, chunks, start, 0)
    acc[...] = jnp.zeros_like(acc)
    own_copy.wait()
    other_copy.wait()

    def chunk(i, carry):
        chunk_copy(values_ref, held, sems, i).wait()
        for g in range(0, CHUNK, 4):
            products = []
            for k in range(g, g + 4):
                t = i * CHUNK + k
                place = place_of(cols_ref[t], core)
                products.append(jnp.dot(held[t], gathered[place], preferred_element_type=f32))
            for k in range(g, g + 4):
                t = i * CHUNK + k
                row = jnp.where(t < count, jnp.bitwise_and(rows_ref[t], N_Y - 1), N_Y)
                acc[row] += products[k - g]
        return carry

    lax.fori_loop(0, chunks, chunk, 0)
    out_ref[...] = acc[0:N_Y].astype(bf16)


def middle_kernel(
    degrees_ref, parts_ref, scaled_ref, weight_ref, bias_ref, cotangent_ref, mixed_ref, send_ref
):
    total = jnp.sum(parts_ref[...].astype(f32), axis=0) + scaled_ref[0].astype(f32)
    aggregated = (scale_square(degrees_ref) * total).astype(bf16)
    preact = (
        lax.dot_general(weight_ref[...], aggregated, (((1,), (1,)), ((), ())), preferred_element_type=f32)
        + bias_ref[...]
    )
    gate = jax.nn.sigmoid(preact)
    mixed_ref[...] = (preact * gate).astype(bf16)
    slope = gate * (1.0 + preact * (1.0 - gate))
    grad_pre = (cotangent_ref[...].astype(f32) * slope).astype(bf16)
    lifted = (scale_row(degrees_ref) * grad_pre.astype(f32)).astype(bf16)
    weight_part = jnp.dot(grad_pre, aggregated, preferred_element_type=f32).astype(bf16)
    send_ref[:, 0] = jnp.broadcast_to(lifted[None], (N_Y, F_OUT, BLOCK))
    send_ref[:, 1] = jnp.broadcast_to(weight_part[None], (N_Y, F_OUT, F_IN))


def backward_kernel(
    rows_ref, cols_ref, count_ref, core_ref, group_ref, values_ref, keep_ref, send_ref, held, acc, sems
):
    count = count_ref[0]
    core = core_ref[0]
    chunks = lax.div(count + (CHUNK - 1), CHUNK)

    def start(i, carry):
        chunk_copy(values_ref, held, sems, i).start()
        return carry

    lax.fori_loop(0, chunks, start, 0)
    acc[...] = jnp.zeros_like(acc)

    def chunk(i, carry):
        chunk_copy(values_ref, held, sems, i).wait()
        for g in range(0, CHUNK, 4):
            products = []
            for k in range(g, g + 4):
                t = i * CHUNK + k
                row = jnp.bitwise_and(rows_ref[t], N_Y - 1)
                products.append(jnp.dot(group_ref[row, 0], held[t], preferred_element_type=f32))
            for k in range(g, g + 4):
                t = i * CHUNK + k
                place = jnp.where(t < count, place_of(cols_ref[t], core), 2 * HALF)
                acc[place] += products[k - g]
        return carry

    lax.fori_loop(0, chunks, chunk, 0)
    weight_part = jnp.sum(group_ref[:, 1].astype(f32), axis=0).astype(bf16)
    for x in range(N_X):
        keep_ref[x, 0:N_Z] = acc[x * N_Z : (x + 1) * N_Z].astype(bf16)
        send_ref[x, 0:N_Z] = acc[HALF + x * N_Z : HALF + (x + 1) * N_Z].astype(bf16)
        keep_ref[x, N_Z] = weight_part
        send_ref[x, N_Z] = weight_part


def core_sum_kernel(keep_ref, recv_ref, out_ref):
    out_ref[...] = (keep_ref[...].astype(f32) + recv_ref[...].astype(f32)).astype(bf16)


def x_sum_kernel(recv_ref, out_ref):
    total = jnp.sum(recv_ref[...].astype(f32), axis=0).astype(bf16)
    out_ref[:, 0] = total[0:N_Z]
    out_ref[:, 1] = jnp.broadcast_to(total[N_Z][None], (N_Z, F_OUT, F_IN))


def final_kernel(degrees_ref, recv_ref, sent_ref, weight_ref, grad_features_ref, grad_weight_ref):
    total = jnp.sum(recv_ref[...].astype(f32), axis=0)
    grad_scaled = scale_row(degrees_ref) * (total[0] + sent_ref[0, 0].astype(f32))
    turned = jnp.transpose(grad_scaled).astype(bf16)
    grad_features_ref[...] = jnp.dot(turned, weight_ref[...], preferred_element_type=f32).astype(bf16)
    node_total = BLOCK * N_Z * N_X * N_C * N_Y
    grad_weight_ref[...] = total[1] * (1.0 / np.sqrt(node_total))


def vmem():
    return pl.BlockSpec(memory_space=pltpu.VMEM)


def smem():
    return pl.BlockSpec(memory_space=pltpu.SMEM)


def shards(
    features, degrees, tile_values, tile_row, tile_col, tile_count, weight, out_bias, cotangent
):
    slots = tile_values.shape[0]
    core = lax.axis_index("c").astype(jnp.int32).reshape(1)
    degrees = degrees.reshape(1, BLOCK)
    weight_t = weight.T
    cotangent_t = cotangent.T
    bias = jnp.broadcast_to(out_bias.astype(f32)[:, None], (F_OUT, BLOCK))
    params = pltpu.CompilerParams(vmem_limit_bytes=VMEM_BYTES)

    scaled = pl.pallas_call(
        start_kernel,
        out_shape=jax.ShapeDtypeStruct((N_Z, BLOCK, F_IN), bf16),
        in_specs=[vmem(), vmem()],
        out_specs=vmem(),
        compiler_params=params,
        name="start",
    )(degrees, features)
    by_z = lax.all_to_all(scaled, "z", 0, 0)
    by_xz = lax.all_to_all(jnp.broadcast_to(by_z[None], (N_X,) + by_z.shape), "x", 0, 0)
    own = by_xz.reshape(HALF, BLOCK, F_IN)
    other = lax.ppermute(own, "c", [(0, 1), (1, 0)])

    parts = pl.pallas_call(
        forward_kernel,
        out_shape=jax.ShapeDtypeStruct((N_Y, BLOCK, F_IN), bf16),
        in_specs=[smem()] * 4 + [pl.BlockSpec(memory_space=pl.ANY)] * 3,
        out_specs=vmem(),
        scratch_shapes=[
            pltpu.VMEM((slots, BLOCK, BLOCK), bf16),
            pltpu.VMEM((2 * HALF, BLOCK, F_IN), bf16),
            pltpu.VMEM((N_Y + 1, BLOCK, F_IN), f32),
            pltpu.SemaphoreType.DMA((slots // CHUNK,)),
            pltpu.SemaphoreType.DMA((2,)),
        ],
        compiler_params=params,
        name="forward",
    )(tile_row, tile_col, tile_count, core, own, other, tile_values)
    parts = lax.all_to_all(parts, "y", 0, 0)

    mixed_t, send = pl.pallas_call(
        middle_kernel,
        out_shape=(
            jax.ShapeDtypeStruct((F_OUT, BLOCK), bf16),
            jax.ShapeDtypeStruct((N_Y, 2, F_OUT, BLOCK), bf16),
        ),
        in_specs=[vmem()] * 6,
        out_specs=(vmem(), vmem()),
        compiler_params=params,
        name="middle",
    )(degrees, parts, scaled, weight_t, bias, cotangent_t)
    group = lax.all_to_all(send, "y", 0, 0)

    half = jax.ShapeDtypeStruct((N_X, N_Z + 1, F_OUT, BLOCK), bf16)
    keep, away = pl.pallas_call(
        backward_kernel,
        out_shape=(half, half),
        in_specs=[smem()] * 4 + [vmem(), pl.BlockSpec(memory_space=pl.ANY)],
        out_specs=(vmem(), vmem()),
        scratch_shapes=[
            pltpu.VMEM((slots, BLOCK, BLOCK), bf16),
            pltpu.VMEM((2 * HALF + 1, F_OUT, BLOCK), f32),
            pltpu.SemaphoreType.DMA((slots // CHUNK,)),
        ],
        compiler_params=params,
        name="backward",
    )(tile_row, tile_col, tile_count, core, group, tile_values)
    recv = lax.ppermute(away, "c", [(0, 1), (1, 0)])
    by_core = pl.pallas_call(
        core_sum_kernel,
        out_shape=half,
        in_specs=[vmem()] * 2,
        out_specs=vmem(),
        compiler_params=params,
        name="core_sum",
    )(keep, recv)
    by_x = lax.all_to_all(by_core, "x", 0, 0)
    by_x = pl.pallas_call(
        x_sum_kernel,
        out_shape=jax.ShapeDtypeStruct((N_Z, 2, F_OUT, BLOCK), bf16),
        in_specs=[vmem()],
        out_specs=vmem(),
        compiler_params=params,
        name="x_sum",
    )(by_x)
    last = lax.all_to_all(by_x, "z", 0, 0)
    grad_features, grad_weight_t = pl.pallas_call(
        final_kernel,
        out_shape=(
            jax.ShapeDtypeStruct((BLOCK, F_IN), bf16),
            jax.ShapeDtypeStruct((F_OUT, F_IN), f32),
        ),
        in_specs=[vmem()] * 4,
        out_specs=(vmem(), vmem()),
        compiler_params=params,
        name="final",
    )(degrees, last, send, weight_t)
    return (mixed_t.T, grad_features, grad_weight_t.T)


def solution(mesh):
    devices = np.asarray(mesh.devices).reshape(N_Z, N_X, N_C, N_Y)
    fine = Mesh(devices, ("z", "x", "c", "y"))
    every = ("z", "x", "c", "y")
    in_specs = (
        P(every, None),
        P(every),
        P(every, None, None),
        P(every),
        P(every),
        P(every),
        P(),
        P(),
        P(every, None),
    )
    out_specs = (P(every, None), P(every, None), P())
    return jax.shard_map(shards, mesh=fine, in_specs=in_specs, out_specs=out_specs, check_vma=False)
```

time: 428 us -> 121 us (0.28)
  the two profiles are of different devices: /device:TPU:32 before, /device:TPU:8 now
where the time goes in v1:
time: 121 us
  blocking collectives  103 us (85%)
  Pallas kernels  6.61 us (5%)
  waiting for transfers between devices  4.29 us (4%)
  starting transfers between devices  3.97 us (3%)
  local copies, waits for them, and re-layouts  1.92 us (2%)
  between operations  1.38 us (1%)
    all_to_all x1, blocking collectives, shards(): by_z = lax.all_to_all(scaled, 'z', 0, 0)  22 us
    all_to_all x1, blocking collectives, shards(): parts = lax.all_to_all(parts, 'y', 0, 0)  20.2 us
    all_to_all x1, blocking collectives, shards(): lax.all_to_all(jnp.broadcast_to(by_z[None], (N_X,) + by_z.shape), 'x', 0, 0)  17.5 us
    all_to_all x1, blocking collectives, shards(): last = lax.all_to_all(by_x, 'z', 0, 0)  14.9 us
    all_to_all x1, blocking collectives, shards(): by_x = lax.all_to_all(by_core, 'x', 0, 0)  14.5 us
    all_to_all x1, blocking collectives, shards(): group = lax.all_to_all(send, 'y', 0, 0)  13.5 us
    pallas_call x1, Pallas kernels, shards(): pl.pallas_call(forward_kernel, out_shape=jax.ShapeDtypeStruct((N_Y, BLOCK...  2.96 us
  transfers between devices with their start and end apart: 2, of which 2 were waited for; matrix products, arithmetic and copies ran while one was open for 0% of the time, Pallas kernels for 0%

profile of v1, /device:TPU:8, one launch (start us, length us, event | category | flops | bytes accessed | tf_op | source)
XLA Modules:
  0.0 120.7 jit_solution(3050264846663462035)
XLA Ops:
  0.6 0.0 copy-start
  0.6 0.0 copy-start.2
  0.7 0.9 copy-done.2
  1.6 0.0 copy-start.4
  1.6 0.7 copy-done.4
  2.2 0.0 copy-start.6
  2.3 0.1 start.1.scaled_ref
  2.4 22.0 %all_to_all.30 = bf16[8,128,128]{2,1,0:T(8,128)(2,1)S(1)} all-to-all(bf16[8,128,128]{2,1,0:T(8,128)(2,1)S(1)} %start.1.scaled_ref), channel_id=1, replica_groups=mesh['z'=8,'x'=4,'c'=2,'y'=8] {'z'}, dimensions={0} | all-to-all | bytes 524288 | tf_op jit(solution)/shard_map/all_to_all | solution.py:188
  24.4 0.2 broadcast_in_dim.4
  24.6 17.5 %all_to_all.31 = bf16[4,8,128,128]{3,2,1,0:T(8,128)(2,1)} all-to-all(bf16[4,8,128,128]{3,2,1,0:T(8,128)(2,1)S(1)} %broadcast_in_dim.4), channel_id=1, replica_groups=mesh['z'=8,'x'=4,'c'=2,'y'=8] {'x'}, dimensions={0} | all-to-all | bytes 2097152 | tf_op jit(solution)/shard_map/all_to_all | solution.py:189
  42.1 2.1 %collective-permute-start = (bf16[32,128,128]{2,1,0:T(8,128)(2,1)}, bf16[32,128,128]{2,1,0:T(8,128)(2,1)}, u32[]{:S(2)}, u32[]{:S(2)}) collective-permute-start(bf16[32,128,128]{2,1,0:T(8,128)(2,1)} %bitcast.2.own_ref), channel_id=1, source_target_pairs={{0,8},{8,0},{1,9},{9,1},{2,10},{10,2},{3,11},{11,3},{4,12},{12,4},... | collective-permute-start | bytes 3145736 | tf_op jit(solution)/shard_map/ppermute | solution.py:191
  44.8 2.3 %collective-permute-done.other_ref = bf16[32,128,128]{2,1,0:T(8,128)(2,1)} collective-permute-done((bf16[32,128,128]{2,1,0:T(8,128)(2,1)}, bf16[32,128,128]{2,1,0:T(8,128)(2,1)}, u32[]{:S(2)}, u32[]{:S(2)}) %collective-permute-start) | collective-permute-done | bytes 1048608 | tf_op jit(solution)/shard_map/ppermute | solution.py:191
  47.1 0.0 copy-done
  47.1 0.0 copy-done.6
  47.1 0.0 copy-done.7
  47.2 3.0 %forward.1 = bf16[8,128,128]{2,1,0:T(8,128)(2,1)S(1)} custom-call(s32[96]{0:T(128)S(1)} %copy-done.6, s32[96]{0:T(128)S(1)} %copy-done.7, s32[1]{0:T(128)S(6)} %copy.12.count_ref, s32[1]{0:T(128)} %bitcast.1.core_ref, bf16[32,128,128]{2,1,0:T(8,128)(2,1)} %bitcast.2.own_ref, bf16[32,128,128]{2,1,0:T(8,128)(2,1)} %collective-permute-done.other_ref, ...), custom_call_target="tpu_custom_call" | custom-call | tf_op jit(solution)/shard_map/forward/pallas_call | solution.py:193
  50.1 20.2 %all_to_all.32.parts_ref = bf16[8,128,128]{2,1,0:T(8,128)(2,1)S(1)} all-to-all(bf16[8,128,128]{2,1,0:T(8,128)(2,1)S(1)} %forward.1), channel_id=1, replica_groups=mesh['z'=8,'x'=4,'c'=2,'y'=8] {'y'}, dimensions={0} | all-to-all | bytes 524288 | tf_op jit(solution)/shard_map/all_to_all | solution.py:208
  70.3 0.0 copy-done.8
  70.3 0.1 broadcast_in_dim.5.bias_ref
  70.4 0.0 copy-done.1
  70.4 0.0 copy-done.3
  70.4 0.0 copy-done.5
  70.4 0.9 middle.1
  71.3 13.5 %all_to_all.33.group_ref = bf16[8,2,64,128]{3,2,1,0:T(8,128)(2,1)S(1)} all-to-all(bf16[8,2,64,128]{3,2,1,0:T(8,128)(2,1)S(1)} %get-tuple-element.10.sent_ref), channel_id=1, replica_groups=mesh['z'=8,'x'=4,'c'=2,'y'=8] {'y'}, dimensions={0} | all-to-all | bytes 524288 | tf_op jit(solution)/shard_map/all_to_all | solution.py:221
  84.8 1.6 %backward.1 = (bf16[4,9,64,128]{3,2,1,0:T(8,128)(2,1)S(1)}, bf16[4,9,64,128]{3,2,1,0:T(8,128)(2,1)S(1)}) custom-call(s32[96]{0:T(128)S(1)} %copy-done.6, s32[96]{0:T(128)S(1)} %copy-done.7, s32[1]{0:T(128)S(6)} %copy.12.count_ref, s32[1]{0:T(128)} %bitcast.1.core_ref, bf16[8,2,64,128]{3,2,1,0:T(8,128)(2,1)S(1)} %all_to_all.33.group_ref, ...), custom_call_target="tpu_custom_call" | custom-call | tf_op jit(solution)/shard_map/backward/pallas_call | solution.py:224
  86.4 1.9 %collective-permute-start.1 = (bf16[4,9,64,128]{3,2,1,0:T(8,128)(2,1)S(1)}, bf16[4,9,64,128]{3,2,1,0:T(8,128)(2,1)S(1)}, u32[]{:S(2)}, u32[]{:S(2)}) collective-permute-start(bf16[4,9,64,128]{3,2,1,0:T(8,128)(2,1)S(1)} %get-tuple-element.12), channel_id=1, source_target_pairs={{0,8},{8,0},{1,9},{9,1},{2,10},{10,2},{3,11},{11,3},{4,12},{12,4},... | collective-permute-start | bytes 1769480 | tf_op jit(solution)/shard_map/ppermute | solution.py:237
  88.3 2.0 %collective-permute-done.1.recv_ref = bf16[4,9,64,128]{3,2,1,0:T(8,128)(2,1)S(1)} collective-permute-done((bf16[4,9,64,128]{3,2,1,0:T(8,128)(2,1)S(1)}, bf16[4,9,64,128]{3,2,1,0:T(8,128)(2,1)S(1)}, u32[]{:S(2)}, u32[]{:S(2)}) %collective-permute-start.1) | collective-permute-done | bytes 589856 | tf_op jit(solution)/shard_map/ppermute | solution.py:237
  90.3 0.1 core_sum.1
  90.5 14.5 %all_to_all.34.recv_ref = bf16[4,9,64,128]{3,2,1,0:T(8,128)(2,1)S(1)} all-to-all(bf16[4,9,64,128]{3,2,1,0:T(8,128)(2,1)S(1)} %core_sum.1), channel_id=1, replica_groups=mesh['z'=8,'x'=4,'c'=2,'y'=8] {'x'}, dimensions={0} | all-to-all | bytes 1179648 | tf_op jit(solution)/shard_map/all_to_all | solution.py:246
  105.0 0.1 x_sum.1
  105.0 14.9 %all_to_all.35.recv_ref = bf16[8,2,64,128]{3,2,1,0:T(8,128)(2,1)S(1)} all-to-all(bf16[8,2,64,128]{3,2,1,0:T(8,128)(2,1)S(1)} %x_sum.1), channel_id=1, replica_groups=mesh['z'=8,'x'=4,'c'=2,'y'=8] {'z'}, dimensions={0} | all-to-all | bytes 524288 | tf_op jit(solution)/shard_map/all_to_all | solution.py:255
  119.9 0.8 final.1
  (5 shorter events, 0.0 us)
Async XLA Ops:
  0.6 46.5 %copy-start = (bf16[96,128,128]{2,1,0:T(8,128)(2,1)S(1)}, bf16[96,128,128]{2,1,0:T(8,128)(2,1)}, u32[]{:S(2)}) copy-start(bf16[96,128,128]{2,1,0:T(8,128)(2,1)} %values_ref.3) | copy-start | bytes 9437188
  0.6 0.9 copy-start.2
  1.6 0.7 copy-start.4
  2.2 44.9 %copy-start.6 = (s32[96]{0:T(128)S(1)}, s32[96]{0:T(128)}, u32[]{:S(2)}) copy-start(s32[96]{0:T(128)} %rows_ref.3) | copy-start | bytes 1156
  2.3 44.9 %copy-start.7 = (s32[96]{0:T(128)S(1)}, s32[96]{0:T(128)}, u32[]{:S(2)}) copy-start(s32[96]{0:T(128)} %cols_ref.3) | copy-start | bytes 1156
  42.1 28.2 %copy-start.8 = (bf16[64]{0:T(256)(128)(2,1)S(1)}, bf16[64]{0:T(256)(128)(2,1)}, u32[]{:S(2)}) copy-start(bf16[64]{0:T(256)(128)(2,1)} %param.16) | copy-start | bytes 388
  42.1 28.3 %copy-start.1 = (bf16[128,64]{0,1:T(8,128)(2,1)S(1)}, bf16[128,64]{0,1:T(8,128)(2,1)}, u32[]{:S(2)}) copy-start(bf16[128,64]{0,1:T(8,128)(2,1)} %param.15) | copy-start | bytes 49156
  42.1 28.3 %copy-start.3 = (bf16[128,64]{0,1:T(8,128)(2,1)S(1)}, bf16[128,64]{0,1:T(8,128)(2,1)}, u32[]{:S(2)}) copy-start(bf16[128,64]{0,1:T(8,128)(2,1)} %param.17) | copy-start | bytes 49156
  42.1 28.3 %copy-start.5 = (s32[128]{0:T(128)S(1)}, s32[128]{0:T(128)}, u32[]{:S(2)}) copy-start(s32[128]{0:T(128)} %param.10) | copy-start | bytes 1540
  42.1 5.0 %collective-permute-start = (bf16[32,128,128]{2,1,0:T(8,128)(2,1)}, bf16[32,128,128]{2,1,0:T(8,128)(2,1)}, u32[]{:S(2)}, u32[]{:S(2)}) collective-permute-start(bf16[32,128,128]{2,1,0:T(8,128)(2,1)} %bitcast.2.own_ref), channel_id=1, source_target_pairs={{0,8},{8,0},{1,9},{9,1},{2,10},{10,2},{3,11},{11,3},{4,12},{12,4},... | collective-permute-start | bytes 3145736 | tf_op jit(solution)/shard_map/ppermute | solution.py:191
  86.4 3.9 %collective-permute-start.1 = (bf16[4,9,64,128]{3,2,1,0:T(8,128)(2,1)S(1)}, bf16[4,9,64,128]{3,2,1,0:T(8,128)(2,1)S(1)}, u32[]{:S(2)}, u32[]{:S(2)}) collective-permute-start(bf16[4,9,64,128]{3,2,1,0:T(8,128)(2,1)S(1)} %get-tuple-element.12), channel_id=1, source_target_pairs={{0,8},{8,0},{1,9},{9,1},{2,10},{10,2},{3,11},{11,3},{4,12},{12,4},... | collective-permute-start | bytes 1769480 | tf_op jit(solution)/shard_map/ppermute | solution.py:237

commit v2 on v1

--- a/solution.py
+++ b/solution.py
@@ -11,9 +11,10 @@
 BLOCK = 128
 F_IN = 128
 F_OUT = 64
-CHUNK = 8
+CHUNK = 48
+GROUP = 8
 HALF = N_X * N_Z
-VMEM_BYTES = 32 * 1024 * 1024
+VMEM_BYTES = 16 * 1024 * 1024
 f32 = jnp.float32
 bf16 = jnp.bfloat16
 
@@ -34,52 +35,40 @@
     return other * HALF + x * N_Z + z
 
 
-def start_kernel(degrees_ref, features_ref, scaled_ref):
-    scaled = (scale_square(degrees_ref) * features_ref[...].astype(f32)).astype(bf16)
+def start_kernel(degrees_ref, features_ref, scaled_ref, degrees_here, features_here, sems):
+    degrees_copy = pltpu.make_async_copy(degrees_ref, degrees_here, sems.at[0])
+    features_copy = pltpu.make_async_copy(features_ref, features_here, sems.at[1])
+    degrees_copy.start()
+    features_copy.start()
+    degrees_copy.wait()
+    square = scale_square(degrees_here)
+    features_copy.wait()
+    scaled = (square * features_here[...].astype(f32)).astype(bf16)
     scaled_ref[...] = jnp.broadcast_to(scaled[None], scaled_ref.shape)
 
 
-def chunk_copy(values_ref, held, sems, i):
-    return pltpu.make_async_copy(
-        values_ref.at[pl.ds(i * CHUNK, CHUNK)], held.at[pl.ds(i * CHUNK, CHUNK)], sems.at[i]
-    )
-
-
 def forward_kernel(
-    rows_ref, cols_ref, count_ref, core_ref, own_ref, other_ref, values_ref, out_ref, held, gathered, acc, sems, gsems
+    rows_ref, cols_ref, count_ref, core_ref, own_ref, other_ref, values_ref, out_ref, gathered, acc
 ):
     count = count_ref[0]
     core = core_ref[0]
-    chunks = lax.div(count + (CHUNK - 1), CHUNK)
-    own_copy = pltpu.make_async_copy(own_ref, gathered.at[pl.ds(0, HALF)], gsems.at[0])
-    other_copy = pltpu.make_async_copy(other_ref, gathered.at[pl.ds(HALF, HALF)], gsems.at[1])
-    own_copy.start()
-    other_copy.start()
-
-    def start(i, carry):
-        chunk_copy(values_ref, held, sems, i).start()
+    gathered[0:HALF] = own_ref[...]
+    gathered[HALF : 2 * HALF] = other_ref[...]
+    acc[...] = jnp.zeros_like(acc)
+
+    def chunk(i, carry):
+        for g in range(0, CHUNK, GROUP):
+            slots = [i * CHUNK + g + k for k in range(GROUP)]
+            products = [
+                jnp.dot(values_ref[t], gathered[place_of(cols_ref[t], core)], preferred_element_type=f32)
+                for t in slots
+            ]
+            for t, product in zip(slots, products):
+                row = jnp.where(t < count, jnp.bitwise_and(rows_ref[t], N_Y - 1), N_Y)
+                acc[row] += product
         return carry
 
-    lax.fori_loop(0, chunks, start, 0)
-    acc[...] = jnp.zeros_like(acc)
-    own_copy.wait()
-    other_copy.wait()
-
-    def chunk(i, carry):
-        chunk_copy(values_ref, held, sems, i).wait()
-        for g in range(0, CHUNK, 4):
-            products = []
-            for k in range(g, g + 4):
-                t = i * CHUNK + k
-                place = place_of(cols_ref[t], core)
-                products.append(jnp.dot(held[t], gathered[place], preferred_element_type=f32))
-            for k in range(g, g + 4):
-                t = i * CHUNK + k
-                row = jnp.where(t < count, jnp.bitwise_and(rows_ref[t], N_Y - 1), N_Y)
-                acc[row] += products[k - g]
-        return carry
-
-    lax.fori_loop(0, chunks, chunk, 0)
+    lax.fori_loop(0, values_ref.shape[0] // CHUNK, chunk, 0)
     out_ref[...] = acc[0:N_Y].astype(bf16)
 
 
@@ -103,34 +92,29 @@
 
 
 def backward_kernel(
-    rows_ref, cols_ref, count_ref, core_ref, group_ref, values_ref, keep_ref, send_ref, held, acc, sems
+    rows_ref, cols_ref, count_ref, core_ref, group_ref, values_ref, keep_ref, send_ref, acc
 ):
     count = count_ref[0]
     core = core_ref[0]
-    chunks = lax.div(count + (CHUNK - 1), CHUNK)
-
-    def start(i, carry):
-        chunk_copy(values_ref, held, sems, i).start()
+    acc[...] = jnp.zeros_like(acc)
+
+    def chunk(i, carry):
+        for g in range(0, CHUNK, GROUP):
+            slots = [i * CHUNK + g + k for k in range(GROUP)]
+            products = [
+                jnp.dot(
+                    group_ref[jnp.bitwise_and(rows_ref[t], N_Y - 1), 0],
+                    values_ref[t],
+                    preferred_element_type=f32,
+                )
+                for t in slots
+            ]
+            for t, product in zip(slots, products):
+                place = jnp.where(t < count, place_of(cols_ref[t], core), 2 * HALF)
+                acc[place] += product
         return carry
 
-    lax.fori_loop(0, chunks, start, 0)
-    acc[...] = jnp.zeros_like(acc)
-
-    def chunk(i, carry):
-        chunk_copy(values_ref, held, sems, i).wait()
-        for g in range(0, CHUNK, 4):
-            products = []
-            for k in range(g, g + 4):
-                t = i * CHUNK + k
-                row = jnp.bitwise_and(rows_ref[t], N_Y - 1)
-                products.append(jnp.dot(group_ref[row, 0], held[t], preferred_element_type=f32))
-            for k in range(g, g + 4):
-                t = i * CHUNK + k
-                place = jnp.where(t < count, place_of(cols_ref[t], core), 2 * HALF)
-                acc[place] += products[k - g]
-        return carry
-
-    lax.fori_loop(0, chunks, chunk, 0)
+    lax.fori_loop(0, values_ref.shape[0] // CHUNK, chunk, 0)
     weight_part = jnp.sum(group_ref[:, 1].astype(f32), axis=0).astype(bf16)
     for x in range(N_X):
         keep_ref[x, 0:N_Z] = acc[x * N_Z : (x + 1) * N_Z].astype(bf16)
@@ -169,7 +153,6 @@
 def shards(
     features, degrees, tile_values, tile_row, tile_col, tile_count, weight, out_bias, cotangent
 ):
-    slots = tile_values.shape[0]
     core = lax.axis_index("c").astype(jnp.int32).reshape(1)
     degrees = degrees.reshape(1, BLOCK)
     weight_t = weight.T
@@ -180,8 +163,13 @@
     scaled = pl.pallas_call(
         start_kernel,
         out_shape=jax.ShapeDtypeStruct((N_Z, BLOCK, F_IN), bf16),
-        in_specs=[vmem(), vmem()],
-        out_specs=vmem(),
+        in_specs=[pl.BlockSpec(memory_space=pltpu.HBM)] * 2,
+        out_specs=vmem(),
+        scratch_shapes=[
+            pltpu.VMEM((1, BLOCK), jnp.int32),
+            pltpu.VMEM((BLOCK, F_IN), bf16),
+            pltpu.SemaphoreType.DMA((2,)),
+        ],
         compiler_params=params,
         name="start",
     )(degrees, features)
@@ -193,14 +181,11 @@
     parts = pl.pallas_call(
         forward_kernel,
         out_shape=jax.ShapeDtypeStruct((N_Y, BLOCK, F_IN), bf16),
-        in_specs=[smem()] * 4 + [pl.BlockSpec(memory_space=pl.ANY)] * 3,
+        in_specs=[smem()] * 4 + [vmem()] * 3,
         out_specs=vmem(),
         scratch_shapes=[
-            pltpu.VMEM((slots, BLOCK, BLOCK), bf16),
             pltpu.VMEM((2 * HALF, BLOCK, F_IN), bf16),
             pltpu.VMEM((N_Y + 1, BLOCK, F_IN), f32),
-            pltpu.SemaphoreType.DMA((slots // CHUNK,)),
-            pltpu.SemaphoreType.DMA((2,)),
         ],
         compiler_params=params,
         name="forward",
@@ -224,13 +209,9 @@
     keep, away = pl.pallas_call(
         backward_kernel,
         out_shape=(half, half),
-        in_specs=[smem()] * 4 + [vmem(), pl.BlockSpec(memory_space=pl.ANY)],
+        in_specs=[smem()] * 4 + [vmem()] * 2,
         out_specs=(vmem(), vmem()),
-        scratch_shapes=[
-            pltpu.VMEM((slots, BLOCK, BLOCK), bf16),
-            pltpu.VMEM((2 * HALF + 1, F_OUT, BLOCK), f32),
-            pltpu.SemaphoreType.DMA((slots // CHUNK,)),
-        ],
+        scratch_shapes=[pltpu.VMEM((2 * HALF + 1, F_OUT, BLOCK), f32)],
         compiler_params=params,
         name="backward",
     )(tile_row, tile_col, tile_count, core, group, tile_values)

time: 121 us -> 117 us (0.967)
  the two profiles are of different devices: /device:TPU:8 before, /device:TPU:2 now
where the time goes in v2:
time: 117 us
  blocking collectives  98.1 us (84%)
  Pallas kernels  7.1 us (6%)
  waiting for transfers between devices  4.29 us (4%)
  starting transfers between devices  3.97 us (3%)
  local copies, waits for them, and re-layouts  1.92 us (2%)
  between operations  1.38 us (1%)
    all_to_all x1, blocking collectives, shards(): by_z = lax.all_to_all(scaled, 'z', 0, 0)  22 us
    all_to_all x1, blocking collectives, shards(): parts = lax.all_to_all(parts, 'y', 0, 0)  19.1 us
    all_to_all x1, blocking collectives, shards(): lax.all_to_all(jnp.broadcast_to(by_z[None], (N_X,) + by_z.shape), 'x', 0, 0)  16.6 us
    all_to_all x1, blocking collectives, shards(): last = lax.all_to_all(by_x, 'z', 0, 0)  13.9 us
    all_to_all x1, blocking collectives, shards(): group = lax.all_to_all(send, 'y', 0, 0)  13.4 us
    all_to_all x1, blocking collectives, shards(): by_x = lax.all_to_all(by_core, 'x', 0, 0)  13.2 us
    pallas_call x1, Pallas kernels, shards(): pl.pallas_call(forward_kernel, out_shape=jax.ShapeDtypeStruct((N_Y, BLOCK...  3.06 us
  transfers between devices with their start and end apart: 2, of which 2 were waited for; matrix products, arithmetic and copies ran while one was open for 0% of the time, Pallas kernels for 0%

profile of v2, /device:TPU:2, one launch (start us, length us, event | category | flops | bytes accessed | tf_op | source)
XLA Modules:
  0.0 116.8 jit_solution(14217049465332748249)
XLA Ops:
  0.6 0.0 copy-start
  0.6 0.0 copy-start.2
  0.7 0.9 copy-done.2
  1.6 0.0 copy-start.4
  1.6 0.7 copy-done.4
  2.2 0.0 copy-start.6
  2.3 0.2 start.1.scaled_ref
  2.4 22.0 %all_to_all.30 = bf16[8,128,128]{2,1,0:T(8,128)(2,1)S(1)} all-to-all(bf16[8,128,128]{2,1,0:T(8,128)(2,1)S(1)} %start.1.scaled_ref), channel_id=1, replica_groups=mesh['z'=8,'x'=4,'c'=2,'y'=8] {'z'}, dimensions={0} | all-to-all | bytes 524288 | tf_op jit(solution)/shard_map/all_to_all | solution.py:176
  24.4 0.2 broadcast_in_dim.4
  24.7 16.6 %all_to_all.31 = bf16[4,8,128,128]{3,2,1,0:T(8,128)(2,1)} all-to-all(bf16[4,8,128,128]{3,2,1,0:T(8,128)(2,1)S(1)} %broadcast_in_dim.4), channel_id=1, replica_groups=mesh['z'=8,'x'=4,'c'=2,'y'=8] {'x'}, dimensions={0} | all-to-all | bytes 2097152 | tf_op jit(solution)/shard_map/all_to_all | solution.py:177
  41.3 2.1 %collective-permute-start = (bf16[32,128,128]{2,1,0:T(8,128)(2,1)}, bf16[32,128,128]{2,1,0:T(8,128)(2,1)}, u32[]{:S(2)}, u32[]{:S(2)}) collective-permute-start(bf16[32,128,128]{2,1,0:T(8,128)(2,1)} %bitcast.2.own_ref), channel_id=1, source_target_pairs={{0,8},{8,0},{1,9},{9,1},{2,10},{10,2},{3,11},{11,3},{4,12},{12,4},... | collective-permute-start | bytes 3145736 | tf_op jit(solution)/shard_map/ppermute | solution.py:179
  44.0 2.3 %collective-permute-done.other_ref = bf16[32,128,128]{2,1,0:T(8,128)(2,1)} collective-permute-done((bf16[32,128,128]{2,1,0:T(8,128)(2,1)}, bf16[32,128,128]{2,1,0:T(8,128)(2,1)}, u32[]{:S(2)}, u32[]{:S(2)}) %collective-permute-start) | collective-permute-done | bytes 1048608 | tf_op jit(solution)/shard_map/ppermute | solution.py:179
  46.3 0.0 copy-done
  46.3 0.0 copy-done.6
  46.3 0.0 copy-done.7
  46.3 3.1 %forward.1 = bf16[8,128,128]{2,1,0:T(8,128)(2,1)S(1)} custom-call(s32[96]{0:T(128)S(1)} %copy-done.6, s32[96]{0:T(128)S(1)} %copy-done.7, s32[1]{0:T(128)S(6)} %copy.12.count_ref, s32[1]{0:T(128)} %bitcast.1.core_ref, bf16[32,128,128]{2,1,0:T(8,128)(2,1)} %bitcast.2.own_ref, bf16[32,128,128]{2,1,0:T(8,128)(2,1)} %collective-permute-done.other_ref, ...), custom_call_target="tpu_custom_call" | custom-call | tf_op jit(solution)/shard_map/forward/pallas_call | solution.py:181
  49.4 19.1 %all_to_all.32.parts_ref = bf16[8,128,128]{2,1,0:T(8,128)(2,1)S(1)} all-to-all(bf16[8,128,128]{2,1,0:T(8,128)(2,1)S(1)} %forward.1), channel_id=1, replica_groups=mesh['z'=8,'x'=4,'c'=2,'y'=8] {'y'}, dimensions={0} | all-to-all | bytes 524288 | tf_op jit(solution)/shard_map/all_to_all | solution.py:193
  68.4 0.0 copy-done.8
  68.4 0.1 broadcast_in_dim.5.bias_ref
  68.5 0.0 copy-done.1
  68.5 0.0 copy-done.3
  68.5 0.0 copy-done.5
  68.5 0.9 middle.1
  69.4 13.4 %all_to_all.33.group_ref = bf16[8,2,64,128]{3,2,1,0:T(8,128)(2,1)S(1)} all-to-all(bf16[8,2,64,128]{3,2,1,0:T(8,128)(2,1)S(1)} %get-tuple-element.10.sent_ref), channel_id=1, replica_groups=mesh['z'=8,'x'=4,'c'=2,'y'=8] {'y'}, dimensions={0} | all-to-all | bytes 524288 | tf_op jit(solution)/shard_map/all_to_all | solution.py:206
  82.8 1.9 %backward.1 = (bf16[4,9,64,128]{3,2,1,0:T(8,128)(2,1)S(1)}, bf16[4,9,64,128]{3,2,1,0:T(8,128)(2,1)S(1)}) custom-call(s32[96]{0:T(128)S(1)} %copy-done.6, s32[96]{0:T(128)S(1)} %copy-done.7, s32[1]{0:T(128)S(6)} %copy.12.count_ref, s32[1]{0:T(128)} %bitcast.1.core_ref, bf16[8,2,64,128]{3,2,1,0:T(8,128)(2,1)S(1)} %all_to_all.33.group_ref, ...), custom_call_target="tpu_custom_call" | custom-call | tf_op jit(solution)/shard_map/backward/pallas_call | solution.py:209
  84.7 1.9 %collective-permute-start.1 = (bf16[4,9,64,128]{3,2,1,0:T(8,128)(2,1)S(1)}, bf16[4,9,64,128]{3,2,1,0:T(8,128)(2,1)S(1)}, u32[]{:S(2)}, u32[]{:S(2)}) collective-permute-start(bf16[4,9,64,128]{3,2,1,0:T(8,128)(2,1)S(1)} %get-tuple-element.12), channel_id=1, source_target_pairs={{0,8},{8,0},{1,9},{9,1},{2,10},{10,2},{3,11},{11,3},{4,12},{12,4},... | collective-permute-start | bytes 1769480 | tf_op jit(solution)/shard_map/ppermute | solution.py:218
  86.7 2.0 %collective-permute-done.1.recv_ref = bf16[4,9,64,128]{3,2,1,0:T(8,128)(2,1)S(1)} collective-permute-done((bf16[4,9,64,128]{3,2,1,0:T(8,128)(2,1)S(1)}, bf16[4,9,64,128]{3,2,1,0:T(8,128)(2,1)S(1)}, u32[]{:S(2)}, u32[]{:S(2)}) %collective-permute-start.1) | collective-permute-done | bytes 589856 | tf_op jit(solution)/shard_map/ppermute | solution.py:218
  88.6 0.1 core_sum.1
  88.8 13.2 %all_to_all.34.recv_ref = bf16[4,9,64,128]{3,2,1,0:T(8,128)(2,1)S(1)} all-to-all(bf16[4,9,64,128]{3,2,1,0:T(8,128)(2,1)S(1)} %core_sum.1), channel_id=1, replica_groups=mesh['z'=8,'x'=4,'c'=2,'y'=8] {'x'}, dimensions={0} | all-to-all | bytes 1179648 | tf_op jit(solution)/shard_map/all_to_all | solution.py:227
  101.9 0.1 x_sum.1
  102.0 13.9 %all_to_all.35.recv_ref = bf16[8,2,64,128]{3,2,1,0:T(8,128)(2,1)S(1)} all-to-all(bf16[8,2,64,128]{3,2,1,0:T(8,128)(2,1)S(1)} %x_sum.1), channel_id=1, replica_groups=mesh['z'=8,'x'=4,'c'=2,'y'=8] {'z'}, dimensions={0} | all-to-all | bytes 524288 | tf_op jit(solution)/shard_map/all_to_all | solution.py:236
  115.9 0.8 final.1
  (5 shorter events, 0.0 us)
Async XLA Ops:
  0.6 45.7 %copy-start = (bf16[96,128,128]{2,1,0:T(8,128)(2,1)S(1)}, bf16[96,128,128]{2,1,0:T(8,128)(2,1)}, u32[]{:S(2)}) copy-start(bf16[96,128,128]{2,1,0:T(8,128)(2,1)} %values_ref.3) | copy-start | bytes 9437188
  0.6 0.9 copy-start.2
  1.6 0.7 copy-start.4
  2.2 44.0 %copy-start.6 = (s32[96]{0:T(128)S(1)}, s32[96]{0:T(128)}, u32[]{:S(2)}) copy-start(s32[96]{0:T(128)} %rows_ref.3) | copy-start | bytes 1156
  2.3 44.0 %copy-start.7 = (s32[96]{0:T(128)S(1)}, s32[96]{0:T(128)}, u32[]{:S(2)}) copy-start(s32[96]{0:T(128)} %cols_ref.3) | copy-start | bytes 1156
  41.3 27.2 %copy-start.8 = (bf16[64]{0:T(256)(128)(2,1)S(1)}, bf16[64]{0:T(256)(128)(2,1)}, u32[]{:S(2)}) copy-start(bf16[64]{0:T(256)(128)(2,1)} %param.16) | copy-start | bytes 388
  41.3 27.3 %copy-start.1 = (bf16[128,64]{0,1:T(8,128)(2,1)S(1)}, bf16[128,64]{0,1:T(8,128)(2,1)}, u32[]{:S(2)}) copy-start(bf16[128,64]{0,1:T(8,128)(2,1)} %param.15) | copy-start | bytes 49156
  41.3 27.3 %copy-start.3 = (bf16[128,64]{0,1:T(8,128)(2,1)S(1)}, bf16[128,64]{0,1:T(8,128)(2,1)}, u32[]{:S(2)}) copy-start(bf16[128,64]{0,1:T(8,128)(2,1)} %param.17) | copy-start | bytes 49156
  41.3 27.3 %copy-start.5 = (s32[128]{0:T(128)S(1)}, s32[128]{0:T(128)}, u32[]{:S(2)}) copy-start(s32[128]{0:T(128)} %param.10) | copy-start | bytes 1540
  41.3 5.0 %collective-permute-start = (bf16[32,128,128]{2,1,0:T(8,128)(2,1)}, bf16[32,128,128]{2,1,0:T(8,128)(2,1)}, u32[]{:S(2)}, u32[]{:S(2)}) collective-permute-start(bf16[32,128,128]{2,1,0:T(8,128)(2,1)} %bitcast.2.own_ref), channel_id=1, source_target_pairs={{0,8},{8,0},{1,9},{9,1},{2,10},{10,2},{3,11},{11,3},{4,12},{12,4},... | collective-permute-start | bytes 3145736 | tf_op jit(solution)/shard_map/ppermute | solution.py:179
  84.7 3.9 %collective-permute-start.1 = (bf16[4,9,64,128]{3,2,1,0:T(8,128)(2,1)S(1)}, bf16[4,9,64,128]{3,2,1,0:T(8,128)(2,1)S(1)}, u32[]{:S(2)}, u32[]{:S(2)}) collective-permute-start(bf16[4,9,64,128]{3,2,1,0:T(8,128)(2,1)S(1)} %get-tuple-element.12), channel_id=1, source_target_pairs={{0,8},{8,0},{1,9},{9,1},{2,10},{10,2},{3,11},{11,3},{4,12},{12,4},... | collective-permute-start | bytes 1769480 | tf_op jit(solution)/shard_map/ppermute | solution.py:218

commit v3 on v2

--- a/solution.py
+++ b/solution.py
@@ -19,12 +19,8 @@
 bf16 = jnp.bfloat16
 
 
-def scale_row(degrees_ref):
-    return lax.rsqrt(degrees_ref[...].astype(f32) + 1.0)
-
-
-def scale_square(degrees_ref):
-    return jnp.transpose(jnp.broadcast_to(scale_row(degrees_ref), (BLOCK, BLOCK)))
+def scale_square(scales_ref):
+    return jnp.transpose(jnp.broadcast_to(scales_ref[...], (BLOCK, BLOCK)))
 
 
 def place_of(col, core):
@@ -35,26 +31,30 @@
     return other * HALF + x * N_Z + z
 
 
-def start_kernel(degrees_ref, features_ref, scaled_ref, degrees_here, features_here, sems):
-    degrees_copy = pltpu.make_async_copy(degrees_ref, degrees_here, sems.at[0])
-    features_copy = pltpu.make_async_copy(features_ref, features_here, sems.at[1])
-    degrees_copy.start()
-    features_copy.start()
-    degrees_copy.wait()
-    square = scale_square(degrees_here)
-    features_copy.wait()
-    scaled = (square * features_here[...].astype(f32)).astype(bf16)
+def start_kernel(scales_ref, features_ref, scaled_ref):
+    scaled = (scale_square(scales_ref) * features_ref[...].astype(f32)).astype(bf16)
     scaled_ref[...] = jnp.broadcast_to(scaled[None], scaled_ref.shape)
 
 
+def slot_copies(rows_ref, cols_ref, count_ref, rows, cols, count, sems):
+    pairs = ((rows_ref, rows), (cols_ref, cols), (count_ref, count))
+    return [pltpu.make_async_copy(src, dst, sems.at[i]) for i, (src, dst) in enumerate(pairs)]
+
+
 def forward_kernel(
-    rows_ref, cols_ref, count_ref, core_ref, own_ref, other_ref, values_ref, out_ref, gathered, acc
-):
-    count = count_ref[0]
-    core = core_ref[0]
+    rows_any, cols_any, count_any, own_ref, other_ref, values_ref, out_ref,
+    rows_ref, cols_ref, count_ref, gathered, acc, sems,
+):
+    copies = slot_copies(rows_any, cols_any, count_any, rows_ref, cols_ref, count_ref, sems)
+    for copy in copies:
+        copy.start()
+    core = lax.axis_index("c")
     gathered[0:HALF] = own_ref[...]
     gathered[HALF : 2 * HALF] = other_ref[...]
     acc[...] = jnp.zeros_like(acc)
+    for copy in copies:
+        copy.wait()
+    count = count_ref[0]
 
     def chunk(i, carry):
         for g in range(0, CHUNK, GROUP):
@@ -73,10 +73,10 @@
 
 
 def middle_kernel(
-    degrees_ref, parts_ref, scaled_ref, weight_ref, bias_ref, cotangent_ref, mixed_ref, send_ref
+    scales_ref, parts_ref, scaled_ref, weight_ref, bias_ref, cotangent_ref, mixed_ref, send_ref
 ):
     total = jnp.sum(parts_ref[...].astype(f32), axis=0) + scaled_ref[0].astype(f32)
-    aggregated = (scale_square(degrees_ref) * total).astype(bf16)
+    aggregated = (scale_square(scales_ref) * total).astype(bf16)
     preact = (
         lax.dot_general(weight_ref[...], aggregated, (((1,), (1,)), ((), ())), preferred_element_type=f32)
         + bias_ref[...]
@@ -85,18 +85,26 @@
     mixed_ref[...] = (preact * gate).astype(bf16)
     slope = gate * (1.0 + preact * (1.0 - gate))
     grad_pre = (cotangent_ref[...].astype(f32) * slope).astype(bf16)
-    lifted = (scale_row(degrees_ref) * grad_pre.astype(f32)).astype(bf16)
+    lifted = (scales_ref[...] * grad_pre.astype(f32)).astype(bf16)
     weight_part = jnp.dot(grad_pre, aggregated, preferred_element_type=f32).astype(bf16)
     send_ref[:, 0] = jnp.broadcast_to(lifted[None], (N_Y, F_OUT, BLOCK))
     send_ref[:, 1] = jnp.broadcast_to(weight_part[None], (N_Y, F_OUT, F_IN))
 
 
 def backward_kernel(
-    rows_ref, cols_ref, count_ref, core_ref, group_ref, values_ref, keep_ref, send_ref, acc
-):
+    rows_any, cols_any, count_any, group_ref, values_ref, mixed_ref, keep_ref, send_ref, mixed_any,
+    rows_ref, cols_ref, count_ref, acc, sems,
+):
+    copies = slot_copies(rows_any, cols_any, count_any, rows_ref, cols_ref, count_ref, sems)
+    mixed_copy = pltpu.make_async_copy(mixed_ref, mixed_any, sems.at[3])
+    for copy in copies:
+        copy.start()
+    mixed_copy.start()
+    core = lax.axis_index("c")
+    acc[...] = jnp.zeros_like(acc)
+    for copy in copies:
+        copy.wait()
     count = count_ref[0]
-    core = core_ref[0]
-    acc[...] = jnp.zeros_like(acc)
 
     def chunk(i, carry):
         for g in range(0, CHUNK, GROUP):
@@ -121,6 +129,7 @@
         send_ref[x, 0:N_Z] = acc[HALF + x * N_Z : HALF + (x + 1) * N_Z].astype(bf16)
         keep_ref[x, N_Z] = weight_part
         send_ref[x, N_Z] = weight_part
+    mixed_copy.wait()
 
 
 def core_sum_kernel(keep_ref, recv_ref, out_ref):
@@ -133,9 +142,9 @@
     out_ref[:, 1] = jnp.broadcast_to(total[N_Z][None], (N_Z, F_OUT, F_IN))
 
 
-def final_kernel(degrees_ref, recv_ref, sent_ref, weight_ref, grad_features_ref, grad_weight_ref):
+def final_kernel(scales_ref, recv_ref, sent_ref, weight_ref, grad_features_ref, grad_weight_ref):
     total = jnp.sum(recv_ref[...].astype(f32), axis=0)
-    grad_scaled = scale_row(degrees_ref) * (total[0] + sent_ref[0, 0].astype(f32))
+    grad_scaled = scales_ref[...] * (total[0] + sent_ref[0, 0].astype(f32))
     turned = jnp.transpose(grad_scaled).astype(bf16)
     grad_features_ref[...] = jnp.dot(turned, weight_ref[...], preferred_element_type=f32).astype(bf16)
     node_total = BLOCK * N_Z * N_X * N_C * N_Y
@@ -146,33 +155,29 @@
     return pl.BlockSpec(memory_space=pltpu.VMEM)
 
 
-def smem():
-    return pl.BlockSpec(memory_space=pltpu.SMEM)
+def anywhere():
+    return pl.BlockSpec(memory_space=pl.ANY)
 
 
 def shards(
     features, degrees, tile_values, tile_row, tile_col, tile_count, weight, out_bias, cotangent
 ):
-    core = lax.axis_index("c").astype(jnp.int32).reshape(1)
-    degrees = degrees.reshape(1, BLOCK)
+    slots = tile_values.shape[0]
+    scales = lax.rsqrt(degrees.astype(f32) + 1.0).reshape(1, BLOCK)
     weight_t = weight.T
     cotangent_t = cotangent.T
     bias = jnp.broadcast_to(out_bias.astype(f32)[:, None], (F_OUT, BLOCK))
+    lists = [pltpu.SMEM((slots,), jnp.int32), pltpu.SMEM((slots,), jnp.int32), pltpu.SMEM((1,), jnp.int32)]
     params = pltpu.CompilerParams(vmem_limit_bytes=VMEM_BYTES)
 
     scaled = pl.pallas_call(
         start_kernel,
         out_shape=jax.ShapeDtypeStruct((N_Z, BLOCK, F_IN), bf16),
-        in_specs=[pl.BlockSpec(memory_space=pltpu.HBM)] * 2,
-        out_specs=vmem(),
-        scratch_shapes=[
-            pltpu.VMEM((1, BLOCK), jnp.int32),
-            pltpu.VMEM((BLOCK, F_IN), bf16),
-            pltpu.SemaphoreType.DMA((2,)),
-        ],
+        in_specs=[vmem()] * 2,
+        out_specs=vmem(),
         compiler_params=params,
         name="start",
-    )(degrees, features)
+    )(scales, features)
     by_z = lax.all_to_all(scaled, "z", 0, 0)
     by_xz = lax.all_to_all(jnp.broadcast_to(by_z[None], (N_X,) + by_z.shape), "x", 0, 0)
     own = by_xz.reshape(HALF, BLOCK, F_IN)
@@ -181,18 +186,20 @@
     parts = pl.pallas_call(
         forward_kernel,
         out_shape=jax.ShapeDtypeStruct((N_Y, BLOCK, F_IN), bf16),
-        in_specs=[smem()] * 4 + [vmem()] * 3,
+        in_specs=[anywhere()] * 3 + [vmem()] * 3,
         out_specs=vmem(),
         scratch_shapes=[
+            *lists,
             pltpu.VMEM((2 * HALF, BLOCK, F_IN), bf16),
             pltpu.VMEM((N_Y + 1, BLOCK, F_IN), f32),
+            pltpu.SemaphoreType.DMA((3,)),
         ],
         compiler_params=params,
         name="forward",
-    )(tile_row, tile_col, tile_count, core, own, other, tile_values)
+    )(tile_row, tile_col, tile_count, own, other, tile_values)
     parts = lax.all_to_all(parts, "y", 0, 0)
 
-    mixed_t, send = pl.pallas_call(
+    mixed_here, send = pl.pallas_call(
         middle_kernel,
         out_shape=(
             jax.ShapeDtypeStruct((F_OUT, BLOCK), bf16),
@@ -202,19 +209,23 @@
         out_specs=(vmem(), vmem()),
         compiler_params=params,
         name="middle",
-    )(degrees, parts, scaled, weight_t, bias, cotangent_t)
+    )(scales, parts, scaled, weight_t, bias, cotangent_t)
     group = lax.all_to_all(send, "y", 0, 0)
 
     half = jax.ShapeDtypeStruct((N_X, N_Z + 1, F_OUT, BLOCK), bf16)
-    keep, away = pl.pallas_call(
+    keep, away, mixed_t = pl.pallas_call(
         backward_kernel,
-        out_shape=(half, half),
-        in_specs=[smem()] * 4 + [vmem()] * 2,
-        out_specs=(vmem(), vmem()),
-        scratch_shapes=[pltpu.VMEM((2 * HALF + 1, F_OUT, BLOCK), f32)],
+        out_shape=(half, half, jax.ShapeDtypeStruct((F_OUT, BLOCK), bf16)),
+        in_specs=[anywhere()] * 3 + [vmem()] * 3,
+        out_specs=(vmem(), vmem(), anywhere()),
+        scratch_shapes=[
+            *lists,
+            pltpu.VMEM((2 * HALF + 1, F_OUT, BLOCK), f32),
+            pltpu.SemaphoreType.DMA((4,)),
+        ],
         compiler_params=params,
         name="backward",
-    )(tile_row, tile_col, tile_count, core, group, tile_values)
+    )(tile_row, tile_col, tile_count, group, tile_values, mixed_here)
     recv = lax.ppermute(away, "c", [(0, 1), (1, 0)])
     by_core = pl.pallas_call(
         core_sum_kernel,
@@ -244,7 +255,7 @@
         out_specs=(vmem(), vmem()),
         compiler_params=params,
         name="final",
-    )(degrees, last, send, weight_t)
+    )(scales, last, send, weight_t)
     return (mixed_t.T, grad_features, grad_weight_t.T)
 
 

time: 117 us -> 115 us (0.983)
  Pallas kernels: 7.1 us -> 5.43 us
where the time goes in v3:
time: 115 us
  blocking collectives  98 us (85%)
  Pallas kernels  5.43 us (5%)
  starting transfers between devices  3.96 us (3%)
  waiting for transfers between devices  3.95 us (3%)
  between operations  1.36 us (1%)
  local copies, waits for them, and re-layouts  1.22 us (1%)
    all_to_all x1, blocking collectives, shards(): by_z = lax.all_to_all(scaled, 'z', 0, 0)  22 us
    all_to_all x1, blocking collectives, shards(): parts = lax.all_to_all(parts, 'y', 0, 0)  19.1 us
    all_to_all x1, blocking collectives, shards(): lax.all_to_all(jnp.broadcast_to(by_z[None], (N_X,) + by_z.shape), 'x', 0, 0)  16.5 us
    all_to_all x1, blocking collectives, shards(): last = lax.all_to_all(by_x, 'z', 0, 0)  13.9 us
    all_to_all x1, blocking collectives, shards(): group = lax.all_to_all(send, 'y', 0, 0)  13.4 us
    all_to_all x1, blocking collectives, shards(): by_x = lax.all_to_all(by_core, 'x', 0, 0)  13.2 us
  transfers between devices with their start and end apart: 2, of which 2 were waited for; matrix products, arithmetic and copies ran while one was open for 0% of the time, Pallas kernels for 0%

profile of v3, /device:TPU:2, one launch (start us, length us, event | category | flops | bytes accessed | tf_op | source)
XLA Modules:
  0.0 114.8 jit_solution(4750214038688390651)
XLA Ops:
  0.6 0.0 copy-start
  0.6 0.8 rsqrt_bitcast_fusion.scales_ref
  1.5 0.9 copy-done.2
  2.4 0.0 copy-start.5
  2.4 0.1 start.1.scaled_ref
  2.5 22.0 %all_to_all.30 = bf16[8,128,128]{2,1,0:T(8,128)(2,1)S(1)} all-to-all(bf16[8,128,128]{2,1,0:T(8,128)(2,1)S(1)} %start.1.scaled_ref), channel_id=1, replica_groups=mesh['z'=8,'x'=4,'c'=2,'y'=8] {'z'}, dimensions={0} | all-to-all | bytes 524288 | tf_op jit(solution)/shard_map/all_to_all | solution.py:181
  24.5 0.2 broadcast_in_dim.4
  24.7 16.5 %all_to_all.31 = bf16[4,8,128,128]{3,2,1,0:T(8,128)(2,1)S(1)} all-to-all(bf16[4,8,128,128]{3,2,1,0:T(8,128)(2,1)S(1)} %broadcast_in_dim.4), channel_id=1, replica_groups=mesh['z'=8,'x'=4,'c'=2,'y'=8] {'x'}, dimensions={0} | all-to-all | bytes 2097152 | tf_op jit(solution)/shard_map/all_to_all | solution.py:182
  41.2 0.0 copy-start.6
  41.2 0.0 copy-start.1
  41.2 0.0 copy-start.3
  41.2 2.0 %collective-permute-start = (bf16[32,128,128]{2,1,0:T(8,128)(2,1)S(1)}, bf16[32,128,128]{2,1,0:T(8,128)(2,1)S(1)}, u32[]{:S(2)}, u32[]{:S(2)}) collective-permute-start(bf16[32,128,128]{2,1,0:T(8,128)(2,1)S(1)} %bitcast.7), channel_id=1, source_target_pairs={{0,8},{8,0},{1,9},{9,1},{2,10},{10,2},{3,11},{11,3},{4,12},{12,4},... | collective-permute-start | bytes 3145736 | tf_op jit(solution)/shard_map/ppermute | solution.py:184
  43.9 2.0 %collective-permute-done.other_ref = bf16[32,128,128]{2,1,0:T(8,128)(2,1)S(1)} collective-permute-done((bf16[32,128,128]{2,1,0:T(8,128)(2,1)S(1)}, bf16[32,128,128]{2,1,0:T(8,128)(2,1)S(1)}, u32[]{:S(2)}, u32[]{:S(2)}) %collective-permute-start) | collective-permute-done | bytes 1048608 | tf_op jit(solution)/shard_map/ppermute | solution.py:184
  45.8 0.0 copy-done
  45.8 0.0 copy-done.4
  45.8 0.0 copy-done.5
  45.9 2.0 %forward.1 = bf16[8,128,128]{2,1,0:T(8,128)(2,1)S(1)} custom-call(s32[96]{0:T(128)S(1)} %copy-done.4, s32[96]{0:T(128)S(1)} %copy-done.5, s32[1]{0:T(128)S(6)} %copy.12.count_any, bf16[32,128,128]{2,1,0:T(8,128)(2,1)S(1)} %bitcast.8, bf16[32,128,128]{2,1,0:T(8,128)(2,1)S(1)} %collective-permute-done.other_ref, bf16[96,128,128]{2,1,0:T(8,128)(2,1)S(1)} %copy-done), custom_call_target="tpu_custom_call" | custom-call | tf_op jit(solution)/shard_map/forward/pallas_call | solution.py:186
  47.8 19.1 %all_to_all.32.parts_ref = bf16[8,128,128]{2,1,0:T(8,128)(2,1)S(1)} all-to-all(bf16[8,128,128]{2,1,0:T(8,128)(2,1)S(1)} %forward.1), channel_id=1, replica_groups=mesh['z'=8,'x'=4,'c'=2,'y'=8] {'y'}, dimensions={0} | all-to-all | bytes 524288 | tf_op jit(solution)/shard_map/all_to_all | solution.py:200
  66.9 0.0 copy-done.6
  66.9 0.1 broadcast_in_dim.5.bias_ref
  67.0 0.0 copy-done.1
  67.0 0.0 copy-done.3
  67.0 0.4 middle.1
  67.4 13.4 %all_to_all.33.group_ref = bf16[8,2,64,128]{3,2,1,0:T(8,128)(2,1)S(1)} all-to-all(bf16[8,2,64,128]{3,2,1,0:T(8,128)(2,1)S(1)} %get-tuple-element.10.sent_ref), channel_id=1, replica_groups=mesh['z'=8,'x'=4,'c'=2,'y'=8] {'y'}, dimensions={0} | all-to-all | bytes 524288 | tf_op jit(solution)/shard_map/all_to_all | solution.py:213
  80.8 1.9 %backward.1 = (bf16[4,9,64,128]{3,2,1,0:T(8,128)(2,1)S(1)}, bf16[4,9,64,128]{3,2,1,0:T(8,128)(2,1)S(1)}, bf16[64,128]{1,0:T(8,128)(2,1)}) custom-call(s32[96]{0:T(128)S(1)} %copy-done.4, s32[96]{0:T(128)S(1)} %copy-done.5, s32[1]{0:T(128)S(6)} %copy.12.count_any, bf16[8,2,64,128]{3,2,1,0:T(8,128)(2,1)S(1)} %all_to_all.33.group_ref, ...), custom_call_target="tpu_custom_call" | custom-call | tf_op jit(solution)/shard_map/backward/pallas_call | solution.py:216
  82.7 1.9 %collective-permute-start.1 = (bf16[4,9,64,128]{3,2,1,0:T(8,128)(2,1)S(1)}, bf16[4,9,64,128]{3,2,1,0:T(8,128)(2,1)S(1)}, u32[]{:S(2)}, u32[]{:S(2)}) collective-permute-start(bf16[4,9,64,128]{3,2,1,0:T(8,128)(2,1)S(1)} %get-tuple-element.14), channel_id=1, source_target_pairs={{0,8},{8,0},{1,9},{9,1},{2,10},{10,2},{3,11},{11,3},{4,12},{12,4},... | collective-permute-start | bytes 1769480 | tf_op jit(solution)/shard_map/ppermute | solution.py:229
  84.7 2.0 %collective-permute-done.1.recv_ref = bf16[4,9,64,128]{3,2,1,0:T(8,128)(2,1)S(1)} collective-permute-done((bf16[4,9,64,128]{3,2,1,0:T(8,128)(2,1)S(1)}, bf16[4,9,64,128]{3,2,1,0:T(8,128)(2,1)S(1)}, u32[]{:S(2)}, u32[]{:S(2)}) %collective-permute-start.1) | collective-permute-done | bytes 589856 | tf_op jit(solution)/shard_map/ppermute | solution.py:229
  86.6 0.1 core_sum.1
  86.8 13.2 %all_to_all.34.recv_ref = bf16[4,9,64,128]{3,2,1,0:T(8,128)(2,1)S(1)} all-to-all(bf16[4,9,64,128]{3,2,1,0:T(8,128)(2,1)S(1)} %core_sum.1), channel_id=1, replica_groups=mesh['z'=8,'x'=4,'c'=2,'y'=8] {'x'}, dimensions={0} | all-to-all | bytes 1179648 | tf_op jit(solution)/shard_map/all_to_all | solution.py:238
  100.0 0.1 x_sum.1
  100.0 13.9 %all_to_all.35.recv_ref = bf16[8,2,64,128]{3,2,1,0:T(8,128)(2,1)S(1)} all-to-all(bf16[8,2,64,128]{3,2,1,0:T(8,128)(2,1)S(1)} %x_sum.1), channel_id=1, replica_groups=mesh['z'=8,'x'=4,'c'=2,'y'=8] {'z'}, dimensions={0} | all-to-all | bytes 524288 | tf_op jit(solution)/shard_map/all_to_all | solution.py:247
  113.9 0.8 final.1
  (2 shorter events, 0.0 us)
Async XLA Ops:
  0.6 45.2 %copy-start = (bf16[96,128,128]{2,1,0:T(8,128)(2,1)S(1)}, bf16[96,128,128]{2,1,0:T(8,128)(2,1)}, u32[]{:S(2)}) copy-start(bf16[96,128,128]{2,1,0:T(8,128)(2,1)} %values_ref.3) | copy-start | bytes 9437188
  1.5 0.9 copy-start.2
  2.4 43.5 %copy-start.4 = (s32[96]{0:T(128)S(1)}, s32[96]{0:T(128)}, u32[]{:S(2)}) copy-start(s32[96]{0:T(128)} %rows_any.3) | copy-start | bytes 1156
  2.4 43.5 %copy-start.5 = (s32[96]{0:T(128)S(1)}, s32[96]{0:T(128)}, u32[]{:S(2)}) copy-start(s32[96]{0:T(128)} %cols_any.3) | copy-start | bytes 1156
  41.2 25.7 %copy-start.6 = (bf16[64]{0:T(256)(128)(2,1)S(1)}, bf16[64]{0:T(256)(128)(2,1)}, u32[]{:S(2)}) copy-start(bf16[64]{0:T(256)(128)(2,1)} %param.16) | copy-start | bytes 388
  41.2 25.8 %copy-start.1 = (bf16[128,64]{0,1:T(8,128)(2,1)S(1)}, bf16[128,64]{0,1:T(8,128)(2,1)}, u32[]{:S(2)}) copy-start(bf16[128,64]{0,1:T(8,128)(2,1)} %param.15) | copy-start | bytes 49156
  41.2 25.8 %copy-start.3 = (bf16[128,64]{0,1:T(8,128)(2,1)S(1)}, bf16[128,64]{0,1:T(8,128)(2,1)}, u32[]{:S(2)}) copy-start(bf16[128,64]{0,1:T(8,128)(2,1)} %param.17) | copy-start | bytes 49156
  41.2 4.7 %collective-permute-start = (bf16[32,128,128]{2,1,0:T(8,128)(2,1)S(1)}, bf16[32,128,128]{2,1,0:T(8,128)(2,1)S(1)}, u32[]{:S(2)}, u32[]{:S(2)}) collective-permute-start(bf16[32,128,128]{2,1,0:T(8,128)(2,1)S(1)} %bitcast.7), channel_id=1, source_target_pairs={{0,8},{8,0},{1,9},{9,1},{2,10},{10,2},{3,11},{11,3},{4,12},{12,4},... | collective-permute-start | bytes 3145736 | tf_op jit(solution)/shard_map/ppermute | solution.py:184
  82.7 3.9 %collective-permute-start.1 = (bf16[4,9,64,128]{3,2,1,0:T(8,128)(2,1)S(1)}, bf16[4,9,64,128]{3,2,1,0:T(8,128)(2,1)S(1)}, u32[]{:S(2)}, u32[]{:S(2)}) collective-permute-start(bf16[4,9,64,128]{3,2,1,0:T(8,128)(2,1)S(1)} %get-tuple-element.14), channel_id=1, source_target_pairs={{0,8},{8,0},{1,9},{9,1},{2,10},{10,2},{3,11},{11,3},{4,12},{12,4},... | collective-permute-start | bytes 1769480 | tf_op jit(solution)/shard_map/ppermute | solution.py:229

commit v4 on v3

--- a/solution.py
+++ b/solution.py
@@ -8,6 +8,7 @@
 from jax.sharding import Mesh, PartitionSpec as P
 
 N_Z, N_X, N_C, N_Y = 8, 4, 2, 8
+SIZES = (N_Z, N_X, N_C, N_Y)
 BLOCK = 128
 F_IN = 128
 F_OUT = 64
@@ -23,12 +24,30 @@
     return jnp.transpose(jnp.broadcast_to(scales_ref[...], (BLOCK, BLOCK)))
 
 
+def own_core():
+    return jnp.bitwise_and(lax.shift_right_logical(lax.axis_index("d"), 3), 1)
+
+
 def place_of(col, core):
     owner = lax.shift_right_logical(col, 3)
     z = lax.shift_right_logical(owner, 3)
     x = jnp.bitwise_and(lax.shift_right_logical(owner, 1), 3)
     other = jnp.bitwise_xor(jnp.bitwise_and(owner, 1), core)
-    return other * HALF + x * N_Z + z
+    return other * HALF + (N_X - 1 - x) * N_Z + (N_Z - 1 - z)
+
+
+def place_in_group(row):
+    return N_Y - 1 - jnp.bitwise_and(row, N_Y - 1)
+
+
+def exchange(blocks, axis):
+    numbers = np.moveaxis(np.arange(np.prod(SIZES)).reshape(SIZES), axis, -1)
+    groups = numbers.reshape(-1, SIZES[axis])[:, ::-1].tolist()
+    return lax.all_to_all(blocks, "d", 0, 0, axis_index_groups=groups)
+
+
+def swap_cores(blocks):
+    return lax.ppermute(blocks, "d", [(i, i ^ N_Y) for i in range(np.prod(SIZES))])
 
 
 def start_kernel(scales_ref, features_ref, scaled_ref):
@@ -48,7 +67,7 @@
     copies = slot_copies(rows_any, cols_any, count_any, rows_ref, cols_ref, count_ref, sems)
     for copy in copies:
         copy.start()
-    core = lax.axis_index("c")
+    core = own_core()
     gathered[0:HALF] = own_ref[...]
     gathered[HALF : 2 * HALF] = other_ref[...]
     acc[...] = jnp.zeros_like(acc)
@@ -64,7 +83,7 @@
                 for t in slots
             ]
             for t, product in zip(slots, products):
-                row = jnp.where(t < count, jnp.bitwise_and(rows_ref[t], N_Y - 1), N_Y)
+                row = jnp.where(t < count, place_in_group(rows_ref[t]), N_Y)
                 acc[row] += product
         return carry
 
@@ -100,7 +119,7 @@
     for copy in copies:
         copy.start()
     mixed_copy.start()
-    core = lax.axis_index("c")
+    core = own_core()
     acc[...] = jnp.zeros_like(acc)
     for copy in copies:
         copy.wait()
@@ -111,7 +130,7 @@
             slots = [i * CHUNK + g + k for k in range(GROUP)]
             products = [
                 jnp.dot(
-                    group_ref[jnp.bitwise_and(rows_ref[t], N_Y - 1), 0],
+                    group_ref[place_in_group(rows_ref[t]), 0],
                     values_ref[t],
                     preferred_element_type=f32,
                 )
@@ -178,10 +197,10 @@
         compiler_params=params,
         name="start",
     )(scales, features)
-    by_z = lax.all_to_all(scaled, "z", 0, 0)
-    by_xz = lax.all_to_all(jnp.broadcast_to(by_z[None], (N_X,) + by_z.shape), "x", 0, 0)
+    by_z = exchange(scaled, 0)
+    by_xz = exchange(jnp.broadcast_to(by_z[None], (N_X,) + by_z.shape), 1)
     own = by_xz.reshape(HALF, BLOCK, F_IN)
-    other = lax.ppermute(own, "c", [(0, 1), (1, 0)])
+    other = swap_cores(own)
 
     parts = pl.pallas_call(
         forward_kernel,
@@ -197,7 +216,7 @@
         compiler_params=params,
         name="forward",
     )(tile_row, tile_col, tile_count, own, other, tile_values)
-    parts = lax.all_to_all(parts, "y", 0, 0)
+    parts = exchange(parts, 3)
 
     mixed_here, send = pl.pallas_call(
         middle_kernel,
@@ -210,7 +229,7 @@
         compiler_params=params,
         name="middle",
     )(scales, parts, scaled, weight_t, bias, cotangent_t)
-    group = lax.all_to_all(send, "y", 0, 0)
+    group = exchange(send, 3)
 
     half = jax.ShapeDtypeStruct((N_X, N_Z + 1, F_OUT, BLOCK), bf16)
     keep, away, mixed_t = pl.pallas_call(
@@ -226,7 +245,7 @@
         compiler_params=params,
         name="backward",
     )(tile_row, tile_col, tile_count, group, tile_values, mixed_here)
-    recv = lax.ppermute(away, "c", [(0, 1), (1, 0)])
+    recv = swap_cores(away)
     by_core = pl.pallas_call(
         core_sum_kernel,
         out_shape=half,
@@ -235,7 +254,7 @@
         compiler_params=params,
         name="core_sum",
     )(keep, recv)
-    by_x = lax.all_to_all(by_core, "x", 0, 0)
+    by_x = exchange(by_core, 1)
     by_x = pl.pallas_call(
         x_sum_kernel,
         out_shape=jax.ShapeDtypeStruct((N_Z, 2, F_OUT, BLOCK), bf16),
@@ -244,7 +263,7 @@
         compiler_params=params,
         name="x_sum",
     )(by_x)
-    last = lax.all_to_all(by_x, "z", 0, 0)
+    last = exchange(by_x, 0)
     grad_features, grad_weight_t = pl.pallas_call(
         final_kernel,
         out_shape=(
@@ -260,19 +279,7 @@
 
 
 def solution(mesh):
-    devices = np.asarray(mesh.devices).reshape(N_Z, N_X, N_C, N_Y)
-    fine = Mesh(devices, ("z", "x", "c", "y"))
-    every = ("z", "x", "c", "y")
-    in_specs = (
-        P(every, None),
-        P(every),
-        P(every, None, None),
-        P(every),
-        P(every),
-        P(every),
-        P(),
-        P(),
-        P(every, None),
-    )
-    out_specs = (P(every, None), P(every, None), P())
-    return jax.shard_map(shards, mesh=fine, in_specs=in_specs, out_specs=out_specs, check_vma=False)
+    line = Mesh(np.asarray(mesh.devices).reshape(-1), ("d",))
+    in_specs = (P("d", None), P("d"), P("d", None, None), P("d"), P("d"), P("d"), P(), P(), P("d", None))
+    out_specs = (P("d", None), P("d", None), P())
+    return jax.shard_map(shards, mesh=line, in_specs=in_specs, out_specs=out_specs, check_vma=False)

time: 115 us -> 111 us (0.965)
  the two profiles are of different devices: /device:TPU:2 before, /device:TPU:56 now
where the time goes in v4:
time: 111 us; the launch traced here: 110 us
  blocking collectives  93.8 us (85%)
  Pallas kernels  5.44 us (5%)
  starting transfers between devices  3.96 us (4%)
  waiting for transfers between devices  3.95 us (4%)
  between operations  1.36 us (1%)
  local copies, waits for them, and re-layouts  1.22 us (1%)
    all_to_all x6, blocking collectives, exchange(): return lax.all_to_all(blocks, 'd', 0, 0, axis_index_groups=groups)  93.8 us
    ppermute x2, starting transfers between devices, swap_cores(): lax.ppermute(blocks, 'd', [(i, i ^ N_Y) for i in range(np.prod(SIZES))])  3.96 us
    ppermute x2, waiting for transfers between devices, swap_cores(): lax.ppermute(blocks, 'd', [(i, i ^ N_Y) for i in range(np.prod(SIZES))])  3.95 us
  transfers between devices with their start and end apart: 2, of which 2 were waited for; matrix products, arithmetic and copies ran while one was open for 0% of the time, Pallas kernels for 0%

profile of v4, /device:TPU:56, one launch (start us, length us, event | category | flops | bytes accessed | tf_op | source)
XLA Modules:
  0.0 110.5 jit_solution(10145545184962537903)
XLA Ops:
  0.6 0.0 copy-start
  0.6 0.8 rsqrt_bitcast_fusion.scales_ref
  1.5 0.0 copy-start.2
  1.5 0.9 copy-done.2
  2.4 0.0 copy-start.4
  2.4 0.0 copy-start.5
  2.4 0.1 start.1.scaled_ref
  2.5 18.7 %all_to_all.30 = bf16[8,128,128]{2,1,0:T(8,128)(2,1)S(1)} all-to-all(bf16[8,128,128]{2,1,0:T(8,128)(2,1)S(1)} %start.1.scaled_ref), channel_id=1, replica_groups={{448,384,320,256,192,128,64,0},{449,385,321,257,193,129,65,1},{450,386,..., dimensions={0} | all-to-all | bytes 524288 | tf_op jit(solution)/shard_map/all_to_all | solution.py:46
  21.2 0.2 broadcast_in_dim.4
  21.4 16.7 %all_to_all.31 = bf16[4,8,128,128]{3,2,1,0:T(8,128)(2,1)S(1)} all-to-all(bf16[4,8,128,128]{3,2,1,0:T(8,128)(2,1)S(1)} %broadcast_in_dim.4), channel_id=1, replica_groups={{48,32,16,0},{49,33,17,1},{50,34,18,2},{51,35,19,3},{52,36,20,4},{53,37..., dimensions={0} | all-to-all | bytes 2097152 | tf_op jit(solution)/shard_map/all_to_all | solution.py:46
  38.1 0.0 copy-start.6
  38.1 2.0 %collective-permute-start = (bf16[32,128,128]{2,1,0:T(8,128)(2,1)S(1)}, bf16[32,128,128]{2,1,0:T(8,128)(2,1)S(1)}, u32[]{:S(2)}, u32[]{:S(2)}) collective-permute-start(bf16[32,128,128]{2,1,0:T(8,128)(2,1)S(1)} %bitcast.7), channel_id=1, source_target_pairs={{0,8},{1,9},{2,10},{3,11},{4,12},{5,13},{6,14},{7,15},{8,0},{9,1},... | collective-permute-start | bytes 3145736 | tf_op jit(solution)/shard_map/ppermute | solution.py:50
  40.8 2.0 %collective-permute-done.other_ref = bf16[32,128,128]{2,1,0:T(8,128)(2,1)S(1)} collective-permute-done((bf16[32,128,128]{2,1,0:T(8,128)(2,1)S(1)}, bf16[32,128,128]{2,1,0:T(8,128)(2,1)S(1)}, u32[]{:S(2)}, u32[]{:S(2)}) %collective-permute-start) | collective-permute-done | bytes 1048608 | tf_op jit(solution)/shard_map/ppermute | solution.py:50
  42.8 0.0 copy-done
  42.8 0.0 copy-done.4
  42.8 0.0 copy-done.5
  42.8 2.0 %forward.1 = bf16[8,128,128]{2,1,0:T(8,128)(2,1)S(1)} custom-call(s32[96]{0:T(128)S(1)} %copy-done.4, s32[96]{0:T(128)S(1)} %copy-done.5, s32[1]{0:T(128)S(6)} %copy.12.count_any, bf16[32,128,128]{2,1,0:T(8,128)(2,1)S(1)} %bitcast.8, bf16[32,128,128]{2,1,0:T(8,128)(2,1)S(1)} %collective-permute-done.other_ref, bf16[96,128,128]{2,1,0:T(8,128)(2,1)S(1)} %copy-done), custom_call_target="tpu_custom_call" | custom-call | tf_op jit(solution)/shard_map/forward/pallas_call | solution.py:205
  44.8 16.2 %all_to_all.32.parts_ref = bf16[8,128,128]{2,1,0:T(8,128)(2,1)S(1)} all-to-all(bf16[8,128,128]{2,1,0:T(8,128)(2,1)S(1)} %forward.1), channel_id=1, replica_groups={{7,6,5,4,3,2,1,0},{15,14,13,12,11,10,9,8},{23,22,21,20,19,18,17,16},{31..., dimensions={0} | all-to-all | bytes 524288 | tf_op jit(solution)/shard_map/all_to_all | solution.py:46
  60.9 0.0 copy-done.6
  61.0 0.1 broadcast_in_dim.5.bias_ref
  61.0 0.0 copy-done.1
  61.0 0.0 copy-done.3
  61.0 0.4 middle.1
  61.4 13.5 %all_to_all.33.group_ref = bf16[8,2,64,128]{3,2,1,0:T(8,128)(2,1)S(1)} all-to-all(bf16[8,2,64,128]{3,2,1,0:T(8,128)(2,1)S(1)} %get-tuple-element.10.sent_ref), channel_id=1, replica_groups={{7,6,5,4,3,2,1,0},{15,14,13,12,11,10,9,8},{23,22,21,20,19,18,17,16},{31..., dimensions={0} | all-to-all | bytes 524288 | tf_op jit(solution)/shard_map/all_to_all | solution.py:46
  74.9 2.0 %backward.1 = (bf16[4,9,64,128]{3,2,1,0:T(8,128)(2,1)S(1)}, bf16[4,9,64,128]{3,2,1,0:T(8,128)(2,1)S(1)}, bf16[64,128]{1,0:T(8,128)(2,1)}) custom-call(s32[96]{0:T(128)S(1)} %copy-done.4, s32[96]{0:T(128)S(1)} %copy-done.5, s32[1]{0:T(128)S(6)} %copy.12.count_any, bf16[8,2,64,128]{3,2,1,0:T(8,128)(2,1)S(1)} %all_to_all.33.group_ref, ...), custom_call_target="tpu_custom_call" | custom-call | tf_op jit(solution)/shard_map/backward/pallas_call | solution.py:235
  76.8 1.9 %collective-permute-start.1 = (bf16[4,9,64,128]{3,2,1,0:T(8,128)(2,1)S(1)}, bf16[4,9,64,128]{3,2,1,0:T(8,128)(2,1)S(1)}, u32[]{:S(2)}, u32[]{:S(2)}) collective-permute-start(bf16[4,9,64,128]{3,2,1,0:T(8,128)(2,1)S(1)} %get-tuple-element.14), channel_id=1, source_target_pairs={{0,8},{1,9},{2,10},{3,11},{4,12},{5,13},{6,14},{7,15},{8,0},{9,1},... | collective-permute-start | bytes 1769480 | tf_op jit(solution)/shard_map/ppermute | solution.py:50
  78.8 2.0 %collective-permute-done.1.recv_ref = bf16[4,9,64,128]{3,2,1,0:T(8,128)(2,1)S(1)} collective-permute-done((bf16[4,9,64,128]{3,2,1,0:T(8,128)(2,1)S(1)}, bf16[4,9,64,128]{3,2,1,0:T(8,128)(2,1)S(1)}, u32[]{:S(2)}, u32[]{:S(2)}) %collective-permute-start.1) | collective-permute-done | bytes 589856 | tf_op jit(solution)/shard_map/ppermute | solution.py:50
  80.7 0.1 core_sum.1
  80.9 13.2 %all_to_all.34.recv_ref = bf16[4,9,64,128]{3,2,1,0:T(8,128)(2,1)S(1)} all-to-all(bf16[4,9,64,128]{3,2,1,0:T(8,128)(2,1)S(1)} %core_sum.1), channel_id=1, replica_groups={{48,32,16,0},{49,33,17,1},{50,34,18,2},{51,35,19,3},{52,36,20,4},{53,37..., dimensions={0} | all-to-all | bytes 1179648 | tf_op jit(solution)/shard_map/all_to_all | solution.py:46
  94.0 0.1 x_sum.1
  94.1 15.5 %all_to_all.35.recv_ref = bf16[8,2,64,128]{3,2,1,0:T(8,128)(2,1)S(1)} all-to-all(bf16[8,2,64,128]{3,2,1,0:T(8,128)(2,1)S(1)} %x_sum.1), channel_id=1, replica_groups={{448,384,320,256,192,128,64,0},{449,385,321,257,193,129,65,1},{450,386,..., dimensions={0} | all-to-all | bytes 524288 | tf_op jit(solution)/shard_map/all_to_all | solution.py:46
  109.6 0.8 final.1
  (2 shorter events, 0.0 us)
Async XLA Ops:
  0.6 42.2 %copy-start = (bf16[96,128,128]{2,1,0:T(8,128)(2,1)S(1)}, bf16[96,128,128]{2,1,0:T(8,128)(2,1)}, u32[]{:S(2)}) copy-start(bf16[96,128,128]{2,1,0:T(8,128)(2,1)} %values_ref.3) | copy-start | bytes 9437188
  1.5 0.9 copy-start.2
  2.4 40.5 %copy-start.4 = (s32[96]{0:T(128)S(1)}, s32[96]{0:T(128)}, u32[]{:S(2)}) copy-start(s32[96]{0:T(128)} %rows_any.3) | copy-start | bytes 1156
  2.4 40.5 %copy-start.5 = (s32[96]{0:T(128)S(1)}, s32[96]{0:T(128)}, u32[]{:S(2)}) copy-start(s32[96]{0:T(128)} %cols_any.3) | copy-start | bytes 1156
  38.1 22.8 %copy-start.6 = (bf16[64]{0:T(256)(128)(2,1)S(1)}, bf16[64]{0:T(256)(128)(2,1)}, u32[]{:S(2)}) copy-start(bf16[64]{0:T(256)(128)(2,1)} %param.16) | copy-start | bytes 388
  38.1 22.9 %copy-start.1 = (bf16[128,64]{0,1:T(8,128)(2,1)S(1)}, bf16[128,64]{0,1:T(8,128)(2,1)}, u32[]{:S(2)}) copy-start(bf16[128,64]{0,1:T(8,128)(2,1)} %param.15) | copy-start | bytes 49156
  38.1 22.9 %copy-start.3 = (bf16[128,64]{0,1:T(8,128)(2,1)S(1)}, bf16[128,64]{0,1:T(8,128)(2,1)}, u32[]{:S(2)}) copy-start(bf16[128,64]{0,1:T(8,128)(2,1)} %param.17) | copy-start | bytes 49156
  38.1 4.7 %collective-permute-start = (bf16[32,128,128]{2,1,0:T(8,128)(2,1)S(1)}, bf16[32,128,128]{2,1,0:T(8,128)(2,1)S(1)}, u32[]{:S(2)}, u32[]{:S(2)}) collective-permute-start(bf16[32,128,128]{2,1,0:T(8,128)(2,1)S(1)} %bitcast.7), channel_id=1, source_target_pairs={{0,8},{1,9},{2,10},{3,11},{4,12},{5,13},{6,14},{7,15},{8,0},{9,1},... | collective-permute-start | bytes 3145736 | tf_op jit(solution)/shard_map/ppermute | solution.py:50
  76.8 3.9 %collective-permute-start.1 = (bf16[4,9,64,128]{3,2,1,0:T(8,128)(2,1)S(1)}, bf16[4,9,64,128]{3,2,1,0:T(8,128)(2,1)S(1)}, u32[]{:S(2)}, u32[]{:S(2)}) collective-permute-start(bf16[4,9,64,128]{3,2,1,0:T(8,128)(2,1)S(1)} %get-tuple-element.14), channel_id=1, source_target_pairs={{0,8},{1,9},{2,10},{3,11},{4,12},{5,13},{6,14},{7,15},{8,0},{9,1},... | collective-permute-start | bytes 1769480 | tf_op jit(solution)/shard_map/ppermute | solution.py:50

commit v5 on v4

--- a/solution.py
+++ b/solution.py
@@ -28,21 +28,32 @@
     return jnp.bitwise_and(lax.shift_right_logical(lax.axis_index("d"), 3), 1)
 
 
+def turned(number):
+    low, high = jnp.bitwise_and(number, 1), lax.shift_right_logical(number, 2)
+    return lax.shift_left(low, 2) + jnp.bitwise_and(number, 2) + high
+
+
 def place_of(col, core):
     owner = lax.shift_right_logical(col, 3)
     z = lax.shift_right_logical(owner, 3)
     x = jnp.bitwise_and(lax.shift_right_logical(owner, 1), 3)
-    other = jnp.bitwise_xor(jnp.bitwise_and(owner, 1), core)
-    return other * HALF + (N_X - 1 - x) * N_Z + (N_Z - 1 - z)
-
-
-def place_in_group(row):
-    return N_Y - 1 - jnp.bitwise_and(row, N_Y - 1)
+    half = jnp.bitwise_and(owner, 1)
+    other = jnp.bitwise_xor(half, core)
+    return other * HALF + (N_X - 1 - x) * N_Z + turned(jnp.bitwise_xor(jnp.bitwise_xor(z, half), N_Z - 1))
+
+
+def place_in_group(row, core):
+    return turned(jnp.bitwise_xor(jnp.bitwise_xor(jnp.bitwise_and(row, N_Y - 1), core), N_Y - 1))
 
 
 def exchange(blocks, axis):
+    size = SIZES[axis]
     numbers = np.moveaxis(np.arange(np.prod(SIZES)).reshape(SIZES), axis, -1)
-    groups = numbers.reshape(-1, SIZES[axis])[:, ::-1].tolist()
+    cores = numbers[..., 0].reshape(-1) // N_Y % N_C
+    groups = []
+    for group, core in zip(numbers.reshape(-1, size), cores):
+        order = [k ^ 7 ^ int(core) for k in (0, 4, 2, 6, 1, 5, 3, 7)] if size == 8 else range(size)[::-1]
+        groups.append([int(group[k]) for k in order])
     return lax.all_to_all(blocks, "d", 0, 0, axis_index_groups=groups)
 
 
@@ -83,7 +94,7 @@
                 for t in slots
             ]
             for t, product in zip(slots, products):
-                row = jnp.where(t < count, place_in_group(rows_ref[t]), N_Y)
+                row = jnp.where(t < count, place_in_group(rows_ref[t], core), N_Y)
                 acc[row] += product
         return carry
 
@@ -130,7 +141,7 @@
             slots = [i * CHUNK + g + k for k in range(GROUP)]
             products = [
                 jnp.dot(
-                    group_ref[place_in_group(rows_ref[t]), 0],
+                    group_ref[place_in_group(rows_ref[t], core), 0],
                     values_ref[t],
                     preferred_element_type=f32,
                 )

time: 111 us -> 110 us (level)
  the two profiles are of different devices: /device:TPU:56 before, /device:TPU:8 now
where the time goes in v5:
time: 110 us
  blocking collectives  92.7 us (84%)
  Pallas kernels  5.68 us (5%)
  starting transfers between devices  3.96 us (4%)
  waiting for transfers between devices  3.95 us (4%)
  between operations  1.36 us (1%)
  local copies, waits for them, and re-layouts  1.22 us (1%)
    all_to_all x6, blocking collectives, exchange(): return lax.all_to_all(blocks, 'd', 0, 0, axis_index_groups=groups)  92.7 us
    ppermute x2, starting transfers between devices, swap_cores(): lax.ppermute(blocks, 'd', [(i, i ^ N_Y) for i in range(np.prod(SIZES))])  3.96 us
    ppermute x2, waiting for transfers between devices, swap_cores(): lax.ppermute(blocks, 'd', [(i, i ^ N_Y) for i in range(np.prod(SIZES))])  3.95 us
  transfers between devices with their start and end apart: 2, of which 2 were waited for; matrix products, arithmetic and copies ran while one was open for 0% of the time, Pallas kernels for 0%

profile of v5, /device:TPU:8, one launch (start us, length us, event | category | flops | bytes accessed | tf_op | source)
XLA Modules:
  0.0 109.7 jit_solution(11433859965025100582)
XLA Ops:
  0.6 0.0 copy-start
  0.6 0.8 rsqrt_bitcast_fusion.scales_ref
  1.5 0.0 copy-start.2
  1.5 0.9 copy-done.2
  2.4 0.0 copy-start.4
  2.4 0.0 copy-start.5
  2.4 0.1 start.1.scaled_ref
  2.5 19.4 %all_to_all.30 = bf16[8,128,128]{2,1,0:T(8,128)(2,1)S(1)} all-to-all(bf16[8,128,128]{2,1,0:T(8,128)(2,1)S(1)} %start.1.scaled_ref), channel_id=1, replica_groups={{448,192,320,64,384,128,256,0},{449,193,321,65,385,129,257,1},{450,194,..., dimensions={0} | all-to-all | bytes 524288 | tf_op jit(solution)/shard_map/all_to_all | solution.py:57
  21.8 0.2 broadcast_in_dim.4
  22.1 18.0 %all_to_all.31 = bf16[4,8,128,128]{3,2,1,0:T(8,128)(2,1)S(1)} all-to-all(bf16[4,8,128,128]{3,2,1,0:T(8,128)(2,1)S(1)} %broadcast_in_dim.4), channel_id=1, replica_groups={{48,32,16,0},{49,33,17,1},{50,34,18,2},{51,35,19,3},{52,36,20,4},{53,37..., dimensions={0} | all-to-all | bytes 2097152 | tf_op jit(solution)/shard_map/all_to_all | solution.py:57
  40.1 0.0 copy-start.6
  40.1 2.0 %collective-permute-start = (bf16[32,128,128]{2,1,0:T(8,128)(2,1)S(1)}, bf16[32,128,128]{2,1,0:T(8,128)(2,1)S(1)}, u32[]{:S(2)}, u32[]{:S(2)}) collective-permute-start(bf16[32,128,128]{2,1,0:T(8,128)(2,1)S(1)} %bitcast.7), channel_id=1, source_target_pairs={{0,8},{1,9},{2,10},{3,11},{4,12},{5,13},{6,14},{7,15},{8,0},{9,1},... | collective-permute-start | bytes 3145736 | tf_op jit(solution)/shard_map/ppermute | solution.py:61
  42.8 2.0 %collective-permute-done.other_ref = bf16[32,128,128]{2,1,0:T(8,128)(2,1)S(1)} collective-permute-done((bf16[32,128,128]{2,1,0:T(8,128)(2,1)S(1)}, bf16[32,128,128]{2,1,0:T(8,128)(2,1)S(1)}, u32[]{:S(2)}, u32[]{:S(2)}) %collective-permute-start) | collective-permute-done | bytes 1048608 | tf_op jit(solution)/shard_map/ppermute | solution.py:61
  44.7 0.0 copy-done
  44.7 0.0 copy-done.4
  44.7 0.0 copy-done.5
  44.7 2.1 %forward.1 = bf16[8,128,128]{2,1,0:T(8,128)(2,1)S(1)} custom-call(s32[96]{0:T(128)S(1)} %copy-done.4, s32[96]{0:T(128)S(1)} %copy-done.5, s32[1]{0:T(128)S(6)} %copy.12.count_any, bf16[32,128,128]{2,1,0:T(8,128)(2,1)S(1)} %bitcast.8, bf16[32,128,128]{2,1,0:T(8,128)(2,1)S(1)} %collective-permute-done.other_ref, bf16[96,128,128]{2,1,0:T(8,128)(2,1)S(1)} %copy-done), custom_call_target="tpu_custom_call" | custom-call | tf_op jit(solution)/shard_map/forward/pallas_call | solution.py:216
  46.8 15.0 %all_to_all.32.parts_ref = bf16[8,128,128]{2,1,0:T(8,128)(2,1)S(1)} all-to-all(bf16[8,128,128]{2,1,0:T(8,128)(2,1)S(1)} %forward.1), channel_id=1, replica_groups={{7,3,5,1,6,2,4,0},{14,10,12,8,15,11,13,9},{23,19,21,17,22,18,20,16},{30..., dimensions={0} | all-to-all | bytes 524288 | tf_op jit(solution)/shard_map/all_to_all | solution.py:57
  61.9 0.0 copy-done.6
  61.9 0.1 broadcast_in_dim.5.bias_ref
  61.9 0.0 copy-done.1
  61.9 0.0 copy-done.3
  62.0 0.4 middle.1
  62.3 13.7 %all_to_all.33.group_ref = bf16[8,2,64,128]{3,2,1,0:T(8,128)(2,1)S(1)} all-to-all(bf16[8,2,64,128]{3,2,1,0:T(8,128)(2,1)S(1)} %get-tuple-element.10.sent_ref), channel_id=1, replica_groups={{7,3,5,1,6,2,4,0},{14,10,12,8,15,11,13,9},{23,19,21,17,22,18,20,16},{30..., dimensions={0} | all-to-all | bytes 524288 | tf_op jit(solution)/shard_map/all_to_all | solution.py:57
  76.0 2.1 %backward.1 = (bf16[4,9,64,128]{3,2,1,0:T(8,128)(2,1)S(1)}, bf16[4,9,64,128]{3,2,1,0:T(8,128)(2,1)S(1)}, bf16[64,128]{1,0:T(8,128)(2,1)}) custom-call(s32[96]{0:T(128)S(1)} %copy-done.4, s32[96]{0:T(128)S(1)} %copy-done.5, s32[1]{0:T(128)S(6)} %copy.12.count_any, bf16[8,2,64,128]{3,2,1,0:T(8,128)(2,1)S(1)} %all_to_all.33.group_ref, ...), custom_call_target="tpu_custom_call" | custom-call | tf_op jit(solution)/shard_map/backward/pallas_call | solution.py:246
  78.1 1.9 %collective-permute-start.1 = (bf16[4,9,64,128]{3,2,1,0:T(8,128)(2,1)S(1)}, bf16[4,9,64,128]{3,2,1,0:T(8,128)(2,1)S(1)}, u32[]{:S(2)}, u32[]{:S(2)}) collective-permute-start(bf16[4,9,64,128]{3,2,1,0:T(8,128)(2,1)S(1)} %get-tuple-element.14), channel_id=1, source_target_pairs={{0,8},{1,9},{2,10},{3,11},{4,12},{5,13},{6,14},{7,15},{8,0},{9,1},... | collective-permute-start | bytes 1769480 | tf_op jit(solution)/shard_map/ppermute | solution.py:61
  80.0 2.0 %collective-permute-done.1.recv_ref = bf16[4,9,64,128]{3,2,1,0:T(8,128)(2,1)S(1)} collective-permute-done((bf16[4,9,64,128]{3,2,1,0:T(8,128)(2,1)S(1)}, bf16[4,9,64,128]{3,2,1,0:T(8,128)(2,1)S(1)}, u32[]{:S(2)}, u32[]{:S(2)}) %collective-permute-start.1) | collective-permute-done | bytes 589856 | tf_op jit(solution)/shard_map/ppermute | solution.py:61
  82.0 0.1 core_sum.1
  82.1 13.1 %all_to_all.34.recv_ref = bf16[4,9,64,128]{3,2,1,0:T(8,128)(2,1)S(1)} all-to-all(bf16[4,9,64,128]{3,2,1,0:T(8,128)(2,1)S(1)} %core_sum.1), channel_id=1, replica_groups={{48,32,16,0},{49,33,17,1},{50,34,18,2},{51,35,19,3},{52,36,20,4},{53,37..., dimensions={0} | all-to-all | bytes 1179648 | tf_op jit(solution)/shard_map/all_to_all | solution.py:57
  95.3 0.1 x_sum.1
  95.4 13.5 %all_to_all.35.recv_ref = bf16[8,2,64,128]{3,2,1,0:T(8,128)(2,1)S(1)} all-to-all(bf16[8,2,64,128]{3,2,1,0:T(8,128)(2,1)S(1)} %x_sum.1), channel_id=1, replica_groups={{448,192,320,64,384,128,256,0},{449,193,321,65,385,129,257,1},{450,194,..., dimensions={0} | all-to-all | bytes 524288 | tf_op jit(solution)/shard_map/all_to_all | solution.py:57
  108.9 0.8 final.1
  (2 shorter events, 0.0 us)
Async XLA Ops:
  0.6 44.1 %copy-start = (bf16[96,128,128]{2,1,0:T(8,128)(2,1)S(1)}, bf16[96,128,128]{2,1,0:T(8,128)(2,1)}, u32[]{:S(2)}) copy-start(bf16[96,128,128]{2,1,0:T(8,128)(2,1)} %values_ref.3) | copy-start | bytes 9437188
  1.5 0.9 copy-start.2
  2.4 42.4 %copy-start.4 = (s32[96]{0:T(128)S(1)}, s32[96]{0:T(128)}, u32[]{:S(2)}) copy-start(s32[96]{0:T(128)} %rows_any.3) | copy-start | bytes 1156
  2.4 42.4 %copy-start.5 = (s32[96]{0:T(128)S(1)}, s32[96]{0:T(128)}, u32[]{:S(2)}) copy-start(s32[96]{0:T(128)} %cols_any.3) | copy-start | bytes 1156
  40.1 21.8 %copy-start.6 = (bf16[64]{0:T(256)(128)(2,1)S(1)}, bf16[64]{0:T(256)(128)(2,1)}, u32[]{:S(2)}) copy-start(bf16[64]{0:T(256)(128)(2,1)} %param.16) | copy-start | bytes 388
  40.1 21.9 %copy-start.1 = (bf16[128,64]{0,1:T(8,128)(2,1)S(1)}, bf16[128,64]{0,1:T(8,128)(2,1)}, u32[]{:S(2)}) copy-start(bf16[128,64]{0,1:T(8,128)(2,1)} %param.15) | copy-start | bytes 49156
  40.1 21.9 %copy-start.3 = (bf16[128,64]{0,1:T(8,128)(2,1)S(1)}, bf16[128,64]{0,1:T(8,128)(2,1)}, u32[]{:S(2)}) copy-start(bf16[128,64]{0,1:T(8,128)(2,1)} %param.17) | copy-start | bytes 49156
  40.1 4.7 %collective-permute-start = (bf16[32,128,128]{2,1,0:T(8,128)(2,1)S(1)}, bf16[32,128,128]{2,1,0:T(8,128)(2,1)S(1)}, u32[]{:S(2)}, u32[]{:S(2)}) collective-permute-start(bf16[32,128,128]{2,1,0:T(8,128)(2,1)S(1)} %bitcast.7), channel_id=1, source_target_pairs={{0,8},{1,9},{2,10},{3,11},{4,12},{5,13},{6,14},{7,15},{8,0},{9,1},... | collective-permute-start | bytes 3145736 | tf_op jit(solution)/shard_map/ppermute | solution.py:61
  78.1 3.9 %collective-permute-start.1 = (bf16[4,9,64,128]{3,2,1,0:T(8,128)(2,1)S(1)}, bf16[4,9,64,128]{3,2,1,0:T(8,128)(2,1)S(1)}, u32[]{:S(2)}, u32[]{:S(2)}) collective-permute-start(bf16[4,9,64,128]{3,2,1,0:T(8,128)(2,1)S(1)} %get-tuple-element.14), channel_id=1, source_target_pairs={{0,8},{1,9},{2,10},{3,11},{4,12},{5,13},{6,14},{7,15},{8,0},{9,1},... | collective-permute-start | bytes 1769480 | tf_op jit(solution)/shard_map/ppermute | solution.py:61

commit v6 on v5

--- a/solution.py
+++ b/solution.py
@@ -15,6 +15,7 @@
 CHUNK = 48
 GROUP = 8
 HALF = N_X * N_Z
+OPPOSITE = N_Z // 2 * N_X + N_X // 2
 VMEM_BYTES = 16 * 1024 * 1024
 f32 = jnp.float32
 bf16 = jnp.bfloat16
@@ -31,6 +32,13 @@
 def turned(number):
     low, high = jnp.bitwise_and(number, 1), lax.shift_right_logical(number, 2)
     return lax.shift_left(low, 2) + jnp.bitwise_and(number, 2) + high
+
+
+def place_gathered(col, core):
+    owner = lax.shift_right_logical(col, 3)
+    half = jnp.bitwise_and(owner, 1)
+    chip = lax.shift_right_logical(owner, 1)
+    return jnp.bitwise_xor(half, core) * HALF + jnp.bitwise_xor(chip, half * OPPOSITE)
 
 
 def place_of(col, core):
@@ -55,6 +63,12 @@
         order = [k ^ 7 ^ int(core) for k in (0, 4, 2, 6, 1, 5, 3, 7)] if size == 8 else range(size)[::-1]
         groups.append([int(group[k]) for k in order])
     return lax.all_to_all(blocks, "d", 0, 0, axis_index_groups=groups)
+
+
+def gather_plane(copies):
+    numbers = np.arange(np.prod(SIZES)).reshape(HALF, N_C, N_Y)
+    groups = [numbers[np.arange(HALF) ^ (c * OPPOSITE), c, y].tolist() for c in range(N_C) for y in range(N_Y)]
+    return lax.all_to_all(copies, "d", 0, 0, axis_index_groups=groups)
 
 
 def swap_cores(blocks):
@@ -90,7 +104,7 @@
         for g in range(0, CHUNK, GROUP):
             slots = [i * CHUNK + g + k for k in range(GROUP)]
             products = [
-                jnp.dot(values_ref[t], gathered[place_of(cols_ref[t], core)], preferred_element_type=f32)
+                jnp.dot(values_ref[t], gathered[place_gathered(cols_ref[t], core)], preferred_element_type=f32)
                 for t in slots
             ]
             for t, product in zip(slots, products):
@@ -202,15 +216,13 @@
 
     scaled = pl.pallas_call(
         start_kernel,
-        out_shape=jax.ShapeDtypeStruct((N_Z, BLOCK, F_IN), bf16),
+        out_shape=jax.ShapeDtypeStruct((HALF, BLOCK, F_IN), bf16),
         in_specs=[vmem()] * 2,
         out_specs=vmem(),
         compiler_params=params,
         name="start",
     )(scales, features)
-    by_z = exchange(scaled, 0)
-    by_xz = exchange(jnp.broadcast_to(by_z[None], (N_X,) + by_z.shape), 1)
-    own = by_xz.reshape(HALF, BLOCK, F_IN)
+    own = gather_plane(scaled)
     other = swap_cores(own)
 
     parts = pl.pallas_call(

time: 110 us -> 112 us (1.018)
  blocking collectives: 92.7 us -> 95.1 us
    all_to_all x0 -> x1, blocking collectives: none -> 39.5 us  [gather_plane(): return lax.all_to_all(copies, 'd', 0, 0, axis_index_groups=groups)]
    all_to_all x6 -> x4, blocking collectives: 92.7 us -> 55.6 us  [exchange(): return lax.all_to_all(blocks, 'd', 0, 0, axis_index_groups=groups)]
where the time goes in v6:
time: 112 us
  blocking collectives  95.1 us (85%)
  Pallas kernels  5.61 us (5%)
  starting transfers between devices  3.96 us (4%)
  waiting for transfers between devices  3.95 us (4%)
  between operations  1.35 us (1%)
    all_to_all x4, blocking collectives, exchange(): return lax.all_to_all(blocks, 'd', 0, 0, axis_index_groups=groups)  55.6 us
    all_to_all x1, blocking collectives, gather_plane(): return lax.all_to_all(copies, 'd', 0, 0, axis_index_groups=groups)  39.5 us
    ppermute x2, starting transfers between devices, swap_cores(): lax.ppermute(blocks, 'd', [(i, i ^ N_Y) for i in range(np.prod(SIZES))])  3.96 us
    ppermute x2, waiting for transfers between devices, swap_cores(): lax.ppermute(blocks, 'd', [(i, i ^ N_Y) for i in range(np.prod(SIZES))])  3.95 us
  transfers between devices with their start and end apart: 2, of which 2 were waited for; matrix products, arithmetic and copies ran while one was open for 0% of the time, Pallas kernels for 0%

profile of v6, /device:TPU:8, one launch (start us, length us, event | category | flops | bytes accessed | tf_op | source)
XLA Modules:
  0.0 111.8 jit_solution(1543730853942756913)
XLA Ops:
  0.6 0.0 copy-start
  0.6 0.8 rsqrt_bitcast_fusion.scales_ref
  1.5 0.0 copy-start.2
  1.5 0.9 copy-done.2
  2.4 0.0 copy-start.4
  2.4 0.0 copy-start.5
  2.4 0.2 start.1.scaled_ref
  2.5 39.5 %all_to_all.25.own_ref = bf16[32,128,128]{2,1,0:T(8,128)(2,1)S(1)} all-to-all(bf16[32,128,128]{2,1,0:T(8,128)(2,1)S(1)} %start.1.scaled_ref), channel_id=1, replica_groups={{0,16,32,48,64,80,96,112,128,144,160,176,192,208,224,240,256,272,288,30..., dimensions={0} | all-to-all | bytes 2097152 | tf_op jit(solution)/shard_map/all_to_all | solution.py:71
  42.1 0.0 copy-start.6
  42.1 0.0 copy-start.1
  42.1 0.0 copy-start.3
  42.1 2.0 %collective-permute-start = (bf16[32,128,128]{2,1,0:T(8,128)(2,1)S(1)}, bf16[32,128,128]{2,1,0:T(8,128)(2,1)S(1)}, u32[]{:S(2)}, u32[]{:S(2)}) collective-permute-start(bf16[32,128,128]{2,1,0:T(8,128)(2,1)S(1)} %all_to_all.25.own_ref), channel_id=1, source_target_pairs={{0,8},{1,9},{2,10},{3,11},{4,12},{5,13},{6,14},{7,15},{8,0},{9,1},... | collective-permute-start | bytes 3145736 | tf_op jit(solution)/shard_map/ppermute | solution.py:75
  44.8 2.0 %collective-permute-done.other_ref = bf16[32,128,128]{2,1,0:T(8,128)(2,1)S(1)} collective-permute-done((bf16[32,128,128]{2,1,0:T(8,128)(2,1)S(1)}, bf16[32,128,128]{2,1,0:T(8,128)(2,1)S(1)}, u32[]{:S(2)}, u32[]{:S(2)}) %collective-permute-start) | collective-permute-done | bytes 1048608 | tf_op jit(solution)/shard_map/ppermute | solution.py:75
  46.8 0.0 copy-done
  46.8 0.0 copy-done.4
  46.8 0.0 copy-done.5
  46.8 1.9 %forward.1 = bf16[8,128,128]{2,1,0:T(8,128)(2,1)S(1)} custom-call(s32[96]{0:T(128)S(1)} %copy-done.4, s32[96]{0:T(128)S(1)} %copy-done.5, s32[1]{0:T(128)S(6)} %copy.12.count_any, bf16[32,128,128]{2,1,0:T(8,128)(2,1)S(1)} %all_to_all.25.own_ref, bf16[32,128,128]{2,1,0:T(8,128)(2,1)S(1)} %collective-permute-done.other_ref, bf16[96,128,128]{2,1,0:T(8,128)(2,1)S(1)} %copy-done), custom_call_target="tpu_custom_call" | custom-call | tf_op jit(solution)/shard_map/forward/pallas_call | solution.py:228
  48.7 15.1 %all_to_all.26.parts_ref = bf16[8,128,128]{2,1,0:T(8,128)(2,1)S(1)} all-to-all(bf16[8,128,128]{2,1,0:T(8,128)(2,1)S(1)} %forward.1), channel_id=1, replica_groups={{7,3,5,1,6,2,4,0},{14,10,12,8,15,11,13,9},{23,19,21,17,22,18,20,16},{30..., dimensions={0} | all-to-all | bytes 524288 | tf_op jit(solution)/shard_map/all_to_all | solution.py:65
  63.7 0.0 copy-done.6
  63.7 0.1 broadcast_in_dim.2.bias_ref
  63.8 0.0 copy-done.1
  63.8 0.0 copy-done.3
  63.8 0.4 middle.1
  64.2 13.7 %all_to_all.27.group_ref = bf16[8,2,64,128]{3,2,1,0:T(8,128)(2,1)S(1)} all-to-all(bf16[8,2,64,128]{3,2,1,0:T(8,128)(2,1)S(1)} %get-tuple-element.10.sent_ref), channel_id=1, replica_groups={{7,3,5,1,6,2,4,0},{14,10,12,8,15,11,13,9},{23,19,21,17,22,18,20,16},{30..., dimensions={0} | all-to-all | bytes 524288 | tf_op jit(solution)/shard_map/all_to_all | solution.py:65
  77.9 2.1 %backward.1 = (bf16[4,9,64,128]{3,2,1,0:T(8,128)(2,1)S(1)}, bf16[4,9,64,128]{3,2,1,0:T(8,128)(2,1)S(1)}, bf16[64,128]{1,0:T(8,128)(2,1)}) custom-call(s32[96]{0:T(128)S(1)} %copy-done.4, s32[96]{0:T(128)S(1)} %copy-done.5, s32[1]{0:T(128)S(6)} %copy.12.count_any, bf16[8,2,64,128]{3,2,1,0:T(8,128)(2,1)S(1)} %all_to_all.27.group_ref, ...), custom_call_target="tpu_custom_call" | custom-call | tf_op jit(solution)/shard_map/backward/pallas_call | solution.py:258
  80.0 1.9 %collective-permute-start.1 = (bf16[4,9,64,128]{3,2,1,0:T(8,128)(2,1)S(1)}, bf16[4,9,64,128]{3,2,1,0:T(8,128)(2,1)S(1)}, u32[]{:S(2)}, u32[]{:S(2)}) collective-permute-start(bf16[4,9,64,128]{3,2,1,0:T(8,128)(2,1)S(1)} %get-tuple-element.14), channel_id=1, source_target_pairs={{0,8},{1,9},{2,10},{3,11},{4,12},{5,13},{6,14},{7,15},{8,0},{9,1},... | collective-permute-start | bytes 1769480 | tf_op jit(solution)/shard_map/ppermute | solution.py:75
  81.9 2.0 %collective-permute-done.1.recv_ref = bf16[4,9,64,128]{3,2,1,0:T(8,128)(2,1)S(1)} collective-permute-done((bf16[4,9,64,128]{3,2,1,0:T(8,128)(2,1)S(1)}, bf16[4,9,64,128]{3,2,1,0:T(8,128)(2,1)S(1)}, u32[]{:S(2)}, u32[]{:S(2)}) %collective-permute-start.1) | collective-permute-done | bytes 589856 | tf_op jit(solution)/shard_map/ppermute | solution.py:75
  83.9 0.1 core_sum.1
  84.0 13.7 %all_to_all.28.recv_ref = bf16[4,9,64,128]{3,2,1,0:T(8,128)(2,1)S(1)} all-to-all(bf16[4,9,64,128]{3,2,1,0:T(8,128)(2,1)S(1)} %core_sum.1), channel_id=1, replica_groups={{48,32,16,0},{49,33,17,1},{50,34,18,2},{51,35,19,3},{52,36,20,4},{53,37..., dimensions={0} | all-to-all | bytes 1179648 | tf_op jit(solution)/shard_map/all_to_all | solution.py:65
  97.7 0.1 x_sum.1
  97.7 13.2 %all_to_all.29.recv_ref = bf16[8,2,64,128]{3,2,1,0:T(8,128)(2,1)S(1)} all-to-all(bf16[8,2,64,128]{3,2,1,0:T(8,128)(2,1)S(1)} %x_sum.1), channel_id=1, replica_groups={{448,192,320,64,384,128,256,0},{449,193,321,65,385,129,257,1},{450,194,..., dimensions={0} | all-to-all | bytes 524288 | tf_op jit(solution)/shard_map/all_to_all | solution.py:65
  110.9 0.8 final.1
Async XLA Ops:
  0.6 46.1 %copy-start = (bf16[96,128,128]{2,1,0:T(8,128)(2,1)S(1)}, bf16[96,128,128]{2,1,0:T(8,128)(2,1)}, u32[]{:S(2)}) copy-start(bf16[96,128,128]{2,1,0:T(8,128)(2,1)} %values_ref.3) | copy-start | bytes 9437188
  1.5 0.9 copy-start.2
  2.4 44.4 %copy-start.4 = (s32[96]{0:T(128)S(1)}, s32[96]{0:T(128)}, u32[]{:S(2)}) copy-start(s32[96]{0:T(128)} %rows_any.3) | copy-start | bytes 1156
  2.4 44.4 %copy-start.5 = (s32[96]{0:T(128)S(1)}, s32[96]{0:T(128)}, u32[]{:S(2)}) copy-start(s32[96]{0:T(128)} %cols_any.3) | copy-start | bytes 1156
  42.1 21.7 %copy-start.6 = (bf16[64]{0:T(256)(128)(2,1)S(1)}, bf16[64]{0:T(256)(128)(2,1)}, u32[]{:S(2)}) copy-start(bf16[64]{0:T(256)(128)(2,1)} %param.16) | copy-start | bytes 388
  42.1 21.7 %copy-start.1 = (bf16[128,64]{0,1:T(8,128)(2,1)S(1)}, bf16[128,64]{0,1:T(8,128)(2,1)}, u32[]{:S(2)}) copy-start(bf16[128,64]{0,1:T(8,128)(2,1)} %param.15) | copy-start | bytes 49156
  42.1 21.7 %copy-start.3 = (bf16[128,64]{0,1:T(8,128)(2,1)S(1)}, bf16[128,64]{0,1:T(8,128)(2,1)}, u32[]{:S(2)}) copy-start(bf16[128,64]{0,1:T(8,128)(2,1)} %param.17) | copy-start | bytes 49156
  42.1 4.7 %collective-permute-start = (bf16[32,128,128]{2,1,0:T(8,128)(2,1)S(1)}, bf16[32,128,128]{2,1,0:T(8,128)(2,1)S(1)}, u32[]{:S(2)}, u32[]{:S(2)}) collective-permute-start(bf16[32,128,128]{2,1,0:T(8,128)(2,1)S(1)} %all_to_all.25.own_ref), channel_id=1, source_target_pairs={{0,8},{1,9},{2,10},{3,11},{4,12},{5,13},{6,14},{7,15},{8,0},{9,1},... | collective-permute-start | bytes 3145736 | tf_op jit(solution)/shard_map/ppermute | solution.py:75
  80.0 3.9 %collective-permute-start.1 = (bf16[4,9,64,128]{3,2,1,0:T(8,128)(2,1)S(1)}, bf16[4,9,64,128]{3,2,1,0:T(8,128)(2,1)S(1)}, u32[]{:S(2)}, u32[]{:S(2)}) collective-permute-start(bf16[4,9,64,128]{3,2,1,0:T(8,128)(2,1)S(1)} %get-tuple-element.14), channel_id=1, source_target_pairs={{0,8},{1,9},{2,10},{3,11},{4,12},{5,13},{6,14},{7,15},{8,0},{9,1},... | collective-permute-start | bytes 1769480 | tf_op jit(solution)/shard_map/ppermute | solution.py:75

commit v7 on v5

--- a/solution.py
+++ b/solution.py
@@ -33,26 +33,33 @@
     return lax.shift_left(low, 2) + jnp.bitwise_and(number, 2) + high
 
 
-def place_of(col, core):
+def place_of(col, core, last):
     owner = lax.shift_right_logical(col, 3)
     z = lax.shift_right_logical(owner, 3)
     x = jnp.bitwise_and(lax.shift_right_logical(owner, 1), 3)
     half = jnp.bitwise_and(owner, 1)
-    other = jnp.bitwise_xor(half, core)
-    return other * HALF + (N_X - 1 - x) * N_Z + turned(jnp.bitwise_xor(jnp.bitwise_xor(z, half), N_Z - 1))
+    x = jnp.bitwise_xor(x, half * (N_X - 1))
+    x = lax.shift_left(jnp.bitwise_and(x, 1), 1) + lax.shift_right_logical(x, 1)
+    z = N_Z - 1 - z if last else turned(jnp.bitwise_xor(jnp.bitwise_xor(z, half), N_Z - 1))
+    return jnp.bitwise_xor(half, core) * HALF + x * N_Z + z
 
 
 def place_in_group(row, core):
     return turned(jnp.bitwise_xor(jnp.bitwise_xor(jnp.bitwise_and(row, N_Y - 1), core), N_Y - 1))
 
 
-def exchange(blocks, axis):
+def exchange(blocks, axis, last=False):
     size = SIZES[axis]
     numbers = np.moveaxis(np.arange(np.prod(SIZES)).reshape(SIZES), axis, -1)
     cores = numbers[..., 0].reshape(-1) // N_Y % N_C
     groups = []
     for group, core in zip(numbers.reshape(-1, size), cores):
-        order = [k ^ 7 ^ int(core) for k in (0, 4, 2, 6, 1, 5, 3, 7)] if size == 8 else range(size)[::-1]
+        if last:
+            order = list(range(size))[::-1]
+        elif size == 8:
+            order = [k ^ 7 ^ int(core) for k in (0, 4, 2, 6, 1, 5, 3, 7)]
+        else:
+            order = [k ^ (3 * int(core)) for k in (0, 2, 1, 3)]
         groups.append([int(group[k]) for k in order])
     return lax.all_to_all(blocks, "d", 0, 0, axis_index_groups=groups)
 
@@ -90,7 +97,7 @@
         for g in range(0, CHUNK, GROUP):
             slots = [i * CHUNK + g + k for k in range(GROUP)]
             products = [
-                jnp.dot(values_ref[t], gathered[place_of(cols_ref[t], core)], preferred_element_type=f32)
+                jnp.dot(values_ref[t], gathered[place_of(cols_ref[t], core, False)], preferred_element_type=f32)
                 for t in slots
             ]
             for t, product in zip(slots, products):
@@ -148,7 +155,7 @@
                 for t in slots
             ]
             for t, product in zip(slots, products):
-                place = jnp.where(t < count, place_of(cols_ref[t], core), 2 * HALF)
+                place = jnp.where(t < count, place_of(cols_ref[t], core, True), 2 * HALF)
                 acc[place] += product
         return carry
 
@@ -274,7 +281,7 @@
         compiler_params=params,
         name="x_sum",
     )(by_x)
-    last = exchange(by_x, 0)
+    last = exchange(by_x, 0, last=True)
     grad_features, grad_weight_t = pl.pallas_call(
         final_kernel,
         out_shape=(

time: 110 us -> 110 us (level)
  no operation moved by 1% of the time
where the time goes in v7:
time: 110 us
  blocking collectives  92.5 us (84%)
  Pallas kernels  5.77 us (5%)
  starting transfers between devices  3.96 us (4%)
  waiting for transfers between devices  3.95 us (4%)
  between operations  1.36 us (1%)
  local copies, waits for them, and re-layouts  1.22 us (1%)
    all_to_all x6, blocking collectives, exchange(): return lax.all_to_all(blocks, 'd', 0, 0, axis_index_groups=groups)  92.5 us
    ppermute x2, starting transfers between devices, swap_cores(): lax.ppermute(blocks, 'd', [(i, i ^ N_Y) for i in range(np.prod(SIZES))])  3.96 us
    ppermute x2, waiting for transfers between devices, swap_cores(): lax.ppermute(blocks, 'd', [(i, i ^ N_Y) for i in range(np.prod(SIZES))])  3.95 us
    pallas_call x1, Pallas kernels, shards(): pl.pallas_call(forward_kernel, out_shape=jax.ShapeDtypeStruct((N_Y, BLOCK...  2.2 us
  transfers between devices with their start and end apart: 2, of which 2 were waited for; matrix products, arithmetic and copies ran while one was open for 0% of the time, Pallas kernels for 0%

profile of v7, /device:TPU:8, one launch (start us, length us, event | category | flops | bytes accessed | tf_op | source)
XLA Modules:
  0.0 109.6 jit_solution(16563092174197702380)
XLA Ops:
  0.6 0.0 copy-start
  0.6 0.8 rsqrt_bitcast_fusion.scales_ref
  1.5 0.0 copy-start.2
  1.5 0.9 copy-done.2
  2.4 0.0 copy-start.4
  2.4 0.0 copy-start.5
  2.4 0.1 start.1.scaled_ref
  2.5 19.4 %all_to_all.30 = bf16[8,128,128]{2,1,0:T(8,128)(2,1)S(1)} all-to-all(bf16[8,128,128]{2,1,0:T(8,128)(2,1)S(1)} %start.1.scaled_ref), channel_id=1, replica_groups={{448,192,320,64,384,128,256,0},{449,193,321,65,385,129,257,1},{450,194,..., dimensions={0} | all-to-all | bytes 524288 | tf_op jit(solution)/shard_map/all_to_all | solution.py:64
  21.8 0.2 broadcast_in_dim.4
  22.1 17.6 %all_to_all.31 = bf16[4,8,128,128]{3,2,1,0:T(8,128)(2,1)S(1)} all-to-all(bf16[4,8,128,128]{3,2,1,0:T(8,128)(2,1)S(1)} %broadcast_in_dim.4), channel_id=1, replica_groups={{0,32,16,48},{1,33,17,49},{2,34,18,50},{3,35,19,51},{4,36,20,52},{5,37,..., dimensions={0} | all-to-all | bytes 2097152 | tf_op jit(solution)/shard_map/all_to_all | solution.py:64
  39.7 0.0 copy-start.6
  39.7 2.0 %collective-permute-start = (bf16[32,128,128]{2,1,0:T(8,128)(2,1)S(1)}, bf16[32,128,128]{2,1,0:T(8,128)(2,1)S(1)}, u32[]{:S(2)}, u32[]{:S(2)}) collective-permute-start(bf16[32,128,128]{2,1,0:T(8,128)(2,1)S(1)} %bitcast.7), channel_id=1, source_target_pairs={{0,8},{1,9},{2,10},{3,11},{4,12},{5,13},{6,14},{7,15},{8,0},{9,1},... | collective-permute-start | bytes 3145736 | tf_op jit(solution)/shard_map/ppermute | solution.py:68
  42.4 2.0 %collective-permute-done.other_ref = bf16[32,128,128]{2,1,0:T(8,128)(2,1)S(1)} collective-permute-done((bf16[32,128,128]{2,1,0:T(8,128)(2,1)S(1)}, bf16[32,128,128]{2,1,0:T(8,128)(2,1)S(1)}, u32[]{:S(2)}, u32[]{:S(2)}) %collective-permute-start) | collective-permute-done | bytes 1048608 | tf_op jit(solution)/shard_map/ppermute | solution.py:68
  44.4 0.0 copy-done
  44.4 0.0 copy-done.4
  44.4 0.0 copy-done.5
  44.4 2.2 %forward.1 = bf16[8,128,128]{2,1,0:T(8,128)(2,1)S(1)} custom-call(s32[96]{0:T(128)S(1)} %copy-done.4, s32[96]{0:T(128)S(1)} %copy-done.5, s32[1]{0:T(128)S(6)} %copy.12.count_any, bf16[32,128,128]{2,1,0:T(8,128)(2,1)S(1)} %bitcast.8, bf16[32,128,128]{2,1,0:T(8,128)(2,1)S(1)} %collective-permute-done.other_ref, bf16[96,128,128]{2,1,0:T(8,128)(2,1)S(1)} %copy-done), custom_call_target="tpu_custom_call" | custom-call | tf_op jit(solution)/shard_map/forward/pallas_call | solution.py:223
  46.6 15.1 %all_to_all.32.parts_ref = bf16[8,128,128]{2,1,0:T(8,128)(2,1)S(1)} all-to-all(bf16[8,128,128]{2,1,0:T(8,128)(2,1)S(1)} %forward.1), channel_id=1, replica_groups={{7,3,5,1,6,2,4,0},{14,10,12,8,15,11,13,9},{23,19,21,17,22,18,20,16},{30..., dimensions={0} | all-to-all | bytes 524288 | tf_op jit(solution)/shard_map/all_to_all | solution.py:64
  61.7 0.0 copy-done.6
  61.7 0.1 broadcast_in_dim.5.bias_ref
  61.7 0.0 copy-done.1
  61.7 0.0 copy-done.3
  61.7 0.4 middle.1
  62.1 13.7 %all_to_all.33.group_ref = bf16[8,2,64,128]{3,2,1,0:T(8,128)(2,1)S(1)} all-to-all(bf16[8,2,64,128]{3,2,1,0:T(8,128)(2,1)S(1)} %get-tuple-element.10.sent_ref), channel_id=1, replica_groups={{7,3,5,1,6,2,4,0},{14,10,12,8,15,11,13,9},{23,19,21,17,22,18,20,16},{30..., dimensions={0} | all-to-all | bytes 524288 | tf_op jit(solution)/shard_map/all_to_all | solution.py:64
  75.8 2.0 %backward.1 = (bf16[4,9,64,128]{3,2,1,0:T(8,128)(2,1)S(1)}, bf16[4,9,64,128]{3,2,1,0:T(8,128)(2,1)S(1)}, bf16[64,128]{1,0:T(8,128)(2,1)}) custom-call(s32[96]{0:T(128)S(1)} %copy-done.4, s32[96]{0:T(128)S(1)} %copy-done.5, s32[1]{0:T(128)S(6)} %copy.12.count_any, bf16[8,2,64,128]{3,2,1,0:T(8,128)(2,1)S(1)} %all_to_all.33.group_ref, ...), custom_call_target="tpu_custom_call" | custom-call | tf_op jit(solution)/shard_map/backward/pallas_call | solution.py:253
  77.8 1.9 %collective-permute-start.1 = (bf16[4,9,64,128]{3,2,1,0:T(8,128)(2,1)S(1)}, bf16[4,9,64,128]{3,2,1,0:T(8,128)(2,1)S(1)}, u32[]{:S(2)}, u32[]{:S(2)}) collective-permute-start(bf16[4,9,64,128]{3,2,1,0:T(8,128)(2,1)S(1)} %get-tuple-element.14), channel_id=1, source_target_pairs={{0,8},{1,9},{2,10},{3,11},{4,12},{5,13},{6,14},{7,15},{8,0},{9,1},... | collective-permute-start | bytes 1769480 | tf_op jit(solution)/shard_map/ppermute | solution.py:68
  79.8 2.0 %collective-permute-done.1.recv_ref = bf16[4,9,64,128]{3,2,1,0:T(8,128)(2,1)S(1)} collective-permute-done((bf16[4,9,64,128]{3,2,1,0:T(8,128)(2,1)S(1)}, bf16[4,9,64,128]{3,2,1,0:T(8,128)(2,1)S(1)}, u32[]{:S(2)}, u32[]{:S(2)}) %collective-permute-start.1) | collective-permute-done | bytes 589856 | tf_op jit(solution)/shard_map/ppermute | solution.py:68
  81.7 0.1 core_sum.1
  81.9 13.0 %all_to_all.34.recv_ref = bf16[4,9,64,128]{3,2,1,0:T(8,128)(2,1)S(1)} all-to-all(bf16[4,9,64,128]{3,2,1,0:T(8,128)(2,1)S(1)} %core_sum.1), channel_id=1, replica_groups={{0,32,16,48},{1,33,17,49},{2,34,18,50},{3,35,19,51},{4,36,20,52},{5,37,..., dimensions={0} | all-to-all | bytes 1179648 | tf_op jit(solution)/shard_map/all_to_all | solution.py:64
  94.9 0.1 x_sum.1
  95.0 13.8 %all_to_all.35.recv_ref = bf16[8,2,64,128]{3,2,1,0:T(8,128)(2,1)S(1)} all-to-all(bf16[8,2,64,128]{3,2,1,0:T(8,128)(2,1)S(1)} %x_sum.1), channel_id=1, replica_groups={{448,384,320,256,192,128,64,0},{449,385,321,257,193,129,65,1},{450,386,..., dimensions={0} | all-to-all | bytes 524288 | tf_op jit(solution)/shard_map/all_to_all | solution.py:64
  108.8 0.8 final.1
  (2 shorter events, 0.0 us)
Async XLA Ops:
  0.6 43.8 %copy-start = (bf16[96,128,128]{2,1,0:T(8,128)(2,1)S(1)}, bf16[96,128,128]{2,1,0:T(8,128)(2,1)}, u32[]{:S(2)}) copy-start(bf16[96,128,128]{2,1,0:T(8,128)(2,1)} %values_ref.3) | copy-start | bytes 9437188
  1.5 0.9 copy-start.2
  2.4 42.0 %copy-start.4 = (s32[96]{0:T(128)S(1)}, s32[96]{0:T(128)}, u32[]{:S(2)}) copy-start(s32[96]{0:T(128)} %rows_any.3) | copy-start | bytes 1156
  2.4 42.0 %copy-start.5 = (s32[96]{0:T(128)S(1)}, s32[96]{0:T(128)}, u32[]{:S(2)}) copy-start(s32[96]{0:T(128)} %cols_any.3) | copy-start | bytes 1156
  39.7 22.0 %copy-start.6 = (bf16[64]{0:T(256)(128)(2,1)S(1)}, bf16[64]{0:T(256)(128)(2,1)}, u32[]{:S(2)}) copy-start(bf16[64]{0:T(256)(128)(2,1)} %param.16) | copy-start | bytes 388
  39.7 22.0 %copy-start.1 = (bf16[128,64]{0,1:T(8,128)(2,1)S(1)}, bf16[128,64]{0,1:T(8,128)(2,1)}, u32[]{:S(2)}) copy-start(bf16[128,64]{0,1:T(8,128)(2,1)} %param.15) | copy-start | bytes 49156
  39.7 22.0 %copy-start.3 = (bf16[128,64]{0,1:T(8,128)(2,1)S(1)}, bf16[128,64]{0,1:T(8,128)(2,1)}, u32[]{:S(2)}) copy-start(bf16[128,64]{0,1:T(8,128)(2,1)} %param.17) | copy-start | bytes 49156
  39.7 4.7 %collective-permute-start = (bf16[32,128,128]{2,1,0:T(8,128)(2,1)S(1)}, bf16[32,128,128]{2,1,0:T(8,128)(2,1)S(1)}, u32[]{:S(2)}, u32[]{:S(2)}) collective-permute-start(bf16[32,128,128]{2,1,0:T(8,128)(2,1)S(1)} %bitcast.7), channel_id=1, source_target_pairs={{0,8},{1,9},{2,10},{3,11},{4,12},{5,13},{6,14},{7,15},{8,0},{9,1},... | collective-permute-start | bytes 3145736 | tf_op jit(solution)/shard_map/ppermute | solution.py:68
  77.8 3.9 %collective-permute-start.1 = (bf16[4,9,64,128]{3,2,1,0:T(8,128)(2,1)S(1)}, bf16[4,9,64,128]{3,2,1,0:T(8,128)(2,1)S(1)}, u32[]{:S(2)}, u32[]{:S(2)}) collective-permute-start(bf16[4,9,64,128]{3,2,1,0:T(8,128)(2,1)S(1)} %get-tuple-element.14), channel_id=1, source_target_pairs={{0,8},{1,9},{2,10},{3,11},{4,12},{5,13},{6,14},{7,15},{8,0},{9,1},... | collective-permute-start | bytes 1769480 | tf_op jit(solution)/shard_map/ppermute | solution.py:68

commit v8 on v5

--- a/solution.py
+++ b/solution.py
@@ -36,10 +36,11 @@
 def place_of(col, core):
     owner = lax.shift_right_logical(col, 3)
     z = lax.shift_right_logical(owner, 3)
-    x = jnp.bitwise_and(lax.shift_right_logical(owner, 1), 3)
     half = jnp.bitwise_and(owner, 1)
-    other = jnp.bitwise_xor(half, core)
-    return other * HALF + (N_X - 1 - x) * N_Z + turned(jnp.bitwise_xor(jnp.bitwise_xor(z, half), N_Z - 1))
+    x = jnp.bitwise_xor(jnp.bitwise_and(lax.shift_right_logical(owner, 1), 3), 2 * half)
+    x = jnp.bitwise_xor(x, lax.shift_right_logical(x, 1))
+    z = turned(jnp.bitwise_xor(jnp.bitwise_xor(z, half), N_Z - 1))
+    return jnp.bitwise_xor(half, core) * HALF + x * N_Z + z
 
 
 def place_in_group(row, core):
@@ -52,7 +53,10 @@
     cores = numbers[..., 0].reshape(-1) // N_Y % N_C
     groups = []
     for group, core in zip(numbers.reshape(-1, size), cores):
-        order = [k ^ 7 ^ int(core) for k in (0, 4, 2, 6, 1, 5, 3, 7)] if size == 8 else range(size)[::-1]
+        if size == 8:
+            order = [k ^ 7 ^ int(core) for k in (0, 4, 2, 6, 1, 5, 3, 7)]
+        else:
+            order = [k ^ (2 * int(core)) for k in (0, 1, 3, 2)]
         groups.append([int(group[k]) for k in order])
     return lax.all_to_all(blocks, "d", 0, 0, axis_index_groups=groups)
 

time: 110 us -> 110 us (level)
  the two profiles are of different devices: /device:TPU:8 before, /device:TPU:2 now
where the time goes in v8:
time: 110 us; the launch traced here: 109 us
  blocking collectives  92.3 us (84%)
  Pallas kernels  5.79 us (5%)
  starting transfers between devices  4.06 us (4%)
  waiting for transfers between devices  3.84 us (3%)
  between operations  1.36 us (1%)
  local copies, waits for them, and re-layouts  1.22 us (1%)
    all_to_all x6, blocking collectives, exchange(): return lax.all_to_all(blocks, 'd', 0, 0, axis_index_groups=groups)  92.3 us
    ppermute x2, starting transfers between devices, swap_cores(): lax.ppermute(blocks, 'd', [(i, i ^ N_Y) for i in range(np.prod(SIZES))])  4.06 us
    ppermute x2, waiting for transfers between devices, swap_cores(): lax.ppermute(blocks, 'd', [(i, i ^ N_Y) for i in range(np.prod(SIZES))])  3.84 us
  transfers between devices with their start and end apart: 2, of which 2 were waited for; matrix products, arithmetic and copies ran while one was open for 0% of the time, Pallas kernels for 0%

profile of v8, /device:TPU:2, one launch (start us, length us, event | category | flops | bytes accessed | tf_op | source)
XLA Modules:
  0.0 109.4 jit_solution(5998114654894075974)
XLA Ops:
  0.6 0.0 copy-start
  0.6 0.8 rsqrt_bitcast_fusion.scales_ref
  1.5 0.9 copy-done.2
  2.4 0.0 copy-start.5
  2.4 0.1 start.1.scaled_ref
  2.5 19.4 %all_to_all.30 = bf16[8,128,128]{2,1,0:T(8,128)(2,1)S(1)} all-to-all(bf16[8,128,128]{2,1,0:T(8,128)(2,1)S(1)} %start.1.scaled_ref), channel_id=1, replica_groups={{448,192,320,64,384,128,256,0},{449,193,321,65,385,129,257,1},{450,194,..., dimensions={0} | all-to-all | bytes 524288 | tf_op jit(solution)/shard_map/all_to_all | solution.py:61
  21.8 0.2 broadcast_in_dim.4
  22.1 16.9 %all_to_all.31 = bf16[4,8,128,128]{3,2,1,0:T(8,128)(2,1)S(1)} all-to-all(bf16[4,8,128,128]{3,2,1,0:T(8,128)(2,1)S(1)} %broadcast_in_dim.4), channel_id=1, replica_groups={{0,16,48,32},{1,17,49,33},{2,18,50,34},{3,19,51,35},{4,20,52,36},{5,21,..., dimensions={0} | all-to-all | bytes 2097152 | tf_op jit(solution)/shard_map/all_to_all | solution.py:61
  39.0 0.0 copy-start.6
  39.0 0.0 copy-start.1
  39.0 0.0 copy-start.3
  39.0 2.1 %collective-permute-start = (bf16[32,128,128]{2,1,0:T(8,128)(2,1)S(1)}, bf16[32,128,128]{2,1,0:T(8,128)(2,1)S(1)}, u32[]{:S(2)}, u32[]{:S(2)}) collective-permute-start(bf16[32,128,128]{2,1,0:T(8,128)(2,1)S(1)} %bitcast.7), channel_id=1, source_target_pairs={{0,8},{1,9},{2,10},{3,11},{4,12},{5,13},{6,14},{7,15},{8,0},{9,1},... | collective-permute-start | bytes 3145736 | tf_op jit(solution)/shard_map/ppermute | solution.py:65
  41.8 1.9 %collective-permute-done.other_ref = bf16[32,128,128]{2,1,0:T(8,128)(2,1)S(1)} collective-permute-done((bf16[32,128,128]{2,1,0:T(8,128)(2,1)S(1)}, bf16[32,128,128]{2,1,0:T(8,128)(2,1)S(1)}, u32[]{:S(2)}, u32[]{:S(2)}) %collective-permute-start) | collective-permute-done | bytes 1048608 | tf_op jit(solution)/shard_map/ppermute | solution.py:65
  43.7 0.0 copy-done
  43.7 0.0 copy-done.4
  43.7 0.0 copy-done.5
  43.7 2.1 %forward.1 = bf16[8,128,128]{2,1,0:T(8,128)(2,1)S(1)} custom-call(s32[96]{0:T(128)S(1)} %copy-done.4, s32[96]{0:T(128)S(1)} %copy-done.5, s32[1]{0:T(128)S(6)} %copy.12.count_any, bf16[32,128,128]{2,1,0:T(8,128)(2,1)S(1)} %bitcast.8, bf16[32,128,128]{2,1,0:T(8,128)(2,1)S(1)} %collective-permute-done.other_ref, bf16[96,128,128]{2,1,0:T(8,128)(2,1)S(1)} %copy-done), custom_call_target="tpu_custom_call" | custom-call | tf_op jit(solution)/shard_map/forward/pallas_call | solution.py:220
  45.8 15.4 %all_to_all.32.parts_ref = bf16[8,128,128]{2,1,0:T(8,128)(2,1)S(1)} all-to-all(bf16[8,128,128]{2,1,0:T(8,128)(2,1)S(1)} %forward.1), channel_id=1, replica_groups={{7,3,5,1,6,2,4,0},{14,10,12,8,15,11,13,9},{23,19,21,17,22,18,20,16},{30..., dimensions={0} | all-to-all | bytes 524288 | tf_op jit(solution)/shard_map/all_to_all | solution.py:61
  61.3 0.0 copy-done.6
  61.3 0.1 broadcast_in_dim.5.bias_ref
  61.3 0.0 copy-done.1
  61.3 0.0 copy-done.3
  61.4 0.4 middle.1
  61.7 13.7 %all_to_all.33.group_ref = bf16[8,2,64,128]{3,2,1,0:T(8,128)(2,1)S(1)} all-to-all(bf16[8,2,64,128]{3,2,1,0:T(8,128)(2,1)S(1)} %get-tuple-element.10.sent_ref), channel_id=1, replica_groups={{7,3,5,1,6,2,4,0},{14,10,12,8,15,11,13,9},{23,19,21,17,22,18,20,16},{30..., dimensions={0} | all-to-all | bytes 524288 | tf_op jit(solution)/shard_map/all_to_all | solution.py:61
  75.4 2.1 %backward.1 = (bf16[4,9,64,128]{3,2,1,0:T(8,128)(2,1)S(1)}, bf16[4,9,64,128]{3,2,1,0:T(8,128)(2,1)S(1)}, bf16[64,128]{1,0:T(8,128)(2,1)}) custom-call(s32[96]{0:T(128)S(1)} %copy-done.4, s32[96]{0:T(128)S(1)} %copy-done.5, s32[1]{0:T(128)S(6)} %copy.12.count_any, bf16[8,2,64,128]{3,2,1,0:T(8,128)(2,1)S(1)} %all_to_all.33.group_ref, ...), custom_call_target="tpu_custom_call" | custom-call | tf_op jit(solution)/shard_map/backward/pallas_call | solution.py:250
  77.5 1.9 %collective-permute-start.1 = (bf16[4,9,64,128]{3,2,1,0:T(8,128)(2,1)S(1)}, bf16[4,9,64,128]{3,2,1,0:T(8,128)(2,1)S(1)}, u32[]{:S(2)}, u32[]{:S(2)}) collective-permute-start(bf16[4,9,64,128]{3,2,1,0:T(8,128)(2,1)S(1)} %get-tuple-element.14), channel_id=1, source_target_pairs={{0,8},{1,9},{2,10},{3,11},{4,12},{5,13},{6,14},{7,15},{8,0},{9,1},... | collective-permute-start | bytes 1769480 | tf_op jit(solution)/shard_map/ppermute | solution.py:65
  79.5 2.0 %collective-permute-done.1.recv_ref = bf16[4,9,64,128]{3,2,1,0:T(8,128)(2,1)S(1)} collective-permute-done((bf16[4,9,64,128]{3,2,1,0:T(8,128)(2,1)S(1)}, bf16[4,9,64,128]{3,2,1,0:T(8,128)(2,1)S(1)}, u32[]{:S(2)}, u32[]{:S(2)}) %collective-permute-start.1) | collective-permute-done | bytes 589856 | tf_op jit(solution)/shard_map/ppermute | solution.py:65
  81.4 0.1 core_sum.1
  81.6 12.9 %all_to_all.34.recv_ref = bf16[4,9,64,128]{3,2,1,0:T(8,128)(2,1)S(1)} all-to-all(bf16[4,9,64,128]{3,2,1,0:T(8,128)(2,1)S(1)} %core_sum.1), channel_id=1, replica_groups={{0,16,48,32},{1,17,49,33},{2,18,50,34},{3,19,51,35},{4,20,52,36},{5,21,..., dimensions={0} | all-to-all | bytes 1179648 | tf_op jit(solution)/shard_map/all_to_all | solution.py:61
  94.5 0.1 x_sum.1
  94.6 13.9 %all_to_all.35.recv_ref = bf16[8,2,64,128]{3,2,1,0:T(8,128)(2,1)S(1)} all-to-all(bf16[8,2,64,128]{3,2,1,0:T(8,128)(2,1)S(1)} %x_sum.1), channel_id=1, replica_groups={{448,192,320,64,384,128,256,0},{449,193,321,65,385,129,257,1},{450,194,..., dimensions={0} | all-to-all | bytes 524288 | tf_op jit(solution)/shard_map/all_to_all | solution.py:61
  108.5 0.8 final.1
  (2 shorter events, 0.0 us)
Async XLA Ops:
  0.6 43.0 %copy-start = (bf16[96,128,128]{2,1,0:T(8,128)(2,1)S(1)}, bf16[96,128,128]{2,1,0:T(8,128)(2,1)}, u32[]{:S(2)}) copy-start(bf16[96,128,128]{2,1,0:T(8,128)(2,1)} %values_ref.3) | copy-start | bytes 9437188
  1.5 0.9 copy-start.2
  2.4 41.3 %copy-start.4 = (s32[96]{0:T(128)S(1)}, s32[96]{0:T(128)}, u32[]{:S(2)}) copy-start(s32[96]{0:T(128)} %rows_any.3) | copy-start | bytes 1156
  2.4 41.3 %copy-start.5 = (s32[96]{0:T(128)S(1)}, s32[96]{0:T(128)}, u32[]{:S(2)}) copy-start(s32[96]{0:T(128)} %cols_any.3) | copy-start | bytes 1156
  39.0 22.3 %copy-start.6 = (bf16[64]{0:T(256)(128)(2,1)S(1)}, bf16[64]{0:T(256)(128)(2,1)}, u32[]{:S(2)}) copy-start(bf16[64]{0:T(256)(128)(2,1)} %param.16) | copy-start | bytes 388
  39.0 22.4 %copy-start.1 = (bf16[128,64]{0,1:T(8,128)(2,1)S(1)}, bf16[128,64]{0,1:T(8,128)(2,1)}, u32[]{:S(2)}) copy-start(bf16[128,64]{0,1:T(8,128)(2,1)} %param.15) | copy-start | bytes 49156
  39.0 22.4 %copy-start.3 = (bf16[128,64]{0,1:T(8,128)(2,1)S(1)}, bf16[128,64]{0,1:T(8,128)(2,1)}, u32[]{:S(2)}) copy-start(bf16[128,64]{0,1:T(8,128)(2,1)} %param.17) | copy-start | bytes 49156
  39.0 4.7 %collective-permute-start = (bf16[32,128,128]{2,1,0:T(8,128)(2,1)S(1)}, bf16[32,128,128]{2,1,0:T(8,128)(2,1)S(1)}, u32[]{:S(2)}, u32[]{:S(2)}) collective-permute-start(bf16[32,128,128]{2,1,0:T(8,128)(2,1)S(1)} %bitcast.7), channel_id=1, source_target_pairs={{0,8},{1,9},{2,10},{3,11},{4,12},{5,13},{6,14},{7,15},{8,0},{9,1},... | collective-permute-start | bytes 3145736 | tf_op jit(solution)/shard_map/ppermute | solution.py:65
  77.5 3.9 %collective-permute-start.1 = (bf16[4,9,64,128]{3,2,1,0:T(8,128)(2,1)S(1)}, bf16[4,9,64,128]{3,2,1,0:T(8,128)(2,1)S(1)}, u32[]{:S(2)}, u32[]{:S(2)}) collective-permute-start(bf16[4,9,64,128]{3,2,1,0:T(8,128)(2,1)S(1)} %get-tuple-element.14), channel_id=1, source_target_pairs={{0,8},{1,9},{2,10},{3,11},{4,12},{5,13},{6,14},{7,15},{8,0},{9,1},... | collective-permute-start | bytes 1769480 | tf_op jit(solution)/shard_map/ppermute | solution.py:65

commit v9 on v8

--- a/solution.py
+++ b/solution.py
@@ -37,8 +37,8 @@
     owner = lax.shift_right_logical(col, 3)
     z = lax.shift_right_logical(owner, 3)
     half = jnp.bitwise_and(owner, 1)
-    x = jnp.bitwise_xor(jnp.bitwise_and(lax.shift_right_logical(owner, 1), 3), 2 * half)
-    x = jnp.bitwise_xor(x, lax.shift_right_logical(x, 1))
+    x = jnp.bitwise_xor(jnp.bitwise_and(lax.shift_right_logical(owner, 1), 3), 3 * half)
+    x = lax.shift_left(jnp.bitwise_and(x, 1), 1) + lax.shift_right_logical(x, 1)
     z = turned(jnp.bitwise_xor(jnp.bitwise_xor(z, half), N_Z - 1))
     return jnp.bitwise_xor(half, core) * HALF + x * N_Z + z
 
@@ -56,7 +56,7 @@
         if size == 8:
             order = [k ^ 7 ^ int(core) for k in (0, 4, 2, 6, 1, 5, 3, 7)]
         else:
-            order = [k ^ (2 * int(core)) for k in (0, 1, 3, 2)]
+            order = [k ^ (3 * int(core)) for k in (0, 2, 1, 3)]
         groups.append([int(group[k]) for k in order])
     return lax.all_to_all(blocks, "d", 0, 0, axis_index_groups=groups)
 

time: 110 us -> 110 us (level)
  no operation moved by 1% of the time
where the time goes in v9:
time: 110 us
  blocking collectives  92.8 us (84%)
  Pallas kernels  5.88 us (5%)
  starting transfers between devices  3.96 us (4%)
  waiting for transfers between devices  3.95 us (4%)
  between operations  1.36 us (1%)
  local copies, waits for them, and re-layouts  1.22 us (1%)
    all_to_all x6, blocking collectives, exchange(): return lax.all_to_all(blocks, 'd', 0, 0, axis_index_groups=groups)  92.8 us
    ppermute x2, starting transfers between devices, swap_cores(): lax.ppermute(blocks, 'd', [(i, i ^ N_Y) for i in range(np.prod(SIZES))])  3.96 us
    ppermute x2, waiting for transfers between devices, swap_cores(): lax.ppermute(blocks, 'd', [(i, i ^ N_Y) for i in range(np.prod(SIZES))])  3.95 us
  transfers between devices with their start and end apart: 2, of which 2 were waited for; matrix products, arithmetic and copies ran while one was open for 0% of the time, Pallas kernels for 0%

profile of v9, /device:TPU:2, one launch (start us, length us, event | category | flops | bytes accessed | tf_op | source)
XLA Modules:
  0.0 110.0 jit_solution(13886764149026581308)
XLA Ops:
  0.6 0.0 copy-start
  0.6 0.8 rsqrt_bitcast_fusion.scales_ref
  1.5 0.9 copy-done.2
  2.4 0.0 copy-start.5
  2.4 0.1 start.1.scaled_ref
  2.5 19.4 %all_to_all.30 = bf16[8,128,128]{2,1,0:T(8,128)(2,1)S(1)} all-to-all(bf16[8,128,128]{2,1,0:T(8,128)(2,1)S(1)} %start.1.scaled_ref), channel_id=1, replica_groups={{448,192,320,64,384,128,256,0},{449,193,321,65,385,129,257,1},{450,194,..., dimensions={0} | all-to-all | bytes 524288 | tf_op jit(solution)/shard_map/all_to_all | solution.py:61
  21.8 0.2 broadcast_in_dim.4
  22.1 17.1 %all_to_all.31 = bf16[4,8,128,128]{3,2,1,0:T(8,128)(2,1)S(1)} all-to-all(bf16[4,8,128,128]{3,2,1,0:T(8,128)(2,1)S(1)} %broadcast_in_dim.4), channel_id=1, replica_groups={{0,32,16,48},{1,33,17,49},{2,34,18,50},{3,35,19,51},{4,36,20,52},{5,37,..., dimensions={0} | all-to-all | bytes 2097152 | tf_op jit(solution)/shard_map/all_to_all | solution.py:61
  39.1 0.0 copy-start.6
  39.1 0.0 copy-start.1
  39.1 0.0 copy-start.3
  39.1 2.0 %collective-permute-start = (bf16[32,128,128]{2,1,0:T(8,128)(2,1)S(1)}, bf16[32,128,128]{2,1,0:T(8,128)(2,1)S(1)}, u32[]{:S(2)}, u32[]{:S(2)}) collective-permute-start(bf16[32,128,128]{2,1,0:T(8,128)(2,1)S(1)} %bitcast.7), channel_id=1, source_target_pairs={{0,8},{1,9},{2,10},{3,11},{4,12},{5,13},{6,14},{7,15},{8,0},{9,1},... | collective-permute-start | bytes 3145736 | tf_op jit(solution)/shard_map/ppermute | solution.py:65
  41.8 2.0 %collective-permute-done.other_ref = bf16[32,128,128]{2,1,0:T(8,128)(2,1)S(1)} collective-permute-done((bf16[32,128,128]{2,1,0:T(8,128)(2,1)S(1)}, bf16[32,128,128]{2,1,0:T(8,128)(2,1)S(1)}, u32[]{:S(2)}, u32[]{:S(2)}) %collective-permute-start) | collective-permute-done | bytes 1048608 | tf_op jit(solution)/shard_map/ppermute | solution.py:65
  43.8 0.0 copy-done
  43.8 0.0 copy-done.4
  43.8 0.0 copy-done.5
  43.8 2.2 %forward.1 = bf16[8,128,128]{2,1,0:T(8,128)(2,1)S(1)} custom-call(s32[96]{0:T(128)S(1)} %copy-done.4, s32[96]{0:T(128)S(1)} %copy-done.5, s32[1]{0:T(128)S(6)} %copy.12.count_any, bf16[32,128,128]{2,1,0:T(8,128)(2,1)S(1)} %bitcast.8, bf16[32,128,128]{2,1,0:T(8,128)(2,1)S(1)} %collective-permute-done.other_ref, bf16[96,128,128]{2,1,0:T(8,128)(2,1)S(1)} %copy-done), custom_call_target="tpu_custom_call" | custom-call | tf_op jit(solution)/shard_map/forward/pallas_call | solution.py:220
  46.0 15.4 %all_to_all.32.parts_ref = bf16[8,128,128]{2,1,0:T(8,128)(2,1)S(1)} all-to-all(bf16[8,128,128]{2,1,0:T(8,128)(2,1)S(1)} %forward.1), channel_id=1, replica_groups={{7,3,5,1,6,2,4,0},{14,10,12,8,15,11,13,9},{23,19,21,17,22,18,20,16},{30..., dimensions={0} | all-to-all | bytes 524288 | tf_op jit(solution)/shard_map/all_to_all | solution.py:61
  61.5 0.0 copy-done.6
  61.5 0.1 broadcast_in_dim.5.bias_ref
  61.5 0.0 copy-done.1
  61.5 0.0 copy-done.3
  61.5 0.4 middle.1
  61.9 13.7 %all_to_all.33.group_ref = bf16[8,2,64,128]{3,2,1,0:T(8,128)(2,1)S(1)} all-to-all(bf16[8,2,64,128]{3,2,1,0:T(8,128)(2,1)S(1)} %get-tuple-element.10.sent_ref), channel_id=1, replica_groups={{7,3,5,1,6,2,4,0},{14,10,12,8,15,11,13,9},{23,19,21,17,22,18,20,16},{30..., dimensions={0} | all-to-all | bytes 524288 | tf_op jit(solution)/shard_map/all_to_all | solution.py:61
  75.6 2.2 %backward.1 = (bf16[4,9,64,128]{3,2,1,0:T(8,128)(2,1)S(1)}, bf16[4,9,64,128]{3,2,1,0:T(8,128)(2,1)S(1)}, bf16[64,128]{1,0:T(8,128)(2,1)}) custom-call(s32[96]{0:T(128)S(1)} %copy-done.4, s32[96]{0:T(128)S(1)} %copy-done.5, s32[1]{0:T(128)S(6)} %copy.12.count_any, bf16[8,2,64,128]{3,2,1,0:T(8,128)(2,1)S(1)} %all_to_all.33.group_ref, ...), custom_call_target="tpu_custom_call" | custom-call | tf_op jit(solution)/shard_map/backward/pallas_call | solution.py:250
  77.8 1.9 %collective-permute-start.1 = (bf16[4,9,64,128]{3,2,1,0:T(8,128)(2,1)S(1)}, bf16[4,9,64,128]{3,2,1,0:T(8,128)(2,1)S(1)}, u32[]{:S(2)}, u32[]{:S(2)}) collective-permute-start(bf16[4,9,64,128]{3,2,1,0:T(8,128)(2,1)S(1)} %get-tuple-element.14), channel_id=1, source_target_pairs={{0,8},{1,9},{2,10},{3,11},{4,12},{5,13},{6,14},{7,15},{8,0},{9,1},... | collective-permute-start | bytes 1769480 | tf_op jit(solution)/shard_map/ppermute | solution.py:65
  79.7 2.0 %collective-permute-done.1.recv_ref = bf16[4,9,64,128]{3,2,1,0:T(8,128)(2,1)S(1)} collective-permute-done((bf16[4,9,64,128]{3,2,1,0:T(8,128)(2,1)S(1)}, bf16[4,9,64,128]{3,2,1,0:T(8,128)(2,1)S(1)}, u32[]{:S(2)}, u32[]{:S(2)}) %collective-permute-start.1) | collective-permute-done | bytes 589856 | tf_op jit(solution)/shard_map/ppermute | solution.py:65
  81.7 0.1 core_sum.1
  81.8 12.0 %all_to_all.34.recv_ref = bf16[4,9,64,128]{3,2,1,0:T(8,128)(2,1)S(1)} all-to-all(bf16[4,9,64,128]{3,2,1,0:T(8,128)(2,1)S(1)} %core_sum.1), channel_id=1, replica_groups={{0,32,16,48},{1,33,17,49},{2,34,18,50},{3,35,19,51},{4,36,20,52},{5,37,..., dimensions={0} | all-to-all | bytes 1179648 | tf_op jit(solution)/shard_map/all_to_all | solution.py:61
  93.8 0.1 x_sum.1
  93.9 15.2 %all_to_all.35.recv_ref = bf16[8,2,64,128]{3,2,1,0:T(8,128)(2,1)S(1)} all-to-all(bf16[8,2,64,128]{3,2,1,0:T(8,128)(2,1)S(1)} %x_sum.1), channel_id=1, replica_groups={{448,192,320,64,384,128,256,0},{449,193,321,65,385,129,257,1},{450,194,..., dimensions={0} | all-to-all | bytes 524288 | tf_op jit(solution)/shard_map/all_to_all | solution.py:61
  109.1 0.8 final.1
  (2 shorter events, 0.0 us)
Async XLA Ops:
  0.6 43.2 %copy-start = (bf16[96,128,128]{2,1,0:T(8,128)(2,1)S(1)}, bf16[96,128,128]{2,1,0:T(8,128)(2,1)}, u32[]{:S(2)}) copy-start(bf16[96,128,128]{2,1,0:T(8,128)(2,1)} %values_ref.3) | copy-start | bytes 9437188
  1.5 0.9 copy-start.2
  2.4 41.5 %copy-start.4 = (s32[96]{0:T(128)S(1)}, s32[96]{0:T(128)}, u32[]{:S(2)}) copy-start(s32[96]{0:T(128)} %rows_any.3) | copy-start | bytes 1156
  2.4 41.5 %copy-start.5 = (s32[96]{0:T(128)S(1)}, s32[96]{0:T(128)}, u32[]{:S(2)}) copy-start(s32[96]{0:T(128)} %cols_any.3) | copy-start | bytes 1156
  39.1 22.3 %copy-start.6 = (bf16[64]{0:T(256)(128)(2,1)S(1)}, bf16[64]{0:T(256)(128)(2,1)}, u32[]{:S(2)}) copy-start(bf16[64]{0:T(256)(128)(2,1)} %param.16) | copy-start | bytes 388
  39.1 22.4 %copy-start.1 = (bf16[128,64]{0,1:T(8,128)(2,1)S(1)}, bf16[128,64]{0,1:T(8,128)(2,1)}, u32[]{:S(2)}) copy-start(bf16[128,64]{0,1:T(8,128)(2,1)} %param.15) | copy-start | bytes 49156
  39.1 22.4 %copy-start.3 = (bf16[128,64]{0,1:T(8,128)(2,1)S(1)}, bf16[128,64]{0,1:T(8,128)(2,1)}, u32[]{:S(2)}) copy-start(bf16[128,64]{0,1:T(8,128)(2,1)} %param.17) | copy-start | bytes 49156
  39.1 4.7 %collective-permute-start = (bf16[32,128,128]{2,1,0:T(8,128)(2,1)S(1)}, bf16[32,128,128]{2,1,0:T(8,128)(2,1)S(1)}, u32[]{:S(2)}, u32[]{:S(2)}) collective-permute-start(bf16[32,128,128]{2,1,0:T(8,128)(2,1)S(1)} %bitcast.7), channel_id=1, source_target_pairs={{0,8},{1,9},{2,10},{3,11},{4,12},{5,13},{6,14},{7,15},{8,0},{9,1},... | collective-permute-start | bytes 3145736 | tf_op jit(solution)/shard_map/ppermute | solution.py:65
  77.8 3.9 %collective-permute-start.1 = (bf16[4,9,64,128]{3,2,1,0:T(8,128)(2,1)S(1)}, bf16[4,9,64,128]{3,2,1,0:T(8,128)(2,1)S(1)}, u32[]{:S(2)}, u32[]{:S(2)}) collective-permute-start(bf16[4,9,64,128]{3,2,1,0:T(8,128)(2,1)S(1)} %get-tuple-element.14), channel_id=1, source_target_pairs={{0,8},{1,9},{2,10},{3,11},{4,12},{5,13},{6,14},{7,15},{8,0},{9,1},... | collective-permute-start | bytes 1769480 | tf_op jit(solution)/shard_map/ppermute | solution.py:65

commit v10 on v8

--- a/solution.py
+++ b/solution.py
@@ -65,41 +65,63 @@
     return lax.ppermute(blocks, "d", [(i, i ^ N_Y) for i in range(np.prod(SIZES))])
 
 
+def list_places(rows_ref, cols_ref, count_ref, core, lists_ref):
+    slots = rows_ref.shape[0]
+    count = count_ref[0]
+
+    def slot(t, carry):
+        live = t < count
+        place = place_of(cols_ref[t], core)
+        row = place_in_group(rows_ref[t], core)
+        lists_ref[t] = place
+        lists_ref[slots + t] = row
+        lists_ref[2 * slots + t] = jnp.where(live, row, N_Y)
+        lists_ref[3 * slots + t] = jnp.where(live, place, 2 * HALF)
+        return carry
+
+    lax.fori_loop(0, slots, slot, 0)
+
+
 def start_kernel(scales_ref, features_ref, scaled_ref):
     scaled = (scale_square(scales_ref) * features_ref[...].astype(f32)).astype(bf16)
     scaled_ref[...] = jnp.broadcast_to(scaled[None], scaled_ref.shape)
 
 
+def lists_kernel(rows_any, cols_any, count_any, after_any, lists_ref, rows_ref, cols_ref, count_ref, sems):
+    del after_any
+    copies = slot_copies(rows_any, cols_any, count_any, rows_ref, cols_ref, count_ref, sems)
+    for copy in copies:
+        copy.start()
+    for copy in copies:
+        copy.wait()
+    list_places(rows_ref, cols_ref, count_ref, own_core(), lists_ref)
+
+
 def slot_copies(rows_ref, cols_ref, count_ref, rows, cols, count, sems):
     pairs = ((rows_ref, rows), (cols_ref, cols), (count_ref, count))
     return [pltpu.make_async_copy(src, dst, sems.at[i]) for i, (src, dst) in enumerate(pairs)]
 
 
 def forward_kernel(
-    rows_any, cols_any, count_any, own_ref, other_ref, values_ref, out_ref,
-    rows_ref, cols_ref, count_ref, gathered, acc, sems,
+    lists_any, own_ref, other_ref, values_ref, out_ref, lists_ref, gathered, acc, sems
 ):
-    copies = slot_copies(rows_any, cols_any, count_any, rows_ref, cols_ref, count_ref, sems)
-    for copy in copies:
-        copy.start()
-    core = own_core()
+    lists_copy = pltpu.make_async_copy(lists_any, lists_ref, sems.at[0])
+    lists_copy.start()
+    total = values_ref.shape[0]
     gathered[0:HALF] = own_ref[...]
     gathered[HALF : 2 * HALF] = other_ref[...]
     acc[...] = jnp.zeros_like(acc)
-    for copy in copies:
-        copy.wait()
-    count = count_ref[0]
+    lists_copy.wait()
 
     def chunk(i, carry):
         for g in range(0, CHUNK, GROUP):
             slots = [i * CHUNK + g + k for k in range(GROUP)]
             products = [
-                jnp.dot(values_ref[t], gathered[place_of(cols_ref[t], core)], preferred_element_type=f32)
+                jnp.dot(values_ref[t], gathered[lists_ref[t]], preferred_element_type=f32)
                 for t in slots
             ]
             for t, product in zip(slots, products):
-                row = jnp.where(t < count, place_in_group(rows_ref[t], core), N_Y)
-                acc[row] += product
+                acc[lists_ref[2 * total + t]] += product
         return carry
 
     lax.fori_loop(0, values_ref.shape[0] // CHUNK, chunk, 0)
@@ -126,34 +148,29 @@
 
 
 def backward_kernel(
-    rows_any, cols_any, count_any, group_ref, values_ref, mixed_ref, keep_ref, send_ref, mixed_any,
-    rows_ref, cols_ref, count_ref, acc, sems,
+    lists_any, group_ref, values_ref, mixed_ref, keep_ref, send_ref, mixed_any, lists_ref, acc, sems
 ):
-    copies = slot_copies(rows_any, cols_any, count_any, rows_ref, cols_ref, count_ref, sems)
-    mixed_copy = pltpu.make_async_copy(mixed_ref, mixed_any, sems.at[3])
-    for copy in copies:
-        copy.start()
+    lists_copy = pltpu.make_async_copy(lists_any, lists_ref, sems.at[0])
+    mixed_copy = pltpu.make_async_copy(mixed_ref, mixed_any, sems.at[1])
+    lists_copy.start()
     mixed_copy.start()
-    core = own_core()
+    total = values_ref.shape[0]
     acc[...] = jnp.zeros_like(acc)
-    for copy in copies:
-        copy.wait()
-    count = count_ref[0]
+    lists_copy.wait()
 
     def chunk(i, carry):
         for g in range(0, CHUNK, GROUP):
             slots = [i * CHUNK + g + k for k in range(GROUP)]
             products = [
                 jnp.dot(
-                    group_ref[place_in_group(rows_ref[t], core), 0],
+                    group_ref[lists_ref[total + t], 0],
                     values_ref[t],
                     preferred_element_type=f32,
                 )
                 for t in slots
             ]
             for t, product in zip(slots, products):
-                place = jnp.where(t < count, place_of(cols_ref[t], core), 2 * HALF)
-                acc[place] += product
+                acc[lists_ref[3 * total + t]] += product
         return carry
 
     lax.fori_loop(0, values_ref.shape[0] // CHUNK, chunk, 0)
@@ -201,7 +218,7 @@
     weight_t = weight.T
     cotangent_t = cotangent.T
     bias = jnp.broadcast_to(out_bias.astype(f32)[:, None], (F_OUT, BLOCK))
-    lists = [pltpu.SMEM((slots,), jnp.int32), pltpu.SMEM((slots,), jnp.int32), pltpu.SMEM((1,), jnp.int32)]
+    slot_lists = [pltpu.SMEM((slots,), jnp.int32), pltpu.SMEM((slots,), jnp.int32), pltpu.SMEM((1,), jnp.int32)]
     params = pltpu.CompilerParams(vmem_limit_bytes=VMEM_BYTES)
 
     scaled = pl.pallas_call(
@@ -216,21 +233,30 @@
     by_xz = exchange(jnp.broadcast_to(by_z[None], (N_X,) + by_z.shape), 1)
     own = by_xz.reshape(HALF, BLOCK, F_IN)
     other = swap_cores(own)
+    lists = pl.pallas_call(
+        lists_kernel,
+        out_shape=jax.ShapeDtypeStruct((4 * slots,), jnp.int32),
+        in_specs=[anywhere()] * 4,
+        out_specs=pl.BlockSpec(memory_space=pltpu.SMEM),
+        scratch_shapes=[*slot_lists, pltpu.SemaphoreType.DMA((3,))],
+        compiler_params=params,
+        name="lists",
+    )(tile_row, tile_col, tile_count, own)
 
     parts = pl.pallas_call(
         forward_kernel,
         out_shape=jax.ShapeDtypeStruct((N_Y, BLOCK, F_IN), bf16),
-        in_specs=[anywhere()] * 3 + [vmem()] * 3,
+        in_specs=[anywhere()] + [vmem()] * 3,
         out_specs=vmem(),
         scratch_shapes=[
-            *lists,
+            pltpu.SMEM((4 * slots,), jnp.int32),
             pltpu.VMEM((2 * HALF, BLOCK, F_IN), bf16),
             pltpu.VMEM((N_Y + 1, BLOCK, F_IN), f32),
-            pltpu.SemaphoreType.DMA((3,)),
+            pltpu.SemaphoreType.DMA((1,)),
         ],
         compiler_params=params,
         name="forward",
-    )(tile_row, tile_col, tile_count, own, other, tile_values)
+    )(lists, own, other, tile_values)
     parts = exchange(parts, 3)
 
     mixed_here, send = pl.pallas_call(
@@ -250,16 +276,16 @@
     keep, away, mixed_t = pl.pallas_call(
         backward_kernel,
         out_shape=(half, half, jax.ShapeDtypeStruct((F_OUT, BLOCK), bf16)),
-        in_specs=[anywhere()] * 3 + [vmem()] * 3,
+        in_specs=[anywhere()] + [vmem()] * 3,
         out_specs=(vmem(), vmem(), anywhere()),
         scratch_shapes=[
-            *lists,
+            pltpu.SMEM((4 * slots,), jnp.int32),
             pltpu.VMEM((2 * HALF + 1, F_OUT, BLOCK), f32),
-            pltpu.SemaphoreType.DMA((4,)),
+            pltpu.SemaphoreType.DMA((2,)),
         ],
         compiler_params=params,
         name="backward",
-    )(tile_row, tile_col, tile_count, group, tile_values, mixed_here)
+    )(lists, group, tile_values, mixed_here)
     recv = swap_cores(away)
     by_core = pl.pallas_call(
         core_sum_kernel,

time: 110 us -> 110 us (level)
  Pallas kernels: 5.79 us -> 8.11 us
  waiting for transfers between devices: 3.84 us -> 1.97 us
    pallas_call x0 -> x1, Pallas kernels: none -> 2.82 us  [shards(): pl.pallas_call(lists_kernel, out_shape=jax.ShapeDtypeStruct((4 * slots,),...]
    ppermute x2, waiting for transfers between devices: 3.84 us -> 1.97 us  [swap_cores(): lax.ppermute(blocks, 'd', [(i, i ^ N_Y) for i in range(np.prod(SIZES))])]
  transfers between devices with their start and end apart: 2 -> 2, of which waited for: 2 -> 1; matrix products, arithmetic and copies ran while one was open for 0% -> 0% of each run, Pallas kernels for 0% -> 3%
where the time goes in v10:
time: 110 us
  blocking collectives  92.5 us (84%)
  Pallas kernels  8.11 us (7%)
  starting transfers between devices  3.93 us (4%)
  waiting for transfers between devices  1.97 us (2%)
  between operations  1.42 us (1%)
  local copies, waits for them, and re-layouts  1.23 us (1%)
    all_to_all x6, blocking collectives, exchange(): return lax.all_to_all(blocks, 'd', 0, 0, axis_index_groups=groups)  92.5 us
    ppermute x2, starting transfers between devices, swap_cores(): lax.ppermute(blocks, 'd', [(i, i ^ N_Y) for i in range(np.prod(SIZES))])  3.93 us
    pallas_call x1, Pallas kernels, shards(): pl.pallas_call(lists_kernel, out_shape=jax.ShapeDtypeStruct((4 * slots,),...  2.82 us
  transfers between devices with their start and end apart: 2, of which 1 were waited for; matrix products, arithmetic and copies ran while one was open for 0% of the time, Pallas kernels for 3%

profile of v10, /device:TPU:2, one launch (start us, length us, event | category | flops | bytes accessed | tf_op | source)
XLA Modules:
  0.0 110.0 jit_solution(11862202726177448872)
XLA Ops:
  0.6 0.0 copy-start
  0.6 0.8 rsqrt_bitcast_fusion.scales_ref
  1.5 0.9 copy-done.2
  2.4 0.1 start.1.scaled_ref
  2.5 19.4 %all_to_all.30 = bf16[8,128,128]{2,1,0:T(8,128)(2,1)S(1)} all-to-all(bf16[8,128,128]{2,1,0:T(8,128)(2,1)S(1)} %start.1.scaled_ref), channel_id=1, replica_groups={{448,192,320,64,384,128,256,0},{449,193,321,65,385,129,257,1},{450,194,..., dimensions={0} | all-to-all | bytes 524288 | tf_op jit(solution)/shard_map/all_to_all | solution.py:61
  21.8 0.2 broadcast_in_dim.4
  22.1 16.9 %all_to_all.31 = bf16[4,8,128,128]{3,2,1,0:T(8,128)(2,1)S(1)} all-to-all(bf16[4,8,128,128]{3,2,1,0:T(8,128)(2,1)S(1)} %broadcast_in_dim.4), channel_id=1, replica_groups={{0,16,48,32},{1,17,49,33},{2,18,50,34},{3,19,51,35},{4,20,52,36},{5,21,..., dimensions={0} | all-to-all | bytes 2097152 | tf_op jit(solution)/shard_map/all_to_all | solution.py:61
  39.0 2.0 %collective-permute-start = (bf16[32,128,128]{2,1,0:T(8,128)(2,1)S(1)}, bf16[32,128,128]{2,1,0:T(8,128)(2,1)S(1)}, u32[]{:S(2)}, u32[]{:S(2)}) collective-permute-start(bf16[32,128,128]{2,1,0:T(8,128)(2,1)S(1)} %bitcast.7), channel_id=1, source_target_pairs={{0,8},{1,9},{2,10},{3,11},{4,12},{5,13},{6,14},{7,15},{8,0},{9,1},... | collective-permute-start | bytes 3145736 | tf_op jit(solution)/shard_map/ppermute | solution.py:65
  41.6 0.0 copy-done.4
  41.7 0.0 copy-done.5
  41.7 2.8 %lists.1.lists_any = s32[384]{0:T(512)S(1)} custom-call(s32[96]{0:T(128)S(1)} %copy-done.4, s32[96]{0:T(128)S(1)} %copy-done.5, s32[1]{0:T(128)S(6)} %copy.12.count_any, bf16[32,128,128]{2,1,0:T(8,128)(2,1)S(1)} %bitcast.8), custom_call_target="tpu_custom_call" | custom-call | tf_op jit(solution)/shard_map/lists/pallas_call | solution.py:236
  44.5 0.0 copy-start.6
  44.5 0.0 copy-start.1
  44.5 0.0 copy-start.3
  44.5 0.0 collective-permute-done.other_ref
  44.5 0.0 copy-done
  44.6 1.9 %forward.1 = bf16[8,128,128]{2,1,0:T(8,128)(2,1)S(1)} custom-call(s32[384]{0:T(512)S(1)} %lists.1.lists_any, bf16[32,128,128]{2,1,0:T(8,128)(2,1)S(1)} %bitcast.9, bf16[32,128,128]{2,1,0:T(8,128)(2,1)S(1)} %collective-permute-done.other_ref, bf16[96,128,128]{2,1,0:T(8,128)(2,1)S(1)} %copy-done), custom_call_target="tpu_custom_call" | custom-call | tf_op jit(solution)/shard_map/forward/pallas_call | solution.py:246
  46.5 16.4 %all_to_all.32.parts_ref = bf16[8,128,128]{2,1,0:T(8,128)(2,1)S(1)} all-to-all(bf16[8,128,128]{2,1,0:T(8,128)(2,1)S(1)} %forward.1), channel_id=1, replica_groups={{7,3,5,1,6,2,4,0},{14,10,12,8,15,11,13,9},{23,19,21,17,22,18,20,16},{30..., dimensions={0} | all-to-all | bytes 524288 | tf_op jit(solution)/shard_map/all_to_all | solution.py:61
  62.9 0.0 copy-done.6
  62.9 0.1 broadcast_in_dim.5.bias_ref
  63.0 0.0 copy-done.1
  63.0 0.0 copy-done.3
  63.0 0.4 middle.1
  63.3 12.9 %all_to_all.33.group_ref = bf16[8,2,64,128]{3,2,1,0:T(8,128)(2,1)S(1)} all-to-all(bf16[8,2,64,128]{3,2,1,0:T(8,128)(2,1)S(1)} %get-tuple-element.10.sent_ref), channel_id=1, replica_groups={{7,3,5,1,6,2,4,0},{14,10,12,8,15,11,13,9},{23,19,21,17,22,18,20,16},{30..., dimensions={0} | all-to-all | bytes 524288 | tf_op jit(solution)/shard_map/all_to_all | solution.py:61
  76.3 1.8 %backward.1 = (bf16[4,9,64,128]{3,2,1,0:T(8,128)(2,1)S(1)}, bf16[4,9,64,128]{3,2,1,0:T(8,128)(2,1)S(1)}, bf16[64,128]{1,0:T(8,128)(2,1)}) custom-call(s32[384]{0:T(512)S(1)} %lists.1.lists_any, bf16[8,2,64,128]{3,2,1,0:T(8,128)(2,1)S(1)} %all_to_all.33.group_ref, bf16[96,128,128]{2,1,0:T(8,128)(2,1)S(1)} %copy-done, ...), custom_call_target="tpu_custom_call" | custom-call | tf_op jit(solution)/shard_map/backward/pallas_call | solution.py:276
  78.1 1.9 %collective-permute-start.1 = (bf16[4,9,64,128]{3,2,1,0:T(8,128)(2,1)S(1)}, bf16[4,9,64,128]{3,2,1,0:T(8,128)(2,1)S(1)}, u32[]{:S(2)}, u32[]{:S(2)}) collective-permute-start(bf16[4,9,64,128]{3,2,1,0:T(8,128)(2,1)S(1)} %get-tuple-element.14), channel_id=1, source_target_pairs={{0,8},{1,9},{2,10},{3,11},{4,12},{5,13},{6,14},{7,15},{8,0},{9,1},... | collective-permute-start | bytes 1769480 | tf_op jit(solution)/shard_map/ppermute | solution.py:65
  80.0 2.0 %collective-permute-done.1.recv_ref = bf16[4,9,64,128]{3,2,1,0:T(8,128)(2,1)S(1)} collective-permute-done((bf16[4,9,64,128]{3,2,1,0:T(8,128)(2,1)S(1)}, bf16[4,9,64,128]{3,2,1,0:T(8,128)(2,1)S(1)}, u32[]{:S(2)}, u32[]{:S(2)}) %collective-permute-start.1) | collective-permute-done | bytes 589856 | tf_op jit(solution)/shard_map/ppermute | solution.py:65
  82.0 0.1 core_sum.1
  82.2 13.0 %all_to_all.34.recv_ref = bf16[4,9,64,128]{3,2,1,0:T(8,128)(2,1)S(1)} all-to-all(bf16[4,9,64,128]{3,2,1,0:T(8,128)(2,1)S(1)} %core_sum.1), channel_id=1, replica_groups={{0,16,48,32},{1,17,49,33},{2,18,50,34},{3,19,51,35},{4,20,52,36},{5,21,..., dimensions={0} | all-to-all | bytes 1179648 | tf_op jit(solution)/shard_map/all_to_all | solution.py:61
  95.1 0.1 x_sum.1
  95.2 13.9 %all_to_all.35.recv_ref = bf16[8,2,64,128]{3,2,1,0:T(8,128)(2,1)S(1)} all-to-all(bf16[8,2,64,128]{3,2,1,0:T(8,128)(2,1)S(1)} %x_sum.1), channel_id=1, replica_groups={{448,192,320,64,384,128,256,0},{449,193,321,65,385,129,257,1},{450,194,..., dimensions={0} | all-to-all | bytes 524288 | tf_op jit(solution)/shard_map/all_to_all | solution.py:61
  109.1 0.8 final.1
  (3 shorter events, 0.0 us)
Async XLA Ops:
  0.6 43.9 %copy-start = (bf16[96,128,128]{2,1,0:T(8,128)(2,1)S(1)}, bf16[96,128,128]{2,1,0:T(8,128)(2,1)}, u32[]{:S(2)}) copy-start(bf16[96,128,128]{2,1,0:T(8,128)(2,1)} %values_ref.3) | copy-start | bytes 9437188
  1.5 0.9 copy-start.2
  2.4 39.3 %copy-start.4 = (s32[96]{0:T(128)S(1)}, s32[96]{0:T(128)}, u32[]{:S(2)}) copy-start(s32[96]{0:T(128)} %rows_any.1) | copy-start | bytes 1156
  2.4 39.3 %copy-start.5 = (s32[96]{0:T(128)S(1)}, s32[96]{0:T(128)}, u32[]{:S(2)}) copy-start(s32[96]{0:T(128)} %cols_any.1) | copy-start | bytes 1156
  39.0 5.6 %collective-permute-start = (bf16[32,128,128]{2,1,0:T(8,128)(2,1)S(1)}, bf16[32,128,128]{2,1,0:T(8,128)(2,1)S(1)}, u32[]{:S(2)}, u32[]{:S(2)}) collective-permute-start(bf16[32,128,128]{2,1,0:T(8,128)(2,1)S(1)} %bitcast.7), channel_id=1, source_target_pairs={{0,8},{1,9},{2,10},{3,11},{4,12},{5,13},{6,14},{7,15},{8,0},{9,1},... | collective-permute-start | bytes 3145736 | tf_op jit(solution)/shard_map/ppermute | solution.py:65
  44.5 18.4 %copy-start.6 = (bf16[64]{0:T(256)(128)(2,1)S(1)}, bf16[64]{0:T(256)(128)(2,1)}, u32[]{:S(2)}) copy-start(bf16[64]{0:T(256)(128)(2,1)} %param.16) | copy-start | bytes 388
  44.5 18.5 %copy-start.1 = (bf16[128,64]{0,1:T(8,128)(2,1)S(1)}, bf16[128,64]{0,1:T(8,128)(2,1)}, u32[]{:S(2)}) copy-start(bf16[128,64]{0,1:T(8,128)(2,1)} %param.15) | copy-start | bytes 49156
  44.5 18.5 %copy-start.3 = (bf16[128,64]{0,1:T(8,128)(2,1)S(1)}, bf16[128,64]{0,1:T(8,128)(2,1)}, u32[]{:S(2)}) copy-start(bf16[128,64]{0,1:T(8,128)(2,1)} %param.17) | copy-start | bytes 49156
  78.1 3.9 %collective-permute-start.1 = (bf16[4,9,64,128]{3,2,1,0:T(8,128)(2,1)S(1)}, bf16[4,9,64,128]{3,2,1,0:T(8,128)(2,1)S(1)}, u32[]{:S(2)}, u32[]{:S(2)}) collective-permute-start(bf16[4,9,64,128]{3,2,1,0:T(8,128)(2,1)S(1)} %get-tuple-element.14), channel_id=1, source_target_pairs={{0,8},{1,9},{2,10},{3,11},{4,12},{5,13},{6,14},{7,15},{8,0},{9,1},... | collective-permute-start | bytes 1769480 | tf_op jit(solution)/shard_map/ppermute | solution.py:65

commit v11 on v10

--- a/solution.py
+++ b/solution.py
@@ -65,41 +65,21 @@
     return lax.ppermute(blocks, "d", [(i, i ^ N_Y) for i in range(np.prod(SIZES))])
 
 
-def list_places(rows_ref, cols_ref, count_ref, core, lists_ref):
-    slots = rows_ref.shape[0]
-    count = count_ref[0]
-
-    def slot(t, carry):
-        live = t < count
-        place = place_of(cols_ref[t], core)
-        row = place_in_group(rows_ref[t], core)
-        lists_ref[t] = place
-        lists_ref[slots + t] = row
-        lists_ref[2 * slots + t] = jnp.where(live, row, N_Y)
-        lists_ref[3 * slots + t] = jnp.where(live, place, 2 * HALF)
-        return carry
-
-    lax.fori_loop(0, slots, slot, 0)
-
-
 def start_kernel(scales_ref, features_ref, scaled_ref):
     scaled = (scale_square(scales_ref) * features_ref[...].astype(f32)).astype(bf16)
     scaled_ref[...] = jnp.broadcast_to(scaled[None], scaled_ref.shape)
 
 
-def lists_kernel(rows_any, cols_any, count_any, after_any, lists_ref, rows_ref, cols_ref, count_ref, sems):
+def lists_kernel(rows_ref, cols_ref, count_ref, after_any, lists_ref):
     del after_any
-    copies = slot_copies(rows_any, cols_any, count_any, rows_ref, cols_ref, count_ref, sems)
-    for copy in copies:
-        copy.start()
-    for copy in copies:
-        copy.wait()
-    list_places(rows_ref, cols_ref, count_ref, own_core(), lists_ref)
-
-
-def slot_copies(rows_ref, cols_ref, count_ref, rows, cols, count, sems):
-    pairs = ((rows_ref, rows), (cols_ref, cols), (count_ref, count))
-    return [pltpu.make_async_copy(src, dst, sems.at[i]) for i, (src, dst) in enumerate(pairs)]
+    core = own_core()
+    place = place_of(cols_ref[...], core)
+    row = place_in_group(rows_ref[...], core)
+    live = lax.broadcasted_iota(jnp.int32, row.shape, 1) < count_ref[0]
+    lists_ref[0:1] = place
+    lists_ref[1:2] = row
+    lists_ref[2:3] = jnp.where(live, row, N_Y)
+    lists_ref[3:4] = jnp.where(live, place, 2 * HALF)
 
 
 def forward_kernel(
@@ -107,7 +87,6 @@
 ):
     lists_copy = pltpu.make_async_copy(lists_any, lists_ref, sems.at[0])
     lists_copy.start()
-    total = values_ref.shape[0]
     gathered[0:HALF] = own_ref[...]
     gathered[HALF : 2 * HALF] = other_ref[...]
     acc[...] = jnp.zeros_like(acc)
@@ -117,11 +96,11 @@
         for g in range(0, CHUNK, GROUP):
             slots = [i * CHUNK + g + k for k in range(GROUP)]
             products = [
-                jnp.dot(values_ref[t], gathered[lists_ref[t]], preferred_element_type=f32)
+                jnp.dot(values_ref[t], gathered[lists_ref[0, t]], preferred_element_type=f32)
                 for t in slots
             ]
             for t, product in zip(slots, products):
-                acc[lists_ref[2 * total + t]] += product
+                acc[lists_ref[2, t]] += product
         return carry
 
     lax.fori_loop(0, values_ref.shape[0] // CHUNK, chunk, 0)
@@ -154,7 +133,6 @@
     mixed_copy = pltpu.make_async_copy(mixed_ref, mixed_any, sems.at[1])
     lists_copy.start()
     mixed_copy.start()
-    total = values_ref.shape[0]
     acc[...] = jnp.zeros_like(acc)
     lists_copy.wait()
 
@@ -163,14 +141,14 @@
             slots = [i * CHUNK + g + k for k in range(GROUP)]
             products = [
                 jnp.dot(
-                    group_ref[lists_ref[total + t], 0],
+                    group_ref[lists_ref[1, t], 0],
                     values_ref[t],
                     preferred_element_type=f32,
                 )
                 for t in slots
             ]
             for t, product in zip(slots, products):
-                acc[lists_ref[3 * total + t]] += product
+                acc[lists_ref[3, t]] += product
         return carry
 
     lax.fori_loop(0, values_ref.shape[0] // CHUNK, chunk, 0)
@@ -218,7 +196,6 @@
     weight_t = weight.T
     cotangent_t = cotangent.T
     bias = jnp.broadcast_to(out_bias.astype(f32)[:, None], (F_OUT, BLOCK))
-    slot_lists = [pltpu.SMEM((slots,), jnp.int32), pltpu.SMEM((slots,), jnp.int32), pltpu.SMEM((1,), jnp.int32)]
     params = pltpu.CompilerParams(vmem_limit_bytes=VMEM_BYTES)
 
     scaled = pl.pallas_call(
@@ -235,13 +212,12 @@
     other = swap_cores(own)
     lists = pl.pallas_call(
         lists_kernel,
-        out_shape=jax.ShapeDtypeStruct((4 * slots,), jnp.int32),
-        in_specs=[anywhere()] * 4,
-        out_specs=pl.BlockSpec(memory_space=pltpu.SMEM),
-        scratch_shapes=[*slot_lists, pltpu.SemaphoreType.DMA((3,))],
+        out_shape=jax.ShapeDtypeStruct((4, slots), jnp.int32),
+        in_specs=[vmem(), vmem(), pl.BlockSpec(memory_space=pltpu.SMEM), anywhere()],
+        out_specs=vmem(),
         compiler_params=params,
         name="lists",
-    )(tile_row, tile_col, tile_count, own)
+    )(tile_row.reshape(1, slots), tile_col.reshape(1, slots), tile_count, own)
 
     parts = pl.pallas_call(
         forward_kernel,
@@ -249,7 +225,7 @@
         in_specs=[anywhere()] + [vmem()] * 3,
         out_specs=vmem(),
         scratch_shapes=[
-            pltpu.SMEM((4 * slots,), jnp.int32),
+            pltpu.SMEM((4, slots), jnp.int32),
             pltpu.VMEM((2 * HALF, BLOCK, F_IN), bf16),
             pltpu.VMEM((N_Y + 1, BLOCK, F_IN), f32),
             pltpu.SemaphoreType.DMA((1,)),
@@ -279,7 +255,7 @@
         in_specs=[anywhere()] + [vmem()] * 3,
         out_specs=(vmem(), vmem(), anywhere()),
         scratch_shapes=[
-            pltpu.SMEM((4 * slots,), jnp.int32),
+            pltpu.SMEM((4, slots), jnp.int32),
             pltpu.VMEM((2 * HALF + 1, F_OUT, BLOCK), f32),
             pltpu.SemaphoreType.DMA((2,)),
         ],

time: 110 us -> 109 us (level)
  Pallas kernels: 8.11 us -> 5.35 us
  waiting for transfers between devices: 1.97 us -> 3.77 us
    pallas_call x1, Pallas kernels: 2.82 us -> 0.02 us  [shards(): pl.pallas_call(lists_kernel, out_shape=jax.ShapeDtypeStruct((4, slots), j...]
    ppermute x2, waiting for transfers between devices: 1.97 us -> 3.77 us  [swap_cores(): lax.ppermute(blocks, 'd', [(i, i ^ N_Y) for i in range(np.prod(SIZES))])]
  transfers between devices with their start and end apart: 2 -> 2, of which waited for: 1 -> 2; matrix products, arithmetic and copies ran while one was open for 0% -> 0% of each run, Pallas kernels for 3% -> 0%
where the time goes in v11:
time: 109 us
  blocking collectives  92.3 us (85%)
  Pallas kernels  5.35 us (5%)
  starting transfers between devices  3.93 us (4%)
  waiting for transfers between devices  3.77 us (3%)
  between operations  1.4 us (1%)
  local copies, waits for them, and re-layouts  1.23 us (1%)
    all_to_all x6, blocking collectives, exchange(): return lax.all_to_all(blocks, 'd', 0, 0, axis_index_groups=groups)  92.3 us
    ppermute x2, starting transfers between devices, swap_cores(): lax.ppermute(blocks, 'd', [(i, i ^ N_Y) for i in range(np.prod(SIZES))])  3.93 us
    ppermute x2, waiting for transfers between devices, swap_cores(): lax.ppermute(blocks, 'd', [(i, i ^ N_Y) for i in range(np.prod(SIZES))])  3.77 us
  transfers between devices with their start and end apart: 2, of which 2 were waited for; matrix products, arithmetic and copies ran while one was open for 0% of the time, Pallas kernels for 0%

profile of v11, /device:TPU:2, one launch (start us, length us, event | category | flops | bytes accessed | tf_op | source)
XLA Modules:
  0.0 108.8 jit_solution(15916967436003181672)
XLA Ops:
  0.6 0.0 copy-start
  0.6 0.8 rsqrt_bitcast_fusion.scales_ref
  1.5 0.0 copy-start.2
  1.5 0.9 copy-done.2
  2.4 0.1 start.1.scaled_ref
  2.5 19.4 %all_to_all.30 = bf16[8,128,128]{2,1,0:T(8,128)(2,1)S(1)} all-to-all(bf16[8,128,128]{2,1,0:T(8,128)(2,1)S(1)} %start.1.scaled_ref), channel_id=1, replica_groups={{448,192,320,64,384,128,256,0},{449,193,321,65,385,129,257,1},{450,194,..., dimensions={0} | all-to-all | bytes 524288 | tf_op jit(solution)/shard_map/all_to_all | solution.py:61
  21.8 0.2 broadcast_in_dim.4
  22.1 16.9 %all_to_all.31 = bf16[4,8,128,128]{3,2,1,0:T(8,128)(2,1)S(1)} all-to-all(bf16[4,8,128,128]{3,2,1,0:T(8,128)(2,1)S(1)} %broadcast_in_dim.4), channel_id=1, replica_groups={{0,16,48,32},{1,17,49,33},{2,18,50,34},{3,19,51,35},{4,20,52,36},{5,21,..., dimensions={0} | all-to-all | bytes 2097152 | tf_op jit(solution)/shard_map/all_to_all | solution.py:61
  39.0 2.0 %collective-permute-start = (bf16[32,128,128]{2,1,0:T(8,128)(2,1)S(1)}, bf16[32,128,128]{2,1,0:T(8,128)(2,1)S(1)}, u32[]{:S(2)}, u32[]{:S(2)}) collective-permute-start(bf16[32,128,128]{2,1,0:T(8,128)(2,1)S(1)} %bitcast.9), channel_id=1, source_target_pairs={{0,8},{1,9},{2,10},{3,11},{4,12},{5,13},{6,14},{7,15},{8,0},{9,1},... | collective-permute-start | bytes 3145736 | tf_op jit(solution)/shard_map/ppermute | solution.py:65
  41.6 0.0 copy-done.4
  41.7 0.0 copy-done.5
  41.7 0.0 copy-start.6
  41.7 0.0 copy-start.1
  41.7 0.0 copy-start.3
  41.7 1.8 %collective-permute-done.other_ref = bf16[32,128,128]{2,1,0:T(8,128)(2,1)S(1)} collective-permute-done((bf16[32,128,128]{2,1,0:T(8,128)(2,1)S(1)}, bf16[32,128,128]{2,1,0:T(8,128)(2,1)S(1)}, u32[]{:S(2)}, u32[]{:S(2)}) %collective-permute-start) | collective-permute-done | bytes 1048608 | tf_op jit(solution)/shard_map/ppermute | solution.py:65
  43.5 0.0 copy-done
  43.5 2.0 %forward.1 = bf16[8,128,128]{2,1,0:T(8,128)(2,1)S(1)} custom-call(s32[4,96]{1,0:T(4,128)S(1)} %lists.1.lists_any, bf16[32,128,128]{2,1,0:T(8,128)(2,1)S(1)} %bitcast.11, bf16[32,128,128]{2,1,0:T(8,128)(2,1)S(1)} %collective-permute-done.other_ref, bf16[96,128,128]{2,1,0:T(8,128)(2,1)S(1)} %copy-done), custom_call_target="tpu_custom_call" | custom-call | tf_op jit(solution)/shard_map/forward/pallas_call | solution.py:222
  45.5 15.4 %all_to_all.32.parts_ref = bf16[8,128,128]{2,1,0:T(8,128)(2,1)S(1)} all-to-all(bf16[8,128,128]{2,1,0:T(8,128)(2,1)S(1)} %forward.1), channel_id=1, replica_groups={{7,3,5,1,6,2,4,0},{14,10,12,8,15,11,13,9},{23,19,21,17,22,18,20,16},{30..., dimensions={0} | all-to-all | bytes 524288 | tf_op jit(solution)/shard_map/all_to_all | solution.py:61
  60.9 0.0 copy-done.6
  60.9 0.1 broadcast_in_dim.5.bias_ref
  61.0 0.0 copy-done.1
  61.0 0.0 copy-done.3
  61.0 0.4 middle.1
  61.4 13.7 %all_to_all.33.group_ref = bf16[8,2,64,128]{3,2,1,0:T(8,128)(2,1)S(1)} all-to-all(bf16[8,2,64,128]{3,2,1,0:T(8,128)(2,1)S(1)} %get-tuple-element.10.sent_ref), channel_id=1, replica_groups={{7,3,5,1,6,2,4,0},{14,10,12,8,15,11,13,9},{23,19,21,17,22,18,20,16},{30..., dimensions={0} | all-to-all | bytes 524288 | tf_op jit(solution)/shard_map/all_to_all | solution.py:61
  75.1 1.9 %backward.1 = (bf16[4,9,64,128]{3,2,1,0:T(8,128)(2,1)S(1)}, bf16[4,9,64,128]{3,2,1,0:T(8,128)(2,1)S(1)}, bf16[64,128]{1,0:T(8,128)(2,1)}) custom-call(s32[4,96]{1,0:T(4,128)S(1)} %lists.1.lists_any, bf16[8,2,64,128]{3,2,1,0:T(8,128)(2,1)S(1)} %all_to_all.33.group_ref, bf16[96,128,128]{2,1,0:T(8,128)(2,1)S(1)} %copy-done, ...), custom_call_target="tpu_custom_call" | custom-call | tf_op jit(solution)/shard_map/backward/pallas_call | solution.py:252
  76.9 1.9 %collective-permute-start.1 = (bf16[4,9,64,128]{3,2,1,0:T(8,128)(2,1)S(1)}, bf16[4,9,64,128]{3,2,1,0:T(8,128)(2,1)S(1)}, u32[]{:S(2)}, u32[]{:S(2)}) collective-permute-start(bf16[4,9,64,128]{3,2,1,0:T(8,128)(2,1)S(1)} %get-tuple-element.14), channel_id=1, source_target_pairs={{0,8},{1,9},{2,10},{3,11},{4,12},{5,13},{6,14},{7,15},{8,0},{9,1},... | collective-permute-start | bytes 1769480 | tf_op jit(solution)/shard_map/ppermute | solution.py:65
  78.9 2.0 %collective-permute-done.1.recv_ref = bf16[4,9,64,128]{3,2,1,0:T(8,128)(2,1)S(1)} collective-permute-done((bf16[4,9,64,128]{3,2,1,0:T(8,128)(2,1)S(1)}, bf16[4,9,64,128]{3,2,1,0:T(8,128)(2,1)S(1)}, u32[]{:S(2)}, u32[]{:S(2)}) %collective-permute-start.1) | collective-permute-done | bytes 589856 | tf_op jit(solution)/shard_map/ppermute | solution.py:65
  80.8 0.1 core_sum.1
  81.0 12.9 %all_to_all.34.recv_ref = bf16[4,9,64,128]{3,2,1,0:T(8,128)(2,1)S(1)} all-to-all(bf16[4,9,64,128]{3,2,1,0:T(8,128)(2,1)S(1)} %core_sum.1), channel_id=1, replica_groups={{0,16,48,32},{1,17,49,33},{2,18,50,34},{3,19,51,35},{4,20,52,36},{5,21,..., dimensions={0} | all-to-all | bytes 1179648 | tf_op jit(solution)/shard_map/all_to_all | solution.py:61
  93.9 0.1 x_sum.1
  94.0 14.0 %all_to_all.35.recv_ref = bf16[8,2,64,128]{3,2,1,0:T(8,128)(2,1)S(1)} all-to-all(bf16[8,2,64,128]{3,2,1,0:T(8,128)(2,1)S(1)} %x_sum.1), channel_id=1, replica_groups={{448,192,320,64,384,128,256,0},{449,193,321,65,385,129,257,1},{450,194,..., dimensions={0} | all-to-all | bytes 524288 | tf_op jit(solution)/shard_map/all_to_all | solution.py:61
  108.0 0.8 final.1
  (3 shorter events, 0.0 us)
Async XLA Ops:
  0.6 42.9 %copy-start = (bf16[96,128,128]{2,1,0:T(8,128)(2,1)S(1)}, bf16[96,128,128]{2,1,0:T(8,128)(2,1)}, u32[]{:S(2)}) copy-start(bf16[96,128,128]{2,1,0:T(8,128)(2,1)} %values_ref.3) | copy-start | bytes 9437188
  1.5 0.9 copy-start.2
  2.4 39.3 %copy-start.4 = (s32[96]{0:T(128)S(1)}, s32[96]{0:T(128)}, u32[]{:S(2)}) copy-start(s32[96]{0:T(128)} %param.12) | copy-start | bytes 1156
  2.4 39.3 %copy-start.5 = (s32[96]{0:T(128)S(1)}, s32[96]{0:T(128)}, u32[]{:S(2)}) copy-start(s32[96]{0:T(128)} %param.13) | copy-start | bytes 1156
  39.0 4.5 %collective-permute-start = (bf16[32,128,128]{2,1,0:T(8,128)(2,1)S(1)}, bf16[32,128,128]{2,1,0:T(8,128)(2,1)S(1)}, u32[]{:S(2)}, u32[]{:S(2)}) collective-permute-start(bf16[32,128,128]{2,1,0:T(8,128)(2,1)S(1)} %bitcast.9), channel_id=1, source_target_pairs={{0,8},{1,9},{2,10},{3,11},{4,12},{5,13},{6,14},{7,15},{8,0},{9,1},... | collective-permute-start | bytes 3145736 | tf_op jit(solution)/shard_map/ppermute | solution.py:65
  41.7 19.2 %copy-start.6 = (bf16[64]{0:T(256)(128)(2,1)S(1)}, bf16[64]{0:T(256)(128)(2,1)}, u32[]{:S(2)}) copy-start(bf16[64]{0:T(256)(128)(2,1)} %param.16) | copy-start | bytes 388
  41.7 19.3 %copy-start.1 = (bf16[128,64]{0,1:T(8,128)(2,1)S(1)}, bf16[128,64]{0,1:T(8,128)(2,1)}, u32[]{:S(2)}) copy-start(bf16[128,64]{0,1:T(8,128)(2,1)} %param.15) | copy-start | bytes 49156
  41.7 19.3 %copy-start.3 = (bf16[128,64]{0,1:T(8,128)(2,1)S(1)}, bf16[128,64]{0,1:T(8,128)(2,1)}, u32[]{:S(2)}) copy-start(bf16[128,64]{0,1:T(8,128)(2,1)} %param.17) | copy-start | bytes 49156
  76.9 3.9 %collective-permute-start.1 = (bf16[4,9,64,128]{3,2,1,0:T(8,128)(2,1)S(1)}, bf16[4,9,64,128]{3,2,1,0:T(8,128)(2,1)S(1)}, u32[]{:S(2)}, u32[]{:S(2)}) collective-permute-start(bf16[4,9,64,128]{3,2,1,0:T(8,128)(2,1)S(1)} %get-tuple-element.14), channel_id=1, source_target_pairs={{0,8},{1,9},{2,10},{3,11},{4,12},{5,13},{6,14},{7,15},{8,0},{9,1},... | collective-permute-start | bytes 1769480 | tf_op jit(solution)/shard_map/ppermute | solution.py:65

commit v12 on v11

--- a/solution.py
+++ b/solution.py
@@ -12,7 +12,7 @@
 BLOCK = 128
 F_IN = 128
 F_OUT = 64
-CHUNK = 48
+CHUNK = 96
 GROUP = 8
 HALF = N_X * N_Z
 VMEM_BYTES = 16 * 1024 * 1024

time: 109 us -> 109 us (level)
  no operation moved by 1% of the time
where the time goes in v12:
time: 109 us
  blocking collectives  92.3 us (85%)
  Pallas kernels  5.15 us (5%)
  starting transfers between devices  3.93 us (4%)
  waiting for transfers between devices  3.77 us (3%)
  between operations  1.4 us (1%)
  local copies, waits for them, and re-layouts  1.23 us (1%)
    all_to_all x6, blocking collectives, exchange(): return lax.all_to_all(blocks, 'd', 0, 0, axis_index_groups=groups)  92.3 us
    ppermute x2, starting transfers between devices, swap_cores(): lax.ppermute(blocks, 'd', [(i, i ^ N_Y) for i in range(np.prod(SIZES))])  3.93 us
    ppermute x2, waiting for transfers between devices, swap_cores(): lax.ppermute(blocks, 'd', [(i, i ^ N_Y) for i in range(np.prod(SIZES))])  3.77 us
  transfers between devices with their start and end apart: 2, of which 2 were waited for; matrix products, arithmetic and copies ran while one was open for 0% of the time, Pallas kernels for 0%

profile of v12, /device:TPU:2, one launch (start us, length us, event | category | flops | bytes accessed | tf_op | source)
XLA Modules:
  0.0 108.5 jit_solution(13237848096654561687)
XLA Ops:
  0.6 0.0 copy-start
  0.6 0.8 rsqrt_bitcast_fusion.scales_ref
  1.5 0.0 copy-start.2
  1.5 0.9 copy-done.2
  2.4 0.1 start.1.scaled_ref
  2.5 19.4 %all_to_all.30 = bf16[8,128,128]{2,1,0:T(8,128)(2,1)S(1)} all-to-all(bf16[8,128,128]{2,1,0:T(8,128)(2,1)S(1)} %start.1.scaled_ref), channel_id=1, replica_groups={{448,192,320,64,384,128,256,0},{449,193,321,65,385,129,257,1},{450,194,..., dimensions={0} | all-to-all | bytes 524288 | tf_op jit(solution)/shard_map/all_to_all | solution.py:61
  21.8 0.2 broadcast_in_dim.4
  22.1 16.9 %all_to_all.31 = bf16[4,8,128,128]{3,2,1,0:T(8,128)(2,1)S(1)} all-to-all(bf16[4,8,128,128]{3,2,1,0:T(8,128)(2,1)S(1)} %broadcast_in_dim.4), channel_id=1, replica_groups={{0,16,48,32},{1,17,49,33},{2,18,50,34},{3,19,51,35},{4,20,52,36},{5,21,..., dimensions={0} | all-to-all | bytes 2097152 | tf_op jit(solution)/shard_map/all_to_all | solution.py:61
  39.0 2.0 %collective-permute-start = (bf16[32,128,128]{2,1,0:T(8,128)(2,1)S(1)}, bf16[32,128,128]{2,1,0:T(8,128)(2,1)S(1)}, u32[]{:S(2)}, u32[]{:S(2)}) collective-permute-start(bf16[32,128,128]{2,1,0:T(8,128)(2,1)S(1)} %bitcast.9), channel_id=1, source_target_pairs={{0,8},{1,9},{2,10},{3,11},{4,12},{5,13},{6,14},{7,15},{8,0},{9,1},... | collective-permute-start | bytes 3145736 | tf_op jit(solution)/shard_map/ppermute | solution.py:65
  41.6 0.0 copy-done.4
  41.7 0.0 copy-done.5
  41.7 0.0 copy-start.6
  41.7 0.0 copy-start.1
  41.7 0.0 copy-start.3
  41.7 1.8 %collective-permute-done.other_ref = bf16[32,128,128]{2,1,0:T(8,128)(2,1)S(1)} collective-permute-done((bf16[32,128,128]{2,1,0:T(8,128)(2,1)S(1)}, bf16[32,128,128]{2,1,0:T(8,128)(2,1)S(1)}, u32[]{:S(2)}, u32[]{:S(2)}) %collective-permute-start) | collective-permute-done | bytes 1048608 | tf_op jit(solution)/shard_map/ppermute | solution.py:65
  43.5 0.0 copy-done
  43.5 1.9 %forward.1 = bf16[8,128,128]{2,1,0:T(8,128)(2,1)S(1)} custom-call(s32[4,96]{1,0:T(4,128)S(1)} %lists.1.lists_any, bf16[32,128,128]{2,1,0:T(8,128)(2,1)S(1)} %bitcast.11, bf16[32,128,128]{2,1,0:T(8,128)(2,1)S(1)} %collective-permute-done.other_ref, bf16[96,128,128]{2,1,0:T(8,128)(2,1)S(1)} %copy-done), custom_call_target="tpu_custom_call" | custom-call | tf_op jit(solution)/shard_map/forward/pallas_call | solution.py:222
  45.4 15.4 %all_to_all.32.parts_ref = bf16[8,128,128]{2,1,0:T(8,128)(2,1)S(1)} all-to-all(bf16[8,128,128]{2,1,0:T(8,128)(2,1)S(1)} %forward.1), channel_id=1, replica_groups={{7,3,5,1,6,2,4,0},{14,10,12,8,15,11,13,9},{23,19,21,17,22,18,20,16},{30..., dimensions={0} | all-to-all | bytes 524288 | tf_op jit(solution)/shard_map/all_to_all | solution.py:61
  60.9 0.0 copy-done.6
  60.9 0.1 broadcast_in_dim.5.bias_ref
  60.9 0.0 copy-done.1
  60.9 0.0 copy-done.3
  60.9 0.4 middle.1
  61.3 13.7 %all_to_all.33.group_ref = bf16[8,2,64,128]{3,2,1,0:T(8,128)(2,1)S(1)} all-to-all(bf16[8,2,64,128]{3,2,1,0:T(8,128)(2,1)S(1)} %get-tuple-element.10.sent_ref), channel_id=1, replica_groups={{7,3,5,1,6,2,4,0},{14,10,12,8,15,11,13,9},{23,19,21,17,22,18,20,16},{30..., dimensions={0} | all-to-all | bytes 524288 | tf_op jit(solution)/shard_map/all_to_all | solution.py:61
  75.0 1.7 %backward.1 = (bf16[4,9,64,128]{3,2,1,0:T(8,128)(2,1)S(1)}, bf16[4,9,64,128]{3,2,1,0:T(8,128)(2,1)S(1)}, bf16[64,128]{1,0:T(8,128)(2,1)}) custom-call(s32[4,96]{1,0:T(4,128)S(1)} %lists.1.lists_any, bf16[8,2,64,128]{3,2,1,0:T(8,128)(2,1)S(1)} %all_to_all.33.group_ref, bf16[96,128,128]{2,1,0:T(8,128)(2,1)S(1)} %copy-done, ...), custom_call_target="tpu_custom_call" | custom-call | tf_op jit(solution)/shard_map/backward/pallas_call | solution.py:252
  76.7 1.9 %collective-permute-start.1 = (bf16[4,9,64,128]{3,2,1,0:T(8,128)(2,1)S(1)}, bf16[4,9,64,128]{3,2,1,0:T(8,128)(2,1)S(1)}, u32[]{:S(2)}, u32[]{:S(2)}) collective-permute-start(bf16[4,9,64,128]{3,2,1,0:T(8,128)(2,1)S(1)} %get-tuple-element.14), channel_id=1, source_target_pairs={{0,8},{1,9},{2,10},{3,11},{4,12},{5,13},{6,14},{7,15},{8,0},{9,1},... | collective-permute-start | bytes 1769480 | tf_op jit(solution)/shard_map/ppermute | solution.py:65
  78.7 2.0 %collective-permute-done.1.recv_ref = bf16[4,9,64,128]{3,2,1,0:T(8,128)(2,1)S(1)} collective-permute-done((bf16[4,9,64,128]{3,2,1,0:T(8,128)(2,1)S(1)}, bf16[4,9,64,128]{3,2,1,0:T(8,128)(2,1)S(1)}, u32[]{:S(2)}, u32[]{:S(2)}) %collective-permute-start.1) | collective-permute-done | bytes 589856 | tf_op jit(solution)/shard_map/ppermute | solution.py:65
  80.6 0.1 core_sum.1
  80.8 12.9 %all_to_all.34.recv_ref = bf16[4,9,64,128]{3,2,1,0:T(8,128)(2,1)S(1)} all-to-all(bf16[4,9,64,128]{3,2,1,0:T(8,128)(2,1)S(1)} %core_sum.1), channel_id=1, replica_groups={{0,16,48,32},{1,17,49,33},{2,18,50,34},{3,19,51,35},{4,20,52,36},{5,21,..., dimensions={0} | all-to-all | bytes 1179648 | tf_op jit(solution)/shard_map/all_to_all | solution.py:61
  93.7 0.1 x_sum.1
  93.8 13.9 %all_to_all.35.recv_ref = bf16[8,2,64,128]{3,2,1,0:T(8,128)(2,1)S(1)} all-to-all(bf16[8,2,64,128]{3,2,1,0:T(8,128)(2,1)S(1)} %x_sum.1), channel_id=1, replica_groups={{448,192,320,64,384,128,256,0},{449,193,321,65,385,129,257,1},{450,194,..., dimensions={0} | all-to-all | bytes 524288 | tf_op jit(solution)/shard_map/all_to_all | solution.py:61
  107.7 0.8 final.1
  (3 shorter events, 0.0 us)
Async XLA Ops:
  0.6 42.9 %copy-start = (bf16[96,128,128]{2,1,0:T(8,128)(2,1)S(1)}, bf16[96,128,128]{2,1,0:T(8,128)(2,1)}, u32[]{:S(2)}) copy-start(bf16[96,128,128]{2,1,0:T(8,128)(2,1)} %values_ref.3) | copy-start | bytes 9437188
  1.5 0.9 copy-start.2
  2.4 39.3 %copy-start.4 = (s32[96]{0:T(128)S(1)}, s32[96]{0:T(128)}, u32[]{:S(2)}) copy-start(s32[96]{0:T(128)} %param.12) | copy-start | bytes 1156
  2.4 39.3 %copy-start.5 = (s32[96]{0:T(128)S(1)}, s32[96]{0:T(128)}, u32[]{:S(2)}) copy-start(s32[96]{0:T(128)} %param.13) | copy-start | bytes 1156
  39.0 4.5 %collective-permute-start = (bf16[32,128,128]{2,1,0:T(8,128)(2,1)S(1)}, bf16[32,128,128]{2,1,0:T(8,128)(2,1)S(1)}, u32[]{:S(2)}, u32[]{:S(2)}) collective-permute-start(bf16[32,128,128]{2,1,0:T(8,128)(2,1)S(1)} %bitcast.9), channel_id=1, source_target_pairs={{0,8},{1,9},{2,10},{3,11},{4,12},{5,13},{6,14},{7,15},{8,0},{9,1},... | collective-permute-start | bytes 3145736 | tf_op jit(solution)/shard_map/ppermute | solution.py:65
  41.7 19.2 %copy-start.6 = (bf16[64]{0:T(256)(128)(2,1)S(1)}, bf16[64]{0:T(256)(128)(2,1)}, u32[]{:S(2)}) copy-start(bf16[64]{0:T(256)(128)(2,1)} %param.16) | copy-start | bytes 388
  41.7 19.2 %copy-start.1 = (bf16[128,64]{0,1:T(8,128)(2,1)S(1)}, bf16[128,64]{0,1:T(8,128)(2,1)}, u32[]{:S(2)}) copy-start(bf16[128,64]{0,1:T(8,128)(2,1)} %param.15) | copy-start | bytes 49156
  41.7 19.2 %copy-start.3 = (bf16[128,64]{0,1:T(8,128)(2,1)S(1)}, bf16[128,64]{0,1:T(8,128)(2,1)}, u32[]{:S(2)}) copy-start(bf16[128,64]{0,1:T(8,128)(2,1)} %param.17) | copy-start | bytes 49156
  76.7 3.9 %collective-permute-start.1 = (bf16[4,9,64,128]{3,2,1,0:T(8,128)(2,1)S(1)}, bf16[4,9,64,128]{3,2,1,0:T(8,128)(2,1)S(1)}, u32[]{:S(2)}, u32[]{:S(2)}) collective-permute-start(bf16[4,9,64,128]{3,2,1,0:T(8,128)(2,1)S(1)} %get-tuple-element.14), channel_id=1, source_target_pairs={{0,8},{1,9},{2,10},{3,11},{4,12},{5,13},{6,14},{7,15},{8,0},{9,1},... | collective-permute-start | bytes 1769480 | tf_op jit(solution)/shard_map/ppermute | solution.py:65
